TPU v7x, 512 devices: a whole 4x4x16 slice. The times are simulated.
512 devices in a mesh: dp: 4 (over y), vocab: 128 (over z, x, core).
Axes of the slice: x: 4, y: 4, z: 16, core: 2. Of those that a mesh axis runs over, the one named last changes fastest.
Arguments:
- hidden: bfloat16 [768, 5120], P('dp', 'vocab'), may hold values from -128 to 128
- head: bfloat16 [114688, 5120], P('vocab', 'dp'), may hold values from -0.125 to 0.125
- targets: int32 [4, 192], P('dp'), may hold values from 0 to 114687
- segments: int32 [4, 192], P('dp'), may hold values from 0 to 15, never falling along the last dimension, each value on 1 to 32 neighbouring positions
- loss_mask: int32 [4, 192], P('dp'), may hold values 0 or 1
Outputs:
- grad_hidden: bfloat16 [768, 5120], P('dp', 'vocab')
- grad_head: bfloat16 [114688, 5120], P('vocab', 'dp')
All inputs are finite; a program needn't handle non-finite values. No bound on the sum of `loss_mask` on one device may be relied on, other than what follows from the above.
Results may differ from a plain program's by a relative error of at most 0.0055.
Values may be sent and summed in bfloat16 or wider, within the bound.
No kernel may reach another device: no remote copies, remote signals or barrier semaphores. Data moves between devices by JAX's collectives and lax.ppermute only.
A program may use at most 64 MiB of HBM per device.

v0:
```python
import jax
import jax.numpy as jnp
from jax import lax
from jax.sharding import PartitionSpec as P

loss_scale = 256.0


def body(hidden, head, targets, segments, loss_mask):
    vocab_rows = head.shape[0]
    features = lax.all_gather(hidden, "vocab", axis=1, tiled=True)
    wide_head = lax.all_gather(head, "dp", axis=1, tiled=True)
    logits = lax.dot_general(
        features, wide_head, (((1,), (1,)), ((), ())), preferred_element_type=jnp.float32
    )
    local_max = jnp.max(logits, axis=1)
    row_max = lax.pmax(local_max, "vocab")
    row_total = lax.psum(jnp.sum(jnp.exp(logits - row_max[:, None]), axis=1), "vocab")
    log_norm = row_max + jnp.log(row_total)
    mask_f = loss_mask[0].astype(jnp.float32)
    seg_ids = segments[0]
    same = (seg_ids[:, None] == seg_ids[None, :]).astype(jnp.float32)
    counts = jnp.dot(same, mask_f)
    weight = loss_scale * mask_f / jnp.maximum(counts, 1.0)
    vocab_start = lax.axis_index("vocab") * vocab_rows
    columns = vocab_start + lax.broadcasted_iota(jnp.int32, (1, vocab_rows), 1)
    onehot = (targets[0][:, None] == columns).astype(jnp.float32)
    grad_logits = (weight[:, None] * (jnp.exp(logits - log_norm[:, None]) - onehot)).astype(
        jnp.bfloat16
    )
    partial_terms = jnp.dot(grad_logits, wide_head, preferred_element_type=jnp.float32)
    grad_hidden = lax.psum_scatter(partial_terms, "vocab", scatter_dimension=1, tiled=True).astype(
        jnp.bfloat16
    )
    group_cols = lax.all_to_all(features, "dp", split_axis=1, concat_axis=0, tiled=True)
    head_total = lax.dot_general(
        lax.all_gather(grad_logits, "dp", axis=0, tiled=True),
        group_cols,
        (((0,), (0,)), ((), ())),
        preferred_element_type=jnp.float32,
    )
    grad_head = head_total.astype(jnp.bfloat16)
    return (grad_hidden, grad_head)


def solution(mesh):
    placed = (P("dp", "vocab"), P("vocab", "dp"), P("dp", None), P("dp", None), P("dp", None))
    return jax.shard_map(
        body,
        mesh=mesh,
        in_specs=placed,
        out_specs=(P("dp", "vocab"), P("vocab", "dp")),
        check_vma=False,
    )
```

profile of v0, /device:TPU:8, one launch (start us, length us, event | category | flops | bytes accessed | tf_op | source)
XLA Modules:
  0.0 1084.5 jit_solution(11283421434849317380)
XLA Ops:
  7.2 0.0 all-gather.4.cloned.1.call-start
  7.2 0.7 all-gather.4.cloned.1.call-update
  7.9 0.0 all-gather.6.cloned.1.call-start
  7.9 0.7 all-gather.6.cloned.1.call-update
  8.6 0.0 all-gather.8.cloned.1.call-start
  8.7 0.7 convert_element_type.19
  9.4 1.0 fusion
  10.4 145.6 %all-gather.4.cloned.1.call-done = bf16[192,5120]{0,1:T(8,128)(2,1)} async-done(((bf16[192,40]{0,1:T(8,128)(2,1)}), bf16[192,5120]{0,1:T(8,128)(2,1)}) %all-gather.4.cloned.1.call-update) | async-done | bytes 1966096 | tf_op jit(solution)/shard_map/all_gather | solution.py:11
  156.0 95.6 %all-gather.6.cloned.1.call-done = bf16[896,5120]{1,0:T(8,128)(2,1)} async-done(((bf16[896,1280]{1,0:T(8,128)(2,1)}), bf16[896,5120]{1,0:T(8,128)(2,1)}) %all-gather.6.cloned.1.call-update) | async-done | bytes 9175056 | tf_op jit(solution)/shard_map/all_gather | solution.py:12
  251.6 7.8 fusion.6
  259.4 252.4 %pmax.7 = f32[192]{0:T(256)S(1)} all-reduce(f32[192]{0:T(256)S(1)} %get-tuple-element.2), channel_id=1, replica_groups=mesh['dp'=4,'vocab'=128] {'vocab'}, use_global_device_ids=true, to_apply=%region_1.0 | all-reduce | flops 192 | bytes 1536 | tf_op jit(solution)/shard_map/pmax | solution.py:17
  511.7 0.3 exponential_reduce_fusion
  512.0 246.8 %psum.7 = f32[192]{0:T(256)S(1)} all-reduce(f32[192]{0:T(256)S(1)} %exponential_reduce_fusion), channel_id=1, replica_groups=mesh['dp'=4,'vocab'=128] {'vocab'}, use_global_device_ids=true, to_apply=%region_3.0 | all-reduce | flops 192 | bytes 1536 | tf_op jit(solution)/shard_map/psum | solution.py:18
  758.8 0.0 copy-done
  758.8 1.0 multiply_convert_fusion
  759.8 0.0 all-gather.8.cloned.1.call-update
  759.8 0.0 reduce-scatter.2.cloned.1.call-start
  759.9 10.0 fusion.7
  769.9 0.0 reduce-scatter.2.cloned.1.call-update
  769.9 3.0 copy.10
  772.9 35.2 %all_to_all.19 = bf16[192,4,1280]{2,0,1:T(8,128)(2,1)} all-to-all(bf16[192,4,1280]{2,0,1:T(8,128)(2,1)S(1)} %copy.10), channel_id=1, replica_groups=mesh['dp'=4,'vocab'=128] {'dp'}, dimensions={1} | all-to-all | bytes 3932160 | tf_op jit(solution)/shard_map/all_to_all | solution.py:35
  808.0 5.3 convolution_convert_fusion
  813.4 263.2 %reduce-scatter.2.cloned.1.call-done = f32[192,40]{0,1:T(8,128)} async-done(((f32[192,5120]{0,1:T(8,128)}), f32[192,40]{0,1:T(8,128)}) %reduce-scatter.2.cloned.1.call-update) | async-done | bytes 30736 | tf_op jit(solution)/shard_map/reduce_scatter | solution.py:32
  1076.6 1.4 convert_element_type.23
  (5 shorter events, 0.0 us)
Async XLA Ops:
  7.2 148.9 %all-gather.4.cloned.1.call-start = ((), (), s32[]{:S(2)}) async-start(), calls=%async_computation.2 | async-start | bytes 2641920 | tf_op jit(solution)/shard_map/all_gather | solution.py:11
  7.9 243.7 %all-gather.6.cloned.1.call-start = ((), (), s32[]{:S(2)}) async-start(), calls=%async_computation.3 | async-start | bytes 11468800 | tf_op jit(solution)/shard_map/all_gather | solution.py:12
  8.6 799.4 %all-gather.8.cloned.1.call-start = ((), (), s32[]{:S(2)}) async-start(), calls=%async_computation.5 | async-start | bytes 1720320 | tf_op jit(solution)/shard_map/all_gather | solution.py:37
  10.4 748.5 %copy-start = (s32[1,192]{1,0:T(1,128)S(1)}, s32[1,192]{1,0:T(1,128)}, u32[]{:S(2)}) copy-start(s32[1,192]{1,0:T(1,128)} %param.7) | copy-start | bytes 2308
  759.8 316.7 %reduce-scatter.2.cloned.1.call-start = ((), (), s32[]{:S(2)}) async-start(), calls=%async_computation.4 | async-start | bytes 5283840 | tf_op jit(solution)/shard_map/reduce_scatter | solution.py:32
Sparse Core Ops, SparseCore 0:
  11.1 144.9 all-gather.3
  158.1 93.4 all-gather.5
  760.0 40.0 all-gather.7
  804.6 271.8 reduce-scatter.1
where the time goes:
time: 1080 us
  blocking collectives  534 us (49%)
  waiting for transfers between devices  506 us (47%)
  matrix products  24.1 us (2%)
  between operations  13.8 us (1%)
    reduce_scatter x1, waiting for transfers between devices, body(): lax.psum_scatter(partial_terms, 'vocab', scatter_dimension=1, tiled=True)  263 us
    pmax x1, blocking collectives, body(): row_max = lax.pmax(local_max, 'vocab')  252 us
    psum x1, blocking collectives, body(): lax.psum(jnp.sum(jnp.exp(logits - row_max[:, None]), axis=1), 'vocab')  247 us
    all_gather x1, waiting for transfers between devices, body(): features = lax.all_gather(hidden, 'vocab', axis=1, tiled=True)  146 us
    all_gather x1, waiting for transfers between devices, body(): wide_head = lax.all_gather(head, 'dp', axis=1, tiled=True)  95.6 us
    all_to_all x1, blocking collectives, body(): lax.all_to_all(features, 'dp', split_axis=1, concat_axis=0, tiled=True)  35.2 us
  transfers between devices with their start and end apart: 4, of which 3 were waited for; matrix products, arithmetic and copies ran while one was open for 2% of the time, Pallas kernels for 0%

commit v1 on v0

v1 whole, which is shorter than its diff:
```python
import jax
import jax.numpy as jnp
from jax import lax
from jax.sharding import Mesh
from jax.sharding import PartitionSpec as P

loss_scale = 256.0
BINS = 4
Z = ("zh", "zl")
f32, bf16 = jnp.float32, jnp.bfloat16


def shift(a, k):
    return lax.ppermute(a, "y", [(i, (i + k) % BINS) for i in range(BINS)])


def swap_core(a):
    return lax.ppermute(a, "c", [(0, 1), (1, 0)])


def swap_pairs():
    return [
        (i * 128 + k * 32 + r, k * 128 + (i - k) % 4 * 32 + r)
        for i in range(4)
        for k in range(4)
        for r in range(32)
    ]


EVERY = ("y", "zh", "zl", "x", "c")


def gather_hidden(hidden):
    tok, cols = hidden.shape
    piece = lax.ppermute(hidden.T, EVERY, swap_pairs())
    along_z = lax.all_to_all(
        jnp.broadcast_to(piece[None], (16, cols, tok)), Z, 0, 0, tiled=True
    )
    along_x = lax.all_to_all(
        jnp.broadcast_to(along_z[None], (4, 16, cols, tok)), "x", 0, 0, tiled=True
    )
    other = swap_core(along_x)
    first = lax.axis_index("c") == 0
    both = jnp.stack([jnp.where(first, along_x, other), jnp.where(first, other, along_x)])
    both = both.reshape(2, 4, BINS, 4, cols, tok)
    return both.transpose(2, 3, 1, 0, 4, 5).reshape(BINS, 32 * cols, tok)


def scatter_hidden(terms, tok, cols):
    parts = terms.astype(bf16).reshape(4, 4, 2, cols, BINS * tok)
    parts = lax.all_to_all(parts.transpose(2, 0, 1, 3, 4), "c", 0, 0, tiled=True)
    parts = jnp.sum(parts.astype(f32), axis=0).astype(bf16)
    parts = lax.all_to_all(parts.transpose(1, 0, 2, 3), "x", 0, 0, tiled=True)
    parts = jnp.sum(parts.astype(f32), axis=0).astype(bf16)
    parts = parts.reshape(4, cols, BINS, tok).transpose(2, 0, 1, 3).reshape(16, cols, tok)
    parts = lax.all_to_all(parts, Z, 0, 0, tiled=True)
    piece = jnp.sum(parts.astype(f32), axis=0).astype(bf16)
    back = lax.ppermute(piece, EVERY, [(b, a) for a, b in swap_pairs()])
    return back.T


def row_stats(local_max, local_sum):
    both = jnp.stack([local_max, local_sum])
    other = swap_core(both)
    top = jnp.maximum(both[0], other[0])
    total = both[1] * jnp.exp(both[0] - top) + other[1] * jnp.exp(other[0] - top)
    both = jnp.stack([top, total])
    every = lax.all_to_all(
        jnp.broadcast_to(both[None], (64,) + both.shape), ("zh", "zl", "x"), 0, 0, tiled=True
    )
    top = jnp.max(every[:, 0], axis=0)
    total = jnp.sum(every[:, 1] * jnp.exp(every[:, 0] - top[None]), axis=0)
    return top + jnp.log(total)


def body(hidden, head, targets, segments, loss_mask):
    tok, cols = hidden.shape
    vocab_rows = head.shape[0]
    half = tok // 2
    features = gather_hidden(hidden)

    def partial_logits(b):
        return lax.dot_general(
            features[b], head, (((0,), (1,)), ((), ())), preferred_element_type=f32
        )

    far = partial_logits(2)
    from_left = shift(far[:half], 1)
    from_right = shift(far[half:], 3)
    up = partial_logits(1)
    down = partial_logits(3)
    up_late = shift(up[half:], 1)
    down_early = shift(down[:half], 3)
    own = partial_logits(0)
    up_early = shift(up[:half] + from_left, 1)
    down_late = shift(down[half:] + from_right, 3)
    logits = own + jnp.concatenate([up_early + down_early, up_late + down_late])

    local_max = jnp.max(logits, axis=1)
    local_sum = jnp.sum(jnp.exp(logits - local_max[:, None]), axis=1)
    log_norm = row_stats(local_max, local_sum)
    mask_f = loss_mask[0].astype(f32)
    seg_ids = segments[0]
    same = (seg_ids[:, None] == seg_ids[None, :]).astype(f32)
    counts = jnp.sum(same * mask_f[None, :], axis=1)
    weight = loss_scale * mask_f / jnp.maximum(counts, 1.0)
    shard = ((lax.axis_index("zh") * 4 + lax.axis_index("zl")) * 4 + lax.axis_index("x")) * 2
    vocab_start = (shard + lax.axis_index("c")) * vocab_rows
    columns = vocab_start + lax.broadcasted_iota(jnp.int32, (1, vocab_rows), 1)
    onehot = (targets[0][:, None] == columns).astype(f32)
    grad_own = (weight[:, None] * (jnp.exp(logits - log_norm[:, None]) - onehot)).astype(bf16)

    grad_down = shift(grad_own, 1)
    grad_up = shift(grad_own, 3)
    far_a = shift(grad_down[:half], 1)
    far_b = shift(grad_up[half:], 3)
    grads = jnp.concatenate([grad_own, grad_up, far_a, far_b, grad_down])

    terms = lax.dot_general(head, grads, (((0,), (1,)), ((), ())), preferred_element_type=f32)
    grad_hidden = scatter_hidden(terms, tok, cols)
    grad_head = sum(
        lax.dot_general(
            grads[b * tok : (b + 1) * tok],
            features[b],
            (((0,), (1,)), ((), ())),
            preferred_element_type=f32,
        )
        for b in range(BINS)
    ).astype(bf16)
    return (grad_hidden, grad_head)


def solution(mesh):
    fine = Mesh(mesh.devices.reshape(4, 4, 4, 4, 2), EVERY)
    row = ("zh", "zl", "x", "c")
    placed = (P("y", row), P(row, "y"), P("y", None), P("y", None), P("y", None))
    return jax.shard_map(
        body,
        mesh=fine,
        in_specs=placed,
        out_specs=(P("y", row), P(row, "y")),
        check_vma=False,
    )
```

time: 1080 us -> 259 us (0.24)
  the two profiles are of different devices: /device:TPU:8 before, /device:TPU:48 now
where the time goes in v1:
time: 259 us; the launch traced here: 258 us
  starting transfers between devices  76.5 us (30%)
  blocking collectives  69.5 us (27%)
  waiting for transfers between devices  66.3 us (26%)
  matrix products  23.8 us (9%)
  local copies, waits for them, and re-layouts  11.8 us (5%)
  other arithmetic  8.93 us (3%)
    ppermute x10, starting transfers between devices, shift(): return lax.ppermute(a, 'y', [(i, (i + k) % BINS) for i in range(BINS)])  38.5 us
    ppermute x10, waiting for transfers between devices, shift(): return lax.ppermute(a, 'y', [(i, (i + k) % BINS) for i in range(BINS)])  26.8 us
    all_to_all x1, blocking collectives, gather_hidden(): lax.all_to_all(jnp.broadcast_to(piece[None], (16, cols, tok)), Z, 0, 0, t...  25.7 us
    all_to_all x1, blocking collectives, gather_hidden(): lax.all_to_all(jnp.broadcast_to(along_z[None], (4, 16, cols, tok)), 'x',...  19.4 us
    all_to_all x1, blocking collectives, scatter_hidden(): parts = lax.all_to_all(parts.transpose(1, 0, 2, 3), 'x', 0, 0, tiled=True)  18.2 us
    all_to_all x1, waiting for transfers between devices, row_stats(): lax.all_to_all(jnp.broadcast_to(both[None], (64,) + both.shape), ('zh', '...  16.9 us
    dot_general x4, matrix products, body(): lax.dot_general(grads[b * tok:(b + 1) * tok], features[b], (((0,), (1,)),...  16.2 us
    ppermute x1, starting transfers between devices, gather_hidden(): piece = lax.ppermute(hidden.T, EVERY, swap_pairs())  14.7 us
  transfers between devices with their start and end apart: 16, of which 14 were waited for; matrix products, arithmetic and copies ran while one was open for 7% of the time, Pallas kernels for 0%

profile of v1, /device:TPU:48, one launch (start us, length us, event | category | flops | bytes accessed | tf_op | source)
XLA Modules:
  0.0 258.1 jit_solution(6910286290654996274)
XLA Ops:
  0.6 14.7 %collective-permute-start = (bf16[40,192]{1,0:T(8,128)(2,1)}, bf16[40,192]{1,0:T(8,128)(2,1)S(1)}, u32[]{:S(2)}, u32[]{:S(2)}) collective-permute-start(bf16[40,192]{1,0:T(8,128)(2,1)} %bitcast.76), channel_id=1, source_target_pairs={{0,0},{1,1},{2,2},{3,3},{4,4},{5,5},{6,6},{7,7},{8,8},{9,9},{10,10... | collective-permute-start | bytes 46088 | tf_op jit(solution)/shard_map/ppermute | solution.py:35
  17.8 25.7 %all_to_all.30 = bf16[16,40,192]{2,1,0:T(8,128)(2,1)S(1)} all-to-all(bf16[16,40,192]{2,1,0:T(8,128)(2,1)S(1)} %broadcast_in_dim.6), channel_id=1, replica_groups=mesh['y'=4,'zh'=4,'zl'=4,'x'=4,'c'=2] {'zh','zl'}, dimensions={0} | all-to-all | bytes 491520 | tf_op jit(solution)/shard_map/all_to_all | solution.py:36
  43.6 19.4 %all_to_all.31 = bf16[4,16,40,192]{3,2,1,0:T(8,128)(2,1)} all-to-all(bf16[4,16,40,192]{3,2,1,0:T(8,128)(2,1)S(1)} %broadcast_in_dim.7), channel_id=1, replica_groups=mesh['y'=4,'zh'=4,'zl'=4,'x'=4,'c'=2] {'x'}, dimensions={0} | all-to-all | bytes 1966080 | tf_op jit(solution)/shard_map/all_to_all | solution.py:39
  64.9 3.3 %collective-permute-done.1 = bf16[4,16,40,192]{3,2,1,0:T(8,128)(2,1)} collective-permute-done((bf16[4,16,40,192]{3,2,1,0:T(8,128)(2,1)}, bf16[4,16,40,192]{3,2,1,0:T(8,128)(2,1)}, u32[]{:S(2)}, u32[]{:S(2)}) %collective-permute-start.1) | collective-permute-done | bytes 983072 | tf_op jit(solution)/shard_map/ppermute | solution.py:18
  72.0 9.2 %collective-permute-start.2 = (f32[96,896]{1,0:T(8,128)S(1)}, f32[96,896]{1,0:T(8,128)S(1)}, u32[]{:S(2)}, u32[]{:S(2)}) collective-permute-start(f32[96,896]{1,0:T(8,128)S(1)} %get-tuple-element.14), channel_id=1, source_target_pairs={{0,128},{128,256},{256,384},{384,0},{1,129},{129,257},{257,385},{3... | collective-permute-start | bytes 1032200 | tf_op jit(solution)/shard_map/ppermute | solution.py:14
  85.2 9.3 %collective-permute-done.6 = f32[96,896]{1,0:T(8,128)S(1)} collective-permute-done((f32[96,896]{1,0:T(8,128)S(1)}, f32[96,896]{1,0:T(8,128)S(1)}, u32[]{:S(2)}, u32[]{:S(2)}) %collective-permute-start.6) | collective-permute-done | bytes 344096 | tf_op jit(solution)/shard_map/ppermute | solution.py:14
  96.5 4.9 %collective-permute-start.3 = (f32[96,896]{1,0:T(8,128)S(1)}, f32[96,896]{1,0:T(8,128)S(1)}, u32[]{:S(2)}, u32[]{:S(2)}) collective-permute-start(f32[96,896]{1,0:T(8,128)S(1)} %get-tuple-element.12), channel_id=1, source_target_pairs={{0,128},{128,256},{256,384},{384,0},{1,129},{129,257},{257,385},{3... | collective-permute-start | bytes 1032200 | tf_op jit(solution)/shard_map/ppermute | solution.py:14
  103.3 5.1 %collective-permute-start.5 = (f32[96,896]{1,0:T(8,128)S(1)}, f32[96,896]{1,0:T(8,128)S(1)}, u32[]{:S(2)}, u32[]{:S(2)}) collective-permute-start(f32[96,896]{1,0:T(8,128)S(1)} %get-tuple-element.13), channel_id=1, source_target_pairs={{0,128},{128,256},{256,384},{384,0},{1,129},{129,257},{257,385},{3... | collective-permute-start | bytes 1032200 | tf_op jit(solution)/shard_map/ppermute | solution.py:14
  108.7 5.3 %collective-permute-done.7 = f32[96,896]{1,0:T(8,128)S(1)} collective-permute-done((f32[96,896]{1,0:T(8,128)S(1)}, f32[96,896]{1,0:T(8,128)S(1)}, u32[]{:S(2)}, u32[]{:S(2)}) %collective-permute-start.7) | collective-permute-done | bytes 344096 | tf_op jit(solution)/shard_map/ppermute | solution.py:14
  120.5 9.3 %all-to-all-start.2 = ((f32[64,2,192]{2,1,0:T(2,128)}), f32[64,2,192]{2,1,0:T(2,128)S(1)}, u32[]{:S(2)}, u32[]{:S(2)}) async-start(f32[64,2,192]{2,1,0:T(2,128)} %broadcast_in_dim.8), calls=%async_computation.2 | async-start | bytes 262144 | tf_op jit(solution)/shard_map/all_to_all | solution.py:68
  130.0 16.9 %all-to-all-done.2 = f32[64,2,192]{2,1,0:T(2,128)S(1)} async-done(((f32[64,2,192]{2,1,0:T(2,128)}), f32[64,2,192]{2,1,0:T(2,128)S(1)}, u32[]{:S(2)}, u32[]{:S(2)}) %all-to-all-start.2) | async-done | bytes 98336 | tf_op jit(solution)/shard_map/all_to_all | solution.py:68
  148.4 4.9 %collective-permute-start.10 = (bf16[192,896]{1,0:T(8,128)(2,1)S(1)}, bf16[192,896]{1,0:T(8,128)(2,1)S(1)}, u32[]{:S(2)}, u32[]{:S(2)}) collective-permute-start(bf16[192,896]{1,0:T(8,128)(2,1)S(1)} %get-tuple-element.3), channel_id=1, source_target_pairs={{0,128},{128,256},{256,384},{384,0},{1,129},{129,257},{257,385},{3... | collective-permute-start | bytes 1032200 | tf_op jit(solution)/shard_map/ppermute | solution.py:14
  155.3 4.5 %collective-permute-done.10 = bf16[192,896]{1,0:T(8,128)(2,1)S(1)} collective-permute-done((bf16[192,896]{1,0:T(8,128)(2,1)S(1)}, bf16[192,896]{1,0:T(8,128)(2,1)S(1)}, u32[]{:S(2)}, u32[]{:S(2)}) %collective-permute-start.10) | collective-permute-done | bytes 344096 | tf_op jit(solution)/shard_map/ppermute | solution.py:14
  159.8 4.7 %collective-permute-start.11 = (bf16[96,896]{1,0:T(8,128)(2,1)S(1)}, bf16[96,896]{1,0:T(8,128)(2,1)S(1)}, u32[]{:S(2)}, u32[]{:S(2)}) collective-permute-start(bf16[96,896]{1,0:T(8,128)(2,1)S(1)} %slice.90), channel_id=1, source_target_pairs={{0,128},{128,256},{256,384},{384,0},{1,129},{129,257},{257,385},{3... | collective-permute-start | bytes 516104 | tf_op jit(solution)/shard_map/ppermute | solution.py:14
  168.8 4.8 %collective-permute-done.12 = bf16[96,896]{1,0:T(8,128)(2,1)S(1)} collective-permute-done((bf16[96,896]{1,0:T(8,128)(2,1)S(1)}, bf16[96,896]{1,0:T(8,128)(2,1)S(1)}, u32[]{:S(2)}, u32[]{:S(2)}) %collective-permute-start.12) | collective-permute-done | bytes 172064 | tf_op jit(solution)/shard_map/ppermute | solution.py:14
  174.3 3.5 %fusion = bf16[1280,768]{0,1:T(8,128)(2,1)} fusion(bf16[768,896]{1,0:T(8,128)(2,1)S(1)} %constant_dynamic-update-slice_fusion, bf16[896,1280]{1,0:T(8,128)(2,1)S(1)} %copy-done), kind=kOutput, calls=%fused_computation.2 | convolution fusion | flops 1762590720 | bytes 5636096 | tf_op jit(solution)/shard_map/dot_general | solution.py:119
  177.8 4.1 %copy.35 = bf16[1280,768]{1,0:T(8,128)(2,1)} copy(bf16[1280,768]{0,1:T(8,128)(2,1)} %fusion) | data formatting | bytes 3932160 | tf_op jit(solution)/shard_map/convert_element_type | solution.py:50
  183.6 6.2 %all_to_all.32 = bf16[2,4,4,40,768]{4,3,2,1,0:T(8,128)(2,1)} all-to-all(bf16[2,4,4,40,768]{4,3,2,1,0:T(8,128)(2,1)S(1)} %copy.36), channel_id=1, replica_groups=mesh['y'=4,'zh'=4,'zl'=4,'x'=4,'c'=2] {'c'}, dimensions={0} | all-to-all | bytes 3932160 | tf_op jit(solution)/shard_map/all_to_all | solution.py:51
  191.9 18.2 %all_to_all.33 = bf16[4,4,40,768]{3,2,1,0:T(8,128)(2,1)} all-to-all(bf16[4,4,40,768]{3,2,1,0:T(8,128)(2,1)S(1)} %copy.37), channel_id=1, replica_groups=mesh['y'=4,'zh'=4,'zl'=4,'x'=4,'c'=2] {'x'}, dimensions={0} | all-to-all | bytes 1966080 | tf_op jit(solution)/shard_map/all_to_all | solution.py:53
  214.2 4.6 %all-to-all-start.5 = ((bf16[16,40,192]{2,1,0:T(8,128)(2,1)}), bf16[16,40,192]{2,1,0:T(8,128)(2,1)}, u32[]{:S(2)}, u32[]{:S(2)}) async-start(bf16[16,40,192]{2,1,0:T(8,128)(2,1)} %bitcast.65), calls=%async_computation.5 | async-start | bytes 655360 | tf_op jit(solution)/shard_map/all_to_all | solution.py:56
  227.9 11.7 %all-to-all-done.5 = bf16[16,40,192]{2,1,0:T(8,128)(2,1)} async-done(((bf16[16,40,192]{2,1,0:T(8,128)(2,1)}), bf16[16,40,192]{2,1,0:T(8,128)(2,1)}, u32[]{:S(2)}, u32[]{:S(2)}) %all-to-all-start.5) | async-done | bytes 245792 | tf_op jit(solution)/shard_map/all_to_all | solution.py:56
  240.7 5.5 %collective-permute-start.13 = (bf16[40,192]{1,0:T(8,128)(2,1)S(1)}, bf16[40,192]{1,0:T(8,128)(2,1)S(1)}, u32[]{:S(2)}, u32[]{:S(2)}) collective-permute-start(bf16[40,192]{1,0:T(8,128)(2,1)S(1)} %reduce_sum.68), channel_id=1, source_target_pairs={{0,0},{1,1},{2,2},{3,3},{4,4},{5,5},{6,6},{7,7},{8,8},{9,9},{10,10... | collective-permute-start | bytes 46088 | tf_op jit(solution)/shard_map/ppermute | solution.py:58
  246.2 7.3 %add_convert_fusion = bf16[896,1280]{1,0:T(8,128)(2,1)} fusion(f32[896,1280]{1,0:T(8,128)} %fusion.1, f32[896,1280]{1,0:T(8,128)} %fusion.19, f32[896,1280]{1,0:T(8,128)} %fusion.20, bf16[192,896]{1,0:T(8,128)(2,1)S(1)} %copy-done.11, bf16[1280,192]{1,0:T(8,128)(2,1)S(1)} %bitcast.55), kind=kOutput, calls=%fused_computation | convolution fusion | flops 444989440 | bytes 16891904 | tf_op jit(solution)/shard_map/dot_general | solution.py:122
  253.5 4.0 %collective-permute-done.13 = bf16[40,192]{1,0:T(8,128)(2,1)S(1)} collective-permute-done((bf16[40,192]{1,0:T(8,128)(2,1)S(1)}, bf16[40,192]{1,0:T(8,128)(2,1)S(1)}, u32[]{:S(2)}, u32[]{:S(2)}) %collective-permute-start.13) | collective-permute-done | bytes 15392 | tf_op jit(solution)/shard_map/ppermute | solution.py:58
  (106 shorter events, 49.7 us)
Async XLA Ops:
  0.6 70.3 %copy-start = (bf16[896,1280]{1,0:T(8,128)(2,1)S(1)}, bf16[896,1280]{1,0:T(8,128)(2,1)}, u32[]{:S(2)}) copy-start(bf16[896,1280]{1,0:T(8,128)(2,1)} %param.6) | copy-start | bytes 6881284
  0.6 17.1 %collective-permute-start = (bf16[40,192]{1,0:T(8,128)(2,1)}, bf16[40,192]{1,0:T(8,128)(2,1)S(1)}, u32[]{:S(2)}, u32[]{:S(2)}) collective-permute-start(bf16[40,192]{1,0:T(8,128)(2,1)} %bitcast.76), channel_id=1, source_target_pairs={{0,0},{1,1},{2,2},{3,3},{4,4},{5,5},{6,6},{7,7},{8,8},{9,9},{10,10... | collective-permute-start | bytes 46088 | tf_op jit(solution)/shard_map/ppermute | solution.py:35
  63.0 5.3 %collective-permute-start.1 = (bf16[4,16,40,192]{3,2,1,0:T(8,128)(2,1)}, bf16[4,16,40,192]{3,2,1,0:T(8,128)(2,1)}, u32[]{:S(2)}, u32[]{:S(2)}) collective-permute-start(bf16[4,16,40,192]{3,2,1,0:T(8,128)(2,1)} %all_to_all.31), channel_id=1, source_target_pairs={{0,1},{1,0},{2,3},{3,2},{4,5},{5,4},{6,7},{7,6},{8,9},{9,8},{10,11... | collective-permute-start | bytes 2949128 | tf_op jit(solution)/shard_map/ppermute | solution.py:18
  70.9 44.4 %copy-start.7 = (bf16[1,4,4,2,40,192]{5,4,3,2,1,0:T(8,128)(2,1)}, bf16[1,4,4,2,40,192]{5,4,3,2,1,0:T(8,128)(2,1)S(1)}, u32[]{:S(2)}) copy-start(bf16[1,4,4,2,40,192]{5,4,3,2,1,0:T(8,128)(2,1)S(1)} %get-tuple-element.7) | copy-start | bytes 1474564
  72.0 24.4 %collective-permute-start.2 = (f32[96,896]{1,0:T(8,128)S(1)}, f32[96,896]{1,0:T(8,128)S(1)}, u32[]{:S(2)}, u32[]{:S(2)}) collective-permute-start(f32[96,896]{1,0:T(8,128)S(1)} %get-tuple-element.14), channel_id=1, source_target_pairs={{0,128},{128,256},{256,384},{384,0},{1,129},{129,257},{257,385},{3... | collective-permute-start | bytes 1032200 | tf_op jit(solution)/shard_map/ppermute | solution.py:14
  81.2 13.2 %collective-permute-start.6 = (f32[96,896]{1,0:T(8,128)S(1)}, f32[96,896]{1,0:T(8,128)S(1)}, u32[]{:S(2)}, u32[]{:S(2)}) collective-permute-start(f32[96,896]{1,0:T(8,128)S(1)} %get-tuple-element.15), channel_id=1, source_target_pairs={{0,384},{128,0},{256,128},{384,256},{1,385},{129,1},{257,129},{385... | collective-permute-start | bytes 1032200 | tf_op jit(solution)/shard_map/ppermute | solution.py:14
  94.5 13.9 %collective-permute-start.4 = (f32[96,896]{1,0:T(8,128)S(1)}, f32[96,896]{1,0:T(8,128)S(1)}, u32[]{:S(2)}, u32[]{:S(2)}) collective-permute-start(f32[96,896]{1,0:T(8,128)S(1)} %get-tuple-element.10), channel_id=1, source_target_pairs={{0,384},{128,0},{256,128},{384,256},{1,385},{129,1},{257,129},{385... | collective-permute-start | bytes 1032200 | tf_op jit(solution)/shard_map/ppermute | solution.py:14
  96.5 12.1 %collective-permute-start.3 = (f32[96,896]{1,0:T(8,128)S(1)}, f32[96,896]{1,0:T(8,128)S(1)}, u32[]{:S(2)}, u32[]{:S(2)}) collective-permute-start(f32[96,896]{1,0:T(8,128)S(1)} %get-tuple-element.12), channel_id=1, source_target_pairs={{0,128},{128,256},{256,384},{384,0},{1,129},{129,257},{257,385},{3... | collective-permute-start | bytes 1032200 | tf_op jit(solution)/shard_map/ppermute | solution.py:14
  101.4 12.6 %collective-permute-start.7 = (f32[96,896]{1,0:T(8,128)S(1)}, f32[96,896]{1,0:T(8,128)S(1)}, u32[]{:S(2)}, u32[]{:S(2)}) collective-permute-start(f32[96,896]{1,0:T(8,128)S(1)} %get-tuple-element.11), channel_id=1, source_target_pairs={{0,384},{128,0},{256,128},{384,256},{1,385},{129,1},{257,129},{385... | collective-permute-start | bytes 1032200 | tf_op jit(solution)/shard_map/ppermute | solution.py:14
  103.3 11.9 %collective-permute-start.5 = (f32[96,896]{1,0:T(8,128)S(1)}, f32[96,896]{1,0:T(8,128)S(1)}, u32[]{:S(2)}, u32[]{:S(2)}) collective-permute-start(f32[96,896]{1,0:T(8,128)S(1)} %get-tuple-element.13), channel_id=1, source_target_pairs={{0,128},{128,256},{256,384},{384,0},{1,129},{129,257},{257,385},{3... | collective-permute-start | bytes 1032200 | tf_op jit(solution)/shard_map/ppermute | solution.py:14
  115.3 31.9 %copy-start.22 = (s32[1,192]{1,0:T(1,128)S(1)}, s32[1,192]{1,0:T(1,128)}, u32[]{:S(2)}) copy-start(s32[1,192]{1,0:T(1,128)} %param.7) | copy-start | bytes 2308
  116.7 3.1 %collective-permute-start.8 = (f32[2,192]{1,0:T(2,128)S(1)}, f32[2,192]{1,0:T(2,128)S(1)}, u32[]{:S(2)}, u32[]{:S(2)}) collective-permute-start(f32[2,192]{1,0:T(2,128)S(1)} %pad_maximum_fusion.1), channel_id=1, source_target_pairs={{0,1},{1,0},{2,3},{3,2},{4,5},{5,4},{6,7},{7,6},{8,9},{9,8},{10,11... | collective-permute-start | bytes 4616 | tf_op jit(solution)/shard_map/ppermute | solution.py:18
  120.5 26.5 %all-to-all-start.2 = ((f32[64,2,192]{2,1,0:T(2,128)}), f32[64,2,192]{2,1,0:T(2,128)S(1)}, u32[]{:S(2)}, u32[]{:S(2)}) async-start(f32[64,2,192]{2,1,0:T(2,128)} %broadcast_in_dim.8), calls=%async_computation.2 | async-start | bytes 262144 | tf_op jit(solution)/shard_map/all_to_all | solution.py:68
  148.4 18.6 %copy-start.14 = (bf16[192,896]{1,0:T(8,128)(2,1)}, bf16[192,896]{1,0:T(8,128)(2,1)S(1)}, u32[]{:S(2)}) copy-start(bf16[192,896]{1,0:T(8,128)(2,1)S(1)} %get-tuple-element.3) | copy-start | bytes 1032196
  148.4 11.4 %collective-permute-start.10 = (bf16[192,896]{1,0:T(8,128)(2,1)S(1)}, bf16[192,896]{1,0:T(8,128)(2,1)S(1)}, u32[]{:S(2)}, u32[]{:S(2)}) collective-permute-start(bf16[192,896]{1,0:T(8,128)(2,1)S(1)} %get-tuple-element.3), channel_id=1, source_target_pairs={{0,128},{128,256},{256,384},{384,0},{1,129},{129,257},{257,385},{3... | collective-permute-start | bytes 1032200 | tf_op jit(solution)/shard_map/ppermute | solution.py:14
  153.3 11.7 %collective-permute-start.9 = (bf16[192,896]{1,0:T(8,128)(2,1)S(1)}, bf16[192,896]{1,0:T(8,128)(2,1)S(1)}, u32[]{:S(2)}, u32[]{:S(2)}) collective-permute-start(bf16[192,896]{1,0:T(8,128)(2,1)S(1)} %get-tuple-element.3), channel_id=1, source_target_pairs={{0,384},{128,0},{256,128},{384,256},{1,385},{129,1},{257,129},{385... | collective-permute-start | bytes 1032200 | tf_op jit(solution)/shard_map/ppermute | solution.py:14
  159.8 8.2 %collective-permute-start.11 = (bf16[96,896]{1,0:T(8,128)(2,1)S(1)}, bf16[96,896]{1,0:T(8,128)(2,1)S(1)}, u32[]{:S(2)}, u32[]{:S(2)}) collective-permute-start(bf16[96,896]{1,0:T(8,128)(2,1)S(1)} %slice.90), channel_id=1, source_target_pairs={{0,128},{128,256},{256,384},{384,0},{1,129},{129,257},{257,385},{3... | collective-permute-start | bytes 516104 | tf_op jit(solution)/shard_map/ppermute | solution.py:14
  165.0 8.6 %collective-permute-start.12 = (bf16[96,896]{1,0:T(8,128)(2,1)S(1)}, bf16[96,896]{1,0:T(8,128)(2,1)S(1)}, u32[]{:S(2)}, u32[]{:S(2)}) collective-permute-start(bf16[96,896]{1,0:T(8,128)(2,1)S(1)} %slice.91), channel_id=1, source_target_pairs={{0,384},{128,0},{256,128},{384,256},{1,385},{129,1},{257,129},{385... | collective-permute-start | bytes 516104 | tf_op jit(solution)/shard_map/ppermute | solution.py:14
  191.9 27.0 %copy-start.8 = (bf16[1,4,4,2,40,192]{5,4,3,2,1,0:T(8,128)(2,1)S(1)}, bf16[1,4,4,2,40,192]{5,4,3,2,1,0:T(8,128)(2,1)}, u32[]{:S(2)}) copy-start(bf16[1,4,4,2,40,192]{5,4,3,2,1,0:T(8,128)(2,1)} %copy-done.7) | copy-start | bytes 1474564
  191.9 27.0 %copy-start.15 = (bf16[192,896]{1,0:T(8,128)(2,1)S(1)}, bf16[192,896]{1,0:T(8,128)(2,1)}, u32[]{:S(2)}) copy-start(bf16[192,896]{1,0:T(8,128)(2,1)} %copy-done.14) | copy-start | bytes 1032196
  214.2 25.4 %all-to-all-start.5 = ((bf16[16,40,192]{2,1,0:T(8,128)(2,1)}), bf16[16,40,192]{2,1,0:T(8,128)(2,1)}, u32[]{:S(2)}, u32[]{:S(2)}) async-start(bf16[16,40,192]{2,1,0:T(8,128)(2,1)} %bitcast.65), calls=%async_computation.5 | async-start | bytes 655360 | tf_op jit(solution)/shard_map/all_to_all | solution.py:56
  224.9 21.4 %copy-start.2 = (bf16[1,4,4,2,40,192]{5,4,3,2,1,0:T(8,128)(2,1)S(1)}, bf16[1,4,4,2,40,192]{5,4,3,2,1,0:T(8,128)(2,1)}, u32[]{:S(2)}) copy-start(bf16[1,4,4,2,40,192]{5,4,3,2,1,0:T(8,128)(2,1)} %copy-done.1) | copy-start | bytes 1474564
  224.9 21.4 %copy-start.11 = (bf16[192,896]{1,0:T(8,128)(2,1)S(1)}, bf16[192,896]{1,0:T(8,128)(2,1)}, u32[]{:S(2)}) copy-start(bf16[192,896]{1,0:T(8,128)(2,1)} %copy-done.10) | copy-start | bytes 1032196
  240.7 16.8 %collective-permute-start.13 = (bf16[40,192]{1,0:T(8,128)(2,1)S(1)}, bf16[40,192]{1,0:T(8,128)(2,1)S(1)}, u32[]{:S(2)}, u32[]{:S(2)}) collective-permute-start(bf16[40,192]{1,0:T(8,128)(2,1)S(1)} %reduce_sum.68), channel_id=1, source_target_pairs={{0,0},{1,1},{2,2},{3,3},{4,4},{5,5},{6,6},{7,7},{8,8},{9,9},{10,10... | collective-permute-start | bytes 46088 | tf_op jit(solution)/shard_map/ppermute | solution.py:58
  (15 other events, 78.6 us)

commit v2 on v0

v2 whole, which is shorter than its diff:
```python
import jax
import jax.numpy as jnp
from jax import lax
from jax.sharding import Mesh
from jax.sharding import PartitionSpec as P

loss_scale = 256.0
BINS = 4
EVERY = ("y", "zh", "zl", "x", "c")
ROW = ("zh", "zl", "x", "c")
Z = ("zh", "zl")
f32, bf16 = jnp.float32, jnp.bfloat16


def shift(a, k):
    return lax.ppermute(a, "y", [(i, (i + k) % BINS) for i in range(BINS)])


def swap_core(a):
    return lax.ppermute(a, "c", [(0, 1), (1, 0)])


def exchange(a, axes):
    return lax.all_to_all(a, axes, 0, 0, tiled=True)


def spread(a, axes, n):
    return exchange(jnp.broadcast_to(a[None], (n,) + a.shape), axes)


def column_order(width, cols):
    half = width // 2
    p = lax.broadcasted_iota(jnp.int32, (width, 1), 0)
    core = lax.rem(lax.axis_index("c") + p // half, 2)
    q = lax.rem(p, half)
    natural = lax.rem(q // cols, 4) * (8 * cols) + q // (4 * cols) * (2 * cols) + core * cols + lax.rem(q, cols)
    return (natural == lax.broadcasted_iota(jnp.int32, (1, width), 1)).astype(bf16)


def dot(a, b, ca, cb):
    return lax.dot_general(a, b, (((ca,), (cb,)), ((), ())), preferred_element_type=f32)


def body(hidden, head, targets, segments, loss_mask):
    tok, cols = hidden.shape
    vocab_rows, width = head.shape
    half, hw = tok // 2, width // 2
    y = lax.axis_index("y")
    at = [lax.rem(y + r, BINS) for r in range(BINS)]

    along_z = spread(hidden.T, Z, 16).reshape(BINS, 1, 4 * cols, tok)
    order = column_order(width, cols)
    head_t = dot(order, head, 1, 1).astype(bf16)
    own_cols = exchange(
        jnp.broadcast_to(along_z, (BINS, 4, 4 * cols, tok)).reshape(16, 4 * cols, tok), ("y", "x")
    ).reshape(BINS, hw, tok)
    other_cols = swap_core(own_cols)

    def pick(a, r):
        return lax.dynamic_index_in_dim(a, at[r], 0, keepdims=False)

    def partial_logits(r):
        return dot(pick(own_cols, r), head_t[:hw], 0, 0) + dot(pick(other_cols, r), head_t[hw:], 0, 0)

    far = partial_logits(2)
    from_left = shift(far[:half], 1)
    from_right = shift(far[half:], 3)
    up = partial_logits(1)
    down = partial_logits(3)
    own = partial_logits(0)
    nothing = jnp.zeros((half, vocab_rows), f32)
    up = shift(up + jnp.concatenate([from_left, nothing]), 1)
    down = shift(down + jnp.concatenate([nothing, from_right]), 3)
    logits = own + up + down

    features = jnp.concatenate(
        [
            (dot(pick(own_cols, r), order[:hw], 0, 0) + dot(pick(other_cols, r), order[hw:], 0, 0)).astype(bf16)
            for r in range(BINS)
        ]
    )

    mask_f = loss_mask[0].astype(f32)
    seg_ids = segments[0]
    same = (seg_ids[:, None] == seg_ids[None, :]).astype(f32)
    counts = jnp.sum(same * mask_f[None, :], axis=1)
    weight = loss_scale * mask_f / jnp.maximum(counts, 1.0)
    shard = ((lax.axis_index("zh") * 4 + lax.axis_index("zl")) * 4 + lax.axis_index("x")) * 2
    vocab_start = (shard + lax.axis_index("c")) * vocab_rows
    places = lax.broadcasted_iota(jnp.int32, (1, vocab_rows), 1)
    target = targets[0]

    local_max = jnp.max(logits, axis=1)
    shifted = jnp.exp(logits - local_max[:, None])
    local_lse = local_max + jnp.log(jnp.sum(shifted, axis=1))
    at_target = jnp.sum(jnp.where((target - vocab_start)[:, None] == places, logits, 0.0), axis=1)
    exps = shifted.astype(bf16)

    exps_down = shift(exps, 1)
    exps_up = shift(exps, 3)

    facts = jnp.stack([local_lse, local_max, at_target, weight, target.astype(f32)])
    facts = spread(facts, ("y", "x", "c"), 32).reshape(BINS, 8, 5, tok)
    lse = facts[:, :, 0]
    top = jnp.max(lse, axis=1)
    lse = top + jnp.log(jnp.sum(jnp.exp(lse - top[:, None]), axis=1))
    lse = spread(lse, Z, 16)
    top = jnp.max(lse, axis=0)
    log_norm = top + jnp.log(jnp.sum(jnp.exp(lse - top[None]), axis=0))
    mine = lax.dynamic_index_in_dim(facts, lax.axis_index("x") * 2 + lax.axis_index("c"), 1, keepdims=False)
    scale = mine[:, 3] * jnp.exp(mine[:, 1] - log_norm)
    hit = mine[:, 3] * (jnp.exp(mine[:, 2] - log_norm) - 1.0)
    place = mine[:, 4].astype(jnp.int32) - vocab_start

    far_a = shift(exps_down[:half], 1)
    far_b = shift(exps_up[half:], 3)
    exps_far = jnp.concatenate([far_a, far_b])

    def grad(e, r):
        s, h, p = pick(scale, r), pick(hit, r), pick(place, r)
        return jnp.where(p[:, None] == places, h[:, None], e.astype(f32) * s[:, None]).astype(bf16)

    grads = [grad(e, r) for r, e in enumerate([exps, exps_up, exps_far, exps_down])]

    kept = jnp.zeros((BINS, hw, tok), f32)
    sent = jnp.zeros((BINS, hw, tok), bf16)
    for r in range(BINS):
        kept = lax.dynamic_update_index_in_dim(kept, dot(head_t[:hw], grads[r], 1, 1), at[r], 0)
        sent = lax.dynamic_update_index_in_dim(sent, dot(head_t[hw:], grads[r], 1, 1).astype(bf16), at[r], 0)
    terms = (kept + swap_core(sent).astype(f32)).astype(bf16).reshape(16, 4 * cols, tok)
    terms = exchange(terms, ("y", "x")).reshape(BINS, 4, 4 * cols, tok)
    terms = jnp.sum(terms.astype(f32), axis=1).astype(bf16).reshape(16, cols, tok)
    terms = exchange(terms, Z)
    grad_hidden = jnp.sum(terms.astype(f32), axis=0).astype(bf16).T

    grad_head = dot(jnp.concatenate(grads), features, 0, 0).astype(bf16)
    return (grad_hidden, grad_head)


def solution(mesh):
    fine = Mesh(mesh.devices.reshape(4, 4, 4, 4, 2), EVERY)
    placed = (P("y", ROW), P(ROW, "y"), P("y", None), P("y", None), P("y", None))
    return jax.shard_map(
        body,
        mesh=fine,
        in_specs=placed,
        out_specs=(P("y", ROW), P(ROW, "y")),
        check_vma=False,
    )
```

time: 1080 us -> 245 us (0.23)
  the two profiles are of different devices: /device:TPU:8 before, /device:TPU:64 now
where the time goes in v2:
time: 245 us; the launch traced here: 243 us
  waiting for transfers between devices  104 us (42%)
  starting transfers between devices  74.5 us (30%)
  matrix products  38.8 us (16%)
  other arithmetic  12.9 us (5%)
  local copies, waits for them, and re-layouts  11.2 us (5%)
    all_to_all x6, waiting for transfers between devices, exchange(): return lax.all_to_all(a, axes, 0, 0, tiled=True)  77.7 us
    all_to_all x6, starting transfers between devices, exchange(): return lax.all_to_all(a, axes, 0, 0, tiled=True)  46.5 us
    dot_general x26, matrix products, dot(): lax.dot_general(a, b, (((ca,), (cb,)), ((), ())), preferred_element_type=...  38.8 us
    ppermute x8, waiting for transfers between devices, shift(): return lax.ppermute(a, 'y', [(i, (i + k) % BINS) for i in range(BINS)])  26.7 us
    ppermute x8, starting transfers between devices, shift(): return lax.ppermute(a, 'y', [(i, (i + k) % BINS) for i in range(BINS)])  24.1 us
  transfers between devices with their start and end apart: 16, of which 12 were waited for; matrix products, arithmetic and copies ran while one was open for 17% of the time, Pallas kernels for 0%

profile of v2, /device:TPU:64, one launch (start us, length us, event | category | flops | bytes accessed | tf_op | source)
XLA Modules:
  0.0 243.2 jit_solution(14618148003595856122)
XLA Ops:
  2.3 14.8 %all-to-all-start = ((bf16[16,40,192]{2,1,0:T(8,128)(2,1)}), bf16[16,40,192]{2,1,0:T(8,128)(2,1)S(1)}, u32[]{:S(2)}, u32[]{:S(2)}) async-start(bf16[16,40,192]{2,1,0:T(8,128)(2,1)} %broadcast_in_dim.111), calls=%async_computation | async-start | bytes 655360 | tf_op jit(solution)/shard_map/all_to_all | solution.py:24
  18.7 19.1 %all-to-all-done = bf16[16,40,192]{2,1,0:T(8,128)(2,1)S(1)} async-done(((bf16[16,40,192]{2,1,0:T(8,128)(2,1)}), bf16[16,40,192]{2,1,0:T(8,128)(2,1)S(1)}, u32[]{:S(2)}, u32[]{:S(2)}) %all-to-all-start) | async-done | bytes 245792 | tf_op jit(solution)/shard_map/all_to_all | solution.py:24
  38.9 7.1 %all-to-all-start.1 = ((bf16[16,160,192]{2,1,0:T(8,128)(2,1)}), bf16[16,160,192]{2,1,0:T(8,128)(2,1)}, u32[]{:S(2)}, u32[]{:S(2)}) async-start(bf16[16,160,192]{2,1,0:T(8,128)(2,1)} %bitcast.152), calls=%async_computation.1 | async-start | bytes 2621440 | tf_op jit(solution)/shard_map/all_to_all | solution.py:24
  48.4 13.8 %all-to-all-done.1 = bf16[16,160,192]{2,1,0:T(8,128)(2,1)} async-done(((bf16[16,160,192]{2,1,0:T(8,128)(2,1)}), bf16[16,160,192]{2,1,0:T(8,128)(2,1)}, u32[]{:S(2)}, u32[]{:S(2)}) %all-to-all-start.1) | async-done | bytes 983072 | tf_op jit(solution)/shard_map/all_to_all | solution.py:24
  66.5 4.0 %convolution_convert_fusion.1 = bf16[1280,896]{1,0:T(8,128)(2,1)S(1)} fusion(bf16[896,1280]{1,0:T(8,128)(2,1)S(1)} %copy-done, s32[1280]{0:T(1024)S(1)} %fusion.107), kind=kOutput, calls=%fused_computation.2 | convolution fusion | flops 2938798080 | bytes 4592640 | tf_op jit(solution)/shard_map/dot_general | solution.py:41
  76.9 3.2 %collective-permute-start.1 = (f32[96,896]{1,0:T(8,128)S(1)}, f32[96,896]{1,0:T(8,128)S(1)}, u32[]{:S(2)}, u32[]{:S(2)}) collective-permute-start(f32[96,896]{1,0:T(8,128)S(1)} %get-tuple-element.6), channel_id=1, source_target_pairs={{0,128},{128,256},{256,384},{384,0},{1,129},{129,257},{257,385},{3... | collective-permute-start | bytes 1032200 | tf_op jit(solution)/shard_map/ppermute | solution.py:16
  81.6 3.5 %collective-permute-done.3 = f32[96,896]{1,0:T(8,128)S(1)} collective-permute-done((f32[96,896]{1,0:T(8,128)S(1)}, f32[96,896]{1,0:T(8,128)S(1)}, u32[]{:S(2)}, u32[]{:S(2)}) %collective-permute-start.3) | collective-permute-done | bytes 344096 | tf_op jit(solution)/shard_map/ppermute | solution.py:16
  85.6 3.9 %collective-permute-start.4 = (f32[192,896]{1,0:T(8,128)S(1)}, f32[192,896]{1,0:T(8,128)S(1)}, u32[]{:S(2)}, u32[]{:S(2)}) collective-permute-start(f32[192,896]{1,0:T(8,128)S(1)} %fusion.18), channel_id=1, source_target_pairs={{0,384},{128,0},{256,128},{384,256},{1,385},{129,1},{257,129},{385... | collective-permute-start | bytes 2064392 | tf_op jit(solution)/shard_map/ppermute | solution.py:16
  94.2 10.4 %collective-permute-done.4 = f32[192,896]{1,0:T(8,128)S(1)} collective-permute-done((f32[192,896]{1,0:T(8,128)S(1)}, f32[192,896]{1,0:T(8,128)S(1)}, u32[]{:S(2)}, u32[]{:S(2)}) %collective-permute-start.4) | collective-permute-done | bytes 688160 | tf_op jit(solution)/shard_map/ppermute | solution.py:16
  104.6 6.0 %collective-permute-done.2 = f32[192,896]{1,0:T(8,128)S(1)} collective-permute-done((f32[192,896]{1,0:T(8,128)S(1)}, f32[192,896]{1,0:T(8,128)S(1)}, u32[]{:S(2)}, u32[]{:S(2)}) %collective-permute-start.2) | collective-permute-done | bytes 688160 | tf_op jit(solution)/shard_map/ppermute | solution.py:16
  113.4 3.8 %all-to-all-start.2 = ((f32[32,1,960]{2,1,0:T(1,128)}), f32[32,1,960]{2,1,0:T(1,128)S(1)}, u32[]{:S(2)}, u32[]{:S(2)}) async-start(f32[32,1,960]{2,1,0:T(1,128)} %reshape.198), calls=%async_computation.2 | async-start | bytes 262144 | tf_op jit(solution)/shard_map/all_to_all | solution.py:24
  120.2 4.9 %all-to-all-done.2 = f32[32,1,960]{2,1,0:T(1,128)S(1)} async-done(((f32[32,1,960]{2,1,0:T(1,128)}), f32[32,1,960]{2,1,0:T(1,128)S(1)}, u32[]{:S(2)}, u32[]{:S(2)}) %all-to-all-start.2) | async-done | bytes 122912 | tf_op jit(solution)/shard_map/all_to_all | solution.py:24
  127.5 10.5 %all-to-all-start.3 = ((f32[16,4,192]{2,1,0:T(4,128)}), f32[16,4,192]{2,1,0:T(4,128)S(1)}, u32[]{:S(2)}, u32[]{:S(2)}) async-start(f32[16,4,192]{2,1,0:T(4,128)} %broadcast_in_dim.116), calls=%async_computation.3 | async-start | bytes 131072 | tf_op jit(solution)/shard_map/all_to_all | solution.py:24
  138.0 11.4 %all-to-all-done.3 = f32[16,4,192]{2,1,0:T(4,128)S(1)} async-done(((f32[16,4,192]{2,1,0:T(4,128)}), f32[16,4,192]{2,1,0:T(4,128)S(1)}, u32[]{:S(2)}, u32[]{:S(2)}) %all-to-all-start.3) | async-done | bytes 49184 | tf_op jit(solution)/shard_map/all_to_all | solution.py:24
  149.9 3.3 %collective-permute-start.5 = (bf16[192,896]{1,0:T(8,128)(2,1)S(1)}, bf16[192,896]{1,0:T(8,128)(2,1)S(1)}, u32[]{:S(2)}, u32[]{:S(2)}) collective-permute-start(bf16[192,896]{1,0:T(8,128)(2,1)S(1)} %get-tuple-element.5), channel_id=1, source_target_pairs={{0,384},{128,0},{256,128},{384,256},{1,385},{129,1},{257,129},{385... | collective-permute-start | bytes 1032200 | tf_op jit(solution)/shard_map/ppermute | solution.py:16
  160.2 4.2 %collective-permute-start.8 = (bf16[96,896]{1,0:T(8,128)(2,1)S(1)}, bf16[96,896]{1,0:T(8,128)(2,1)S(1)}, u32[]{:S(2)}, u32[]{:S(2)}) collective-permute-start(bf16[96,896]{1,0:T(8,128)(2,1)S(1)} %slice.83), channel_id=1, source_target_pairs={{0,384},{128,0},{256,128},{384,256},{1,385},{129,1},{257,129},{385... | collective-permute-start | bytes 516104 | tf_op jit(solution)/shard_map/ppermute | solution.py:16
  167.7 5.3 %collective-permute-done.7 = bf16[96,896]{1,0:T(8,128)(2,1)S(1)} collective-permute-done((bf16[96,896]{1,0:T(8,128)(2,1)S(1)}, bf16[96,896]{1,0:T(8,128)(2,1)S(1)}, u32[]{:S(2)}, u32[]{:S(2)}) %collective-permute-start.7) | collective-permute-done | bytes 172064 | tf_op jit(solution)/shard_map/ppermute | solution.py:16
  181.7 3.5 %add_convert_fusion = bf16[4,640,192]{2,1,0:T(8,128)(2,1)} fusion(f32[4,640,192]{2,1,0:T(8,128)} %copy-done.3, bf16[4,640,192]{2,1,0:T(8,128)(2,1)} %copy.53), kind=kLoop, calls=%fused_computation.7 | loop fusion | flops 1474560 | bytes 3932160 | tf_op jit(solution)/shard_map/convert_element_type | solution.py:130
  185.1 4.4 %all-to-all-start.4 = ((bf16[16,160,192]{2,1,0:T(8,128)(2,1)}), bf16[16,160,192]{2,1,0:T(8,128)(2,1)}, u32[]{:S(2)}, u32[]{:S(2)}) async-start(bf16[16,160,192]{2,1,0:T(8,128)(2,1)} %bitcast.151), calls=%async_computation.4 | async-start | bytes 2621440 | tf_op jit(solution)/shard_map/all_to_all | solution.py:24
  189.6 3.0 %fusion.42 = f32[192,1280]{1,0:T(8,128)} fusion(pred[1280,1280]{1,0:T(32,128)(4,1)} %iota_compare_fusion, bf16[4,640,192]{2,1,0:T(8,128)(2,1)} %bitcast.3, s32[]{:T(128)S(6)} %select_n.100), kind=kOutput, calls=%fused_computation.63 | convolution fusion | flops 314572800 | bytes 2129924 | tf_op jit(solution)/shard_map/dot_general | solution.py:41
  198.2 15.4 %all-to-all-done.4 = bf16[16,160,192]{2,1,0:T(8,128)(2,1)} async-done(((bf16[16,160,192]{2,1,0:T(8,128)(2,1)}), bf16[16,160,192]{2,1,0:T(8,128)(2,1)}, u32[]{:S(2)}, u32[]{:S(2)}) %all-to-all-start.4) | async-done | bytes 983072 | tf_op jit(solution)/shard_map/all_to_all | solution.py:24
  216.0 5.9 %all-to-all-start.5 = ((bf16[16,40,192]{2,1,0:T(8,128)(2,1)}), bf16[16,40,192]{2,1,0:T(8,128)(2,1)S(1)}, u32[]{:S(2)}, u32[]{:S(2)}) async-start(bf16[16,40,192]{2,1,0:T(8,128)(2,1)} %bitcast.46), calls=%async_computation.5 | async-start | bytes 655360 | tf_op jit(solution)/shard_map/all_to_all | solution.py:24
  226.2 3.4 %convolution_convert_fusion = bf16[896,1280]{1,0:T(8,128)(2,1)} fusion(bf16[192,1280]{1,0:T(8,128)(2,1)S(1)} %fusion.3, bf16[192,1280]{1,0:T(8,128)(2,1)S(1)} %copy-done.21, bf16[192,1280]{1,0:T(8,128)(2,1)S(1)} %fusion.1, bf16[192,1280]{1,0:T(8,128)(2,1)S(1)} %fusion, bf16[192,896]{1,0:T(8,128)(2,1)S(1)} %copy-done.13, bf16[192,896]{1,0:T(8,128)(2,1)S(1)} %copy-done.15, ...), kind=kOutput, calls=%fused_computation.1 | convolution fusion | flops 1776123904 | bytes 5636096 | tf_op jit(solution)/shard_map/dot_general | solution.py:41
  229.5 13.0 %all-to-all-done.5 = bf16[16,40,192]{2,1,0:T(8,128)(2,1)S(1)} async-done(((bf16[16,40,192]{2,1,0:T(8,128)(2,1)}), bf16[16,40,192]{2,1,0:T(8,128)(2,1)S(1)}, u32[]{:S(2)}, u32[]{:S(2)}) %all-to-all-start.5) | async-done | bytes 245792 | tf_op jit(solution)/shard_map/all_to_all | solution.py:24
  (123 shorter events, 63.9 us)
Async XLA Ops:
  0.6 65.9 %copy-start = (bf16[896,1280]{1,0:T(8,128)(2,1)S(1)}, bf16[896,1280]{1,0:T(8,128)(2,1)}, u32[]{:S(2)}) copy-start(bf16[896,1280]{1,0:T(8,128)(2,1)} %param.6) | copy-start | bytes 6881284
  2.3 35.5 %all-to-all-start = ((bf16[16,40,192]{2,1,0:T(8,128)(2,1)}), bf16[16,40,192]{2,1,0:T(8,128)(2,1)S(1)}, u32[]{:S(2)}, u32[]{:S(2)}) async-start(bf16[16,40,192]{2,1,0:T(8,128)(2,1)} %broadcast_in_dim.111), calls=%async_computation | async-start | bytes 655360 | tf_op jit(solution)/shard_map/all_to_all | solution.py:24
  38.9 23.3 %all-to-all-start.1 = ((bf16[16,160,192]{2,1,0:T(8,128)(2,1)}), bf16[16,160,192]{2,1,0:T(8,128)(2,1)}, u32[]{:S(2)}, u32[]{:S(2)}) async-start(bf16[16,160,192]{2,1,0:T(8,128)(2,1)} %bitcast.152), calls=%async_computation.1 | async-start | bytes 2621440 | tf_op jit(solution)/shard_map/all_to_all | solution.py:24
  64.5 7.7 %collective-permute-start = (bf16[4,640,192]{1,2,0:T(8,128)(2,1)}, bf16[4,640,192]{1,2,0:T(8,128)(2,1)S(1)}, u32[]{:S(2)}, u32[]{:S(2)}) collective-permute-start(bf16[4,640,192]{1,2,0:T(8,128)(2,1)} %copy.45), channel_id=1, source_target_pairs={{0,1},{1,0},{2,3},{3,2},{4,5},{5,4},{6,7},{7,6},{8,9},{9,8},{10,11... | collective-permute-start | bytes 2949128 | tf_op jit(solution)/shard_map/ppermute | solution.py:20
  70.5 40.1 %copy-start.1 = (bf16[1280,896]{1,0:T(8,128)(2,1)}, bf16[1280,896]{1,0:T(8,128)(2,1)S(1)}, u32[]{:S(2)}) copy-start(bf16[1280,896]{1,0:T(8,128)(2,1)S(1)} %convolution_convert_fusion.1) | copy-start | bytes 6881284
  72.2 18.0 %copy-start.6 = (bf16[4,640,192]{1,2,0:T(8,128)(2,1)}, bf16[4,640,192]{1,2,0:T(8,128)(2,1)S(1)}, u32[]{:S(2)}) copy-start(bf16[4,640,192]{1,2,0:T(8,128)(2,1)S(1)} %collective-permute-done) | copy-start | bytes 2949124
  72.8 12.4 %collective-permute-start.3 = (f32[96,896]{1,0:T(8,128)S(1)}, f32[96,896]{1,0:T(8,128)S(1)}, u32[]{:S(2)}, u32[]{:S(2)}) collective-permute-start(f32[96,896]{1,0:T(8,128)S(1)} %get-tuple-element.7), channel_id=1, source_target_pairs={{0,384},{128,0},{256,128},{384,256},{1,385},{129,1},{257,129},{385... | collective-permute-start | bytes 1032200 | tf_op jit(solution)/shard_map/ppermute | solution.py:16
  76.9 13.3 %collective-permute-start.1 = (f32[96,896]{1,0:T(8,128)S(1)}, f32[96,896]{1,0:T(8,128)S(1)}, u32[]{:S(2)}, u32[]{:S(2)}) collective-permute-start(f32[96,896]{1,0:T(8,128)S(1)} %get-tuple-element.6), channel_id=1, source_target_pairs={{0,128},{128,256},{256,384},{384,0},{1,129},{129,257},{257,385},{3... | collective-permute-start | bytes 1032200 | tf_op jit(solution)/shard_map/ppermute | solution.py:16
  85.6 7.1 %copy-start.17 = (s32[1,192]{1,0:T(1,128)S(1)}, s32[1,192]{1,0:T(1,128)}, u32[]{:S(2)}) copy-start(s32[1,192]{1,0:T(1,128)} %param.7) | copy-start | bytes 2308
  85.6 18.9 %collective-permute-start.4 = (f32[192,896]{1,0:T(8,128)S(1)}, f32[192,896]{1,0:T(8,128)S(1)}, u32[]{:S(2)}, u32[]{:S(2)}) collective-permute-start(f32[192,896]{1,0:T(8,128)S(1)} %fusion.18), channel_id=1, source_target_pairs={{0,384},{128,0},{256,128},{384,256},{1,385},{129,1},{257,129},{385... | collective-permute-start | bytes 2064392 | tf_op jit(solution)/shard_map/ppermute | solution.py:16
  90.7 19.9 %collective-permute-start.2 = (f32[192,896]{1,0:T(8,128)S(1)}, f32[192,896]{1,0:T(8,128)S(1)}, u32[]{:S(2)}, u32[]{:S(2)}) collective-permute-start(f32[192,896]{1,0:T(8,128)S(1)} %fusion.19), channel_id=1, source_target_pairs={{0,128},{128,256},{256,384},{384,0},{1,129},{129,257},{257,385},{3... | collective-permute-start | bytes 2064392 | tf_op jit(solution)/shard_map/ppermute | solution.py:16
  113.4 11.7 %all-to-all-start.2 = ((f32[32,1,960]{2,1,0:T(1,128)}), f32[32,1,960]{2,1,0:T(1,128)S(1)}, u32[]{:S(2)}, u32[]{:S(2)}) async-start(f32[32,1,960]{2,1,0:T(1,128)} %reshape.198), calls=%async_computation.2 | async-start | bytes 262144 | tf_op jit(solution)/shard_map/all_to_all | solution.py:24
  127.5 22.0 %all-to-all-start.3 = ((f32[16,4,192]{2,1,0:T(4,128)}), f32[16,4,192]{2,1,0:T(4,128)S(1)}, u32[]{:S(2)}, u32[]{:S(2)}) async-start(f32[16,4,192]{2,1,0:T(4,128)} %broadcast_in_dim.116), calls=%async_computation.3 | async-start | bytes 131072 | tf_op jit(solution)/shard_map/all_to_all | solution.py:24
  149.9 26.7 %copy-start.8 = (bf16[192,896]{1,0:T(8,128)(2,1)}, bf16[192,896]{1,0:T(8,128)(2,1)S(1)}, u32[]{:S(2)}) copy-start(bf16[192,896]{1,0:T(8,128)(2,1)S(1)} %get-tuple-element.4) | copy-start | bytes 1032196
  149.9 9.1 %copy-start.2 = (bf16[1280,896]{1,0:T(8,128)(2,1)S(1)}, bf16[1280,896]{1,0:T(8,128)(2,1)}, u32[]{:S(2)}) copy-start(bf16[1280,896]{1,0:T(8,128)(2,1)} %copy-done.1) | copy-start | bytes 6881284
  149.9 10.4 %collective-permute-start.5 = (bf16[192,896]{1,0:T(8,128)(2,1)S(1)}, bf16[192,896]{1,0:T(8,128)(2,1)S(1)}, u32[]{:S(2)}, u32[]{:S(2)}) collective-permute-start(bf16[192,896]{1,0:T(8,128)(2,1)S(1)} %get-tuple-element.5), channel_id=1, source_target_pairs={{0,384},{128,0},{256,128},{384,256},{1,385},{129,1},{257,129},{385... | collective-permute-start | bytes 1032200 | tf_op jit(solution)/shard_map/ppermute | solution.py:16
  153.2 11.3 %collective-permute-start.6 = (bf16[192,896]{1,0:T(8,128)(2,1)S(1)}, bf16[192,896]{1,0:T(8,128)(2,1)S(1)}, u32[]{:S(2)}, u32[]{:S(2)}) collective-permute-start(bf16[192,896]{1,0:T(8,128)(2,1)S(1)} %get-tuple-element.5), channel_id=1, source_target_pairs={{0,128},{128,256},{256,384},{384,0},{1,129},{129,257},{257,385},{3... | collective-permute-start | bytes 1032200 | tf_op jit(solution)/shard_map/ppermute | solution.py:16
  160.2 7.4 %collective-permute-start.8 = (bf16[96,896]{1,0:T(8,128)(2,1)S(1)}, bf16[96,896]{1,0:T(8,128)(2,1)S(1)}, u32[]{:S(2)}, u32[]{:S(2)}) collective-permute-start(bf16[96,896]{1,0:T(8,128)(2,1)S(1)} %slice.83), channel_id=1, source_target_pairs={{0,384},{128,0},{256,128},{384,256},{1,385},{129,1},{257,129},{385... | collective-permute-start | bytes 516104 | tf_op jit(solution)/shard_map/ppermute | solution.py:16
  164.5 8.5 %collective-permute-start.7 = (bf16[96,896]{1,0:T(8,128)(2,1)S(1)}, bf16[96,896]{1,0:T(8,128)(2,1)S(1)}, u32[]{:S(2)}, u32[]{:S(2)}) collective-permute-start(bf16[96,896]{1,0:T(8,128)(2,1)S(1)} %slice.82), channel_id=1, source_target_pairs={{0,128},{128,256},{256,384},{384,0},{1,129},{129,257},{257,385},{3... | collective-permute-start | bytes 516104 | tf_op jit(solution)/shard_map/ppermute | solution.py:16
  166.9 10.2 %copy-start.10 = (bf16[192,896]{1,0:T(8,128)(2,1)}, bf16[192,896]{1,0:T(8,128)(2,1)S(1)}, u32[]{:S(2)}) copy-start(bf16[192,896]{1,0:T(8,128)(2,1)S(1)} %select_convert_fusion.2) | copy-start | bytes 1032196
  167.7 10.5 %copy-start.12 = (bf16[192,896]{1,0:T(8,128)(2,1)}, bf16[192,896]{1,0:T(8,128)(2,1)S(1)}, u32[]{:S(2)}) copy-start(bf16[192,896]{1,0:T(8,128)(2,1)S(1)} %select_convert_fusion) | copy-start | bytes 1032196
  174.4 5.8 %collective-permute-start.9 = (bf16[4,640,192]{1,2,0:T(8,128)(2,1)S(1)}, bf16[4,640,192]{1,2,0:T(8,128)(2,1)S(1)}, u32[]{:S(2)}, u32[]{:S(2)}) collective-permute-start(bf16[4,640,192]{1,2,0:T(8,128)(2,1)S(1)} %fusion.33), channel_id=1, source_target_pairs={{0,1},{1,0},{2,3},{3,2},{4,5},{5,4},{6,7},{7,6},{8,9},{9,8},{10,11... | collective-permute-start | bytes 2949128 | tf_op jit(solution)/shard_map/ppermute | solution.py:20
  185.1 28.4 %all-to-all-start.4 = ((bf16[16,160,192]{2,1,0:T(8,128)(2,1)}), bf16[16,160,192]{2,1,0:T(8,128)(2,1)}, u32[]{:S(2)}, u32[]{:S(2)}) async-start(bf16[16,160,192]{2,1,0:T(8,128)(2,1)} %bitcast.151), calls=%async_computation.4 | async-start | bytes 2621440 | tf_op jit(solution)/shard_map/all_to_all | solution.py:24
  216.0 26.6 %all-to-all-start.5 = ((bf16[16,40,192]{2,1,0:T(8,128)(2,1)}), bf16[16,40,192]{2,1,0:T(8,128)(2,1)S(1)}, u32[]{:S(2)}, u32[]{:S(2)}) async-start(bf16[16,40,192]{2,1,0:T(8,128)(2,1)} %bitcast.46), calls=%async_computation.5 | async-start | bytes 655360 | tf_op jit(solution)/shard_map/all_to_all | solution.py:24
  (14 other events, 36.3 us)

commit v3 on v2

v3 whole, which is shorter than its diff:
```python
import functools

import jax
import jax.numpy as jnp
from jax import lax
from jax.experimental import pallas as pl
from jax.experimental.pallas import tpu as pltpu
from jax.sharding import Mesh
from jax.sharding import PartitionSpec as P

loss_scale = 256.0
BINS = 4
EVERY = ("y", "zh", "zl", "x", "c")
ROW = ("zh", "zl", "x", "c")
Z = ("zh", "zl")
COLS, TOK, HIGH, EXTRA = 40, 192, 64, 24
f32, bf16, i32 = jnp.float32, jnp.bfloat16, jnp.int32
VMEM = pl.BlockSpec(memory_space=pltpu.VMEM)
SMEM = pl.BlockSpec(memory_space=pltpu.SMEM)


def shift(a, k):
    return lax.ppermute(a, "y", [(i, (i + k) % BINS) for i in range(BINS)])


def swap_core(a):
    return lax.ppermute(a, "c", [(0, 1), (1, 0)])


def exchange(a, axes):
    return lax.all_to_all(a, axes, 0, 0, tiled=True)


def call(kernel, out, ins, *args, flops=0, nbytes=0):
    return pl.pallas_call(
        kernel,
        out_shape=out,
        in_specs=ins,
        out_specs=[VMEM] * len(out) if isinstance(out, (list, tuple)) else VMEM,
        compiler_params=pltpu.CompilerParams(vmem_limit_bytes=48 * 2**20),
        cost_estimate=pl.CostEstimate(flops=flops, bytes_accessed=nbytes, transcendentals=0),
    )(*args)


def shape(*dims, dtype=f32):
    return jax.ShapeDtypeStruct(dims, dtype)


def packed(piece):
    tail = piece[:, 128:]
    right = jnp.concatenate([tail[EXTRA:], jnp.zeros((2 * EXTRA - COLS, TOK - 128), f32)], axis=0)
    return jnp.concatenate([piece[:, :128], jnp.concatenate([tail[:EXTRA], right], axis=1)], axis=0)


def unpacked(piece):
    tail = jnp.concatenate([piece[COLS:, :64], piece[COLS : 2 * COLS - EXTRA, 64:]], axis=0)
    return jnp.concatenate([piece[:COLS], tail], axis=1)


def pack_kernel(h_ref, o_ref):
    piece = packed(h_ref[...].astype(f32)).astype(bf16)
    for k in range(16):
        o_ref[k] = piece


def unpack_kernel(a_ref, o_ref):
    def one(b, _):
        for p in range(8):
            pair = [unpacked(a_ref[b, 2 * p + k].astype(f32)) for k in range(2)]
            o_ref[b, 2 * COLS * p : 2 * COLS * (p + 1), :] = jnp.concatenate(pair, axis=0).astype(bf16)
        return 0

    lax.fori_loop(0, BINS, one, 0)


def eye():
    return lax.broadcasted_iota(i32, (TOK, TOK), 0) == lax.broadcasted_iota(i32, (TOK, TOK), 1)


def softmax_kernel(own_ref, up_ref, down_ref, place_ref, rows_ref, exps_ref, facts_ref):
    logits = own_ref[...] + up_ref[...] + down_ref[...]
    top = jnp.max(logits, axis=1, keepdims=True)
    shifted = jnp.exp(logits - top)
    lse = top + jnp.log(jnp.sum(shifted, axis=1, keepdims=True))
    places = lax.broadcasted_iota(i32, logits.shape, 1)
    at_target = jnp.sum(jnp.where(place_ref[...] == places, logits, 0.0), axis=1, keepdims=True)
    exps = shifted.astype(bf16)
    for b in range(BINS):
        exps_ref[b] = exps
    same = eye()
    lanes = [jnp.sum(jnp.where(same, v, 0.0), axis=0, keepdims=True) for v in (lse, top, at_target)]
    facts = jnp.concatenate(lanes + [rows_ref[...], jnp.zeros((3, TOK), f32)], axis=0)
    for k in range(32):
        facts_ref[k] = facts


def combine_kernel(facts_ref, o_ref):
    rows = []
    for b in range(BINS):
        part = jnp.concatenate([facts_ref[8 * b + k][0:1] for k in range(8)], axis=0)
        top = jnp.max(part, axis=0, keepdims=True)
        rows.append(top + jnp.log(jnp.sum(jnp.exp(part - top), axis=0, keepdims=True)))
    rows = jnp.concatenate(rows, axis=0)
    for k in range(16):
        o_ref[k] = rows


def grad_kernel(where_ref, lse_ref, facts_ref, exps_ref, head_ref, grads_ref, kept_ref, sent_ref):
    lse = lse_ref[...]
    top = jnp.max(lse, axis=0)
    log_norm = top + jnp.log(jnp.sum(jnp.exp(lse - top[None]), axis=0))
    same = eye()

    def column(row):
        return jnp.sum(jnp.where(same, row, 0.0), axis=1, keepdims=True)

    places = lax.broadcasted_iota(i32, exps_ref.shape[1:], 1) + where_ref[1]
    for b in range(BINS):
        mine = facts_ref[8 * b + where_ref[0]]
        norm = log_norm[b : b + 1]
        scale = column(mine[3:4] * jnp.exp(mine[1:2] - norm))
        hit = column(mine[3:4] * (jnp.exp(mine[2:3] - norm) - 1.0))
        target = column(mine[4:5]).astype(i32)
        grads = jnp.where(target == places, hit, exps_ref[b].astype(f32) * scale).astype(bf16)
        grads_ref[b] = grads
        half = head_ref.shape[0] // 2
        for h, ref in ((1, sent_ref), (0, kept_ref)):
            terms = lax.dot_general(
                head_ref[h * half : (h + 1) * half],
                grads,
                (((1,), (1,)), ((), ())),
                preferred_element_type=f32,
            )
            for p in range(16):
                ref[b, p] = packed(terms[COLS * p : COLS * (p + 1)]).astype(ref.dtype)


def column_order(width):
    half = width // 2
    p = lax.broadcasted_iota(i32, (width, 1), 0)
    core = lax.rem(lax.axis_index("c") + p // half, 2)
    q = lax.rem(p, half)
    natural = lax.rem(q // COLS, 4) * (8 * COLS) + q // (4 * COLS) * (2 * COLS) + core * COLS + lax.rem(q, COLS)
    return (natural == lax.broadcasted_iota(i32, (1, width), 1)).astype(bf16)


def dot(a, b, ca, cb):
    return lax.dot_general(a, b, (((ca,), (cb,)), ((), ())), preferred_element_type=f32)


def body(hidden, head, targets, segments, loss_mask):
    vocab_rows, width = head.shape
    half, hw = TOK // 2, width // 2
    y = lax.axis_index("y")
    at = [lax.rem(y + r, BINS) for r in range(BINS)]

    spread = call(pack_kernel, shape(16, 64, 128, dtype=bf16), [VMEM], hidden.T)
    along_z = exchange(spread, Z).reshape(BINS, 1, 4, 64, 128)
    own_packed = exchange(
        jnp.broadcast_to(along_z, (BINS, 4, 4, 64, 128)).reshape(16, 4, 64, 128), ("y", "x")
    ).reshape(BINS, 16, 64, 128)
    other_packed = swap_core(own_packed)
    order = column_order(width)
    head_t = dot(order, head, 1, 1).astype(bf16)
    unpack = functools.partial(
        call, unpack_kernel, shape(BINS, hw, TOK, dtype=bf16), [VMEM], nbytes=4 * 2**20
    )
    own_cols = unpack(own_packed)
    own_cols, head_t, other_packed = lax.optimization_barrier((own_cols, head_t, other_packed))
    other_cols = unpack(other_packed)

    def pick(a, b):
        return lax.dynamic_index_in_dim(a, b, 0, keepdims=False)

    def partial_logits(r):
        return dot(pick(own_cols, at[r]), head_t[:hw], 0, 0) + dot(pick(other_cols, at[r]), head_t[hw:], 0, 0)

    far = partial_logits(2)
    from_left = shift(far[:half], 1)
    from_right = shift(far[half:], 3)
    up = partial_logits(1)
    down = partial_logits(3)
    own = partial_logits(0)
    nothing = jnp.zeros((half, vocab_rows), f32)
    up = shift(up + jnp.concatenate([from_left, nothing]), 1)
    down = shift(down + jnp.concatenate([nothing, from_right]), 3)

    features = jnp.concatenate(
        [
            (dot(own_cols[b], order[:hw], 0, 0) + dot(other_cols[b], order[hw:], 0, 0)).astype(bf16)
            for b in range(BINS)
        ]
    )

    mask_f = loss_mask[0].astype(f32)
    seg_ids = segments[0]
    same = (seg_ids[:, None] == seg_ids[None, :]).astype(f32)
    counts = jnp.sum(same * mask_f[None, :], axis=1)
    weight = loss_scale * mask_f / jnp.maximum(counts, 1.0)
    shard = ((lax.axis_index("zh") * 4 + lax.axis_index("zl")) * 4 + lax.axis_index("x")) * 2
    vocab_start = (shard + lax.axis_index("c")) * vocab_rows
    place = (targets[0] - vocab_start)[:, None]
    rows = jnp.stack([weight, targets[0].astype(f32)])
    here = jnp.stack([lax.axis_index("x") * 2 + lax.axis_index("c"), vocab_start]).astype(i32)
    up, down, own, features, place, rows = lax.optimization_barrier((up, down, own, features, place, rows))

    exps, facts = call(
        softmax_kernel,
        [shape(BINS, TOK, vocab_rows, dtype=bf16), shape(32, 8, TOK)],
        [VMEM] * 5,
        own,
        up,
        down,
        place,
        rows,
    )
    facts = exchange(facts, ("y", "x", "c"))
    lse = exchange(call(combine_kernel, shape(16, BINS, TOK), [VMEM], facts), Z)
    exps = exchange(exps, "y")

    grads, kept, sent = call(
        grad_kernel,
        [
            shape(BINS, TOK, vocab_rows, dtype=bf16),
            shape(BINS, 16, 64, 128),
            shape(BINS, 16, 64, 128, dtype=bf16),
        ],
        [SMEM] + [VMEM] * 4,
        here,
        lse,
        facts,
        exps,
        head_t,
    )
    terms = swap_core(sent)
    grad_head = dot(grads.reshape(BINS * TOK, vocab_rows), features, 0, 0).astype(bf16)
    terms, grad_head = lax.optimization_barrier((terms, grad_head))
    terms = (kept + terms.astype(f32)).astype(bf16).reshape(16, 4, 64, 128)
    terms = exchange(terms, ("y", "x")).reshape(BINS, 4, 4, 64, 128)
    terms = jnp.sum(terms.astype(f32), axis=1).astype(bf16).reshape(16, 64, 128)
    terms = exchange(terms, Z)
    grad_hidden = unpacked(jnp.sum(terms.astype(f32), axis=0)).astype(bf16).T
    return (grad_hidden, grad_head)


def solution(mesh):
    fine = Mesh(mesh.devices.reshape(4, 4, 4, 4, 2), EVERY)
    placed = (P("y", ROW), P(ROW, "y"), P("y", None), P("y", None), P("y", None))
    return jax.shard_map(
        body,
        mesh=fine,
        in_specs=placed,
        out_specs=(P("y", ROW), P(ROW, "y")),
        check_vma=False,
    )
```

time: 245 us -> 225 us (0.918)
  the two profiles are of different devices: /device:TPU:64 before, /device:TPU:32 now
where the time goes in v3:
time: 225 us; the launch traced here: 224 us
  blocking collectives  74.5 us (33%)
  waiting for transfers between devices  63.8 us (28%)
  starting transfers between devices  42.2 us (19%)
  matrix products  18.9 us (8%)
  Pallas kernels  8.7 us (4%)
  local copies, waits for them, and re-layouts  8.17 us (4%)
  other arithmetic  6.45 us (3%)
    all_to_all x4, blocking collectives, exchange(): return lax.all_to_all(a, axes, 0, 0, tiled=True)  74.5 us
    all_to_all x3, waiting for transfers between devices, exchange(): return lax.all_to_all(a, axes, 0, 0, tiled=True)  44.5 us
    all_to_all x3, starting transfers between devices, exchange(): return lax.all_to_all(a, axes, 0, 0, tiled=True)  26.6 us
    dot_general x18, matrix products, dot(): lax.dot_general(a, b, (((ca,), (cb,)), ((), ())), preferred_element_type=...  18.9 us
    ppermute x4, waiting for transfers between devices, shift(): return lax.ppermute(a, 'y', [(i, (i + k) % BINS) for i in range(BINS)])  18.5 us
    ppermute x4, starting transfers between devices, shift(): return lax.ppermute(a, 'y', [(i, (i + k) % BINS) for i in range(BINS)])  11.9 us
    pallas_call x6, Pallas kernels, call(): pl.pallas_call(kernel, out_shape=out, in_specs=ins, out_specs=[VMEM] * le...  8.7 us
    unnamed x22, local copies, waits for them, and re-layouts  6.69 us
  transfers between devices with their start and end apart: 9, of which 7 were waited for; matrix products, arithmetic and copies ran while one was open for 8% of the time, Pallas kernels for 0%

profile of v3, /device:TPU:32, one launch (start us, length us, event | category | flops | bytes accessed | tf_op | source)
XLA Modules:
  0.0 223.8 jit_solution(7671701617896035990)
XLA Ops:
  2.3 15.2 %all-to-all-start = ((bf16[16,64,128]{2,1,0:T(8,128)(2,1)}), bf16[16,64,128]{2,1,0:T(8,128)(2,1)S(1)}, u32[]{:S(2)}, u32[]{:S(2)}) async-start(bf16[16,64,128]{2,1,0:T(8,128)(2,1)} %shard_map.68), calls=%async_computation | async-start | bytes 524288 | tf_op jit(solution)/shard_map/all_to_all | solution.py:31
  19.8 15.6 %all-to-all-done = bf16[16,64,128]{2,1,0:T(8,128)(2,1)S(1)} async-done(((bf16[16,64,128]{2,1,0:T(8,128)(2,1)}), bf16[16,64,128]{2,1,0:T(8,128)(2,1)S(1)}, u32[]{:S(2)}, u32[]{:S(2)}) %all-to-all-start) | async-done | bytes 262176 | tf_op jit(solution)/shard_map/all_to_all | solution.py:31
  36.7 7.0 %all-to-all-start.1 = ((bf16[16,4,64,128]{3,2,1,0:T(8,128)(2,1)}), bf16[16,4,64,128]{3,2,1,0:T(8,128)(2,1)S(1)}, u32[]{:S(2)}, u32[]{:S(2)}) async-start(bf16[16,4,64,128]{3,2,1,0:T(8,128)(2,1)} %bitcast.73), calls=%async_computation.1 | async-start | bytes 2097152 | tf_op jit(solution)/shard_map/all_to_all | solution.py:31
  43.8 5.0 %convolution_convert_fusion.1.head_ref = bf16[1280,896]{1,0:T(8,128)(2,1)} fusion(bf16[896,1280]{1,0:T(8,128)(2,1)S(1)} %copy-done, s32[1280]{0:T(1024)S(1)} %fusion.59), kind=kOutput, calls=%fused_computation.2 | convolution fusion | flops 2938798080 | bytes 4592640 | tf_op jit(solution)/shard_map/dot_general | solution.py:148
  48.8 11.4 %all-to-all-done.1 = bf16[16,4,64,128]{3,2,1,0:T(8,128)(2,1)S(1)} async-done(((bf16[16,4,64,128]{3,2,1,0:T(8,128)(2,1)}), bf16[16,4,64,128]{3,2,1,0:T(8,128)(2,1)S(1)}, u32[]{:S(2)}, u32[]{:S(2)}) %all-to-all-start.1) | async-done | bytes 1048608 | tf_op jit(solution)/shard_map/all_to_all | solution.py:31
  60.2 1.9 collective-permute-start
  62.1 1.4 iota_compare_fusion
  73.0 2.6 %collective-permute-start.3 = (f32[96,896]{1,0:T(8,128)S(1)}, f32[96,896]{1,0:T(8,128)S(1)}, u32[]{:S(2)}, u32[]{:S(2)}) collective-permute-start(f32[96,896]{1,0:T(8,128)S(1)} %get-tuple-element.34), channel_id=1, source_target_pairs={{0,384},{128,0},{256,128},{384,256},{1,385},{129,1},{257,129},{385... | collective-permute-start | bytes 1032200 | tf_op jit(solution)/shard_map/ppermute | solution.py:23
  76.0 3.3 %collective-permute-start.1 = (f32[96,896]{1,0:T(8,128)S(1)}, f32[96,896]{1,0:T(8,128)S(1)}, u32[]{:S(2)}, u32[]{:S(2)}) collective-permute-start(f32[96,896]{1,0:T(8,128)S(1)} %get-tuple-element.35), channel_id=1, source_target_pairs={{0,128},{128,256},{256,384},{384,0},{1,129},{129,257},{257,385},{3... | collective-permute-start | bytes 1032200 | tf_op jit(solution)/shard_map/ppermute | solution.py:23
  79.8 5.2 %collective-permute-done.3 = f32[96,896]{1,0:T(8,128)S(1)} collective-permute-done((f32[96,896]{1,0:T(8,128)S(1)}, f32[96,896]{1,0:T(8,128)S(1)}, u32[]{:S(2)}, u32[]{:S(2)}) %collective-permute-start.3) | collective-permute-done | bytes 344096 | tf_op jit(solution)/shard_map/ppermute | solution.py:23
  85.5 3.8 %collective-permute-start.4 = (f32[192,896]{1,0:T(8,128)S(1)}, f32[192,896]{1,0:T(8,128)S(1)}, u32[]{:S(2)}, u32[]{:S(2)}) collective-permute-start(f32[192,896]{1,0:T(8,128)S(1)} %fusion.4), channel_id=1, source_target_pairs={{0,384},{128,0},{256,128},{384,256},{1,385},{129,1},{257,129},{385... | collective-permute-start | bytes 2064392 | tf_op jit(solution)/shard_map/ppermute | solution.py:23
  89.8 2.2 %collective-permute-start.2 = (f32[192,896]{1,0:T(8,128)S(1)}, f32[192,896]{1,0:T(8,128)S(1)}, u32[]{:S(2)}, u32[]{:S(2)}) collective-permute-start(f32[192,896]{1,0:T(8,128)S(1)} %fusion.5), channel_id=1, source_target_pairs={{0,128},{128,256},{256,384},{384,0},{1,129},{129,257},{257,385},{3... | collective-permute-start | bytes 2064392 | tf_op jit(solution)/shard_map/ppermute | solution.py:23
  93.7 1.4 pad_maximum_fusion
  95.1 8.9 %collective-permute-done.4.down_ref = f32[192,896]{1,0:T(8,128)S(1)} collective-permute-done((f32[192,896]{1,0:T(8,128)S(1)}, f32[192,896]{1,0:T(8,128)S(1)}, u32[]{:S(2)}, u32[]{:S(2)}) %collective-permute-start.4) | collective-permute-done | bytes 688160 | tf_op jit(solution)/shard_map/ppermute | solution.py:23
  104.9 4.4 %collective-permute-done.2.up_ref = f32[192,896]{1,0:T(8,128)S(1)} collective-permute-done((f32[192,896]{1,0:T(8,128)S(1)}, f32[192,896]{1,0:T(8,128)S(1)}, u32[]{:S(2)}, u32[]{:S(2)}) %collective-permute-start.2) | collective-permute-done | bytes 688160 | tf_op jit(solution)/shard_map/ppermute | solution.py:23
  114.0 11.9 %all_to_all.35.facts_ref = f32[32,8,192]{2,1,0:T(8,128)S(1)} all-to-all(f32[32,8,192]{2,1,0:T(8,128)S(1)} %get-tuple-element.26), channel_id=1, replica_groups=mesh['y'=4,'zh'=4,'zl'=4,'x'=4,'c'=2] {'y','x','c'}, dimensions={0} | all-to-all | bytes 393216 | tf_op jit(solution)/shard_map/all_to_all | solution.py:31
  125.9 19.0 %all_to_all.36.lse_ref = f32[16,4,192]{2,1,0:T(4,128)S(1)} all-to-all(f32[16,4,192]{2,1,0:T(4,128)S(1)} %shard_map.72), channel_id=1, replica_groups=mesh['y'=4,'zh'=4,'zl'=4,'x'=4,'c'=2] {'zh','zl'}, dimensions={0} | all-to-all | bytes 98304 | tf_op jit(solution)/shard_map/all_to_all | solution.py:31
  144.9 4.3 %all-to-all-start.4 = ((bf16[4,192,896]{2,1,0:T(8,128)(2,1)}), bf16[4,192,896]{2,1,0:T(8,128)(2,1)}, u32[]{:S(2)}, u32[]{:S(2)}) async-start(bf16[4,192,896]{2,1,0:T(8,128)(2,1)} %copy-done.1), calls=%async_computation.4 | async-start | bytes 2752512 | tf_op jit(solution)/shard_map/all_to_all | solution.py:31
  149.3 17.5 %all-to-all-done.4.exps_ref = bf16[4,192,896]{2,1,0:T(8,128)(2,1)} async-done(((bf16[4,192,896]{2,1,0:T(8,128)(2,1)}), bf16[4,192,896]{2,1,0:T(8,128)(2,1)}, u32[]{:S(2)}, u32[]{:S(2)}) %all-to-all-start.4) | async-done | bytes 1376288 | tf_op jit(solution)/shard_map/all_to_all | solution.py:31
  166.9 6.7 %shard_map.73 = (bf16[4,192,896]{2,1,0:T(8,128)(2,1)S(1)}, f32[4,16,64,128]{3,2,1,0:T(8,128)}, bf16[4,16,64,128]{3,2,1,0:T(8,128)(2,1)S(1)}) custom-call(s32[2]{0:T(128)S(1)} %pad_add_fusion.where_ref, f32[16,4,192]{2,1,0:T(4,128)S(1)} %all_to_all.36.lse_ref, f32[32,8,192]{2,1,0:T(8,128)S(1)} %all_to_all.35.facts_ref, ...), custom_call_target="tpu_custom_call" | custom-call | tf_op jit(solution)/shard_map/pallas_call | solution.py:35
  173.6 1.9 collective-permute-start.5
  175.5 3.4 %convolution_convert_fusion = bf16[896,1280]{1,0:T(8,128)(2,1)} fusion(bf16[768,896]{1,0:T(8,128)(2,1)S(1)} %bitcast.72, bf16[768,1280]{1,0:T(8,128)(2,1)S(1)} %copy-done.9), kind=kOutput, calls=%fused_computation.1 | convolution fusion | flops 1762754560 | bytes 5636096 | tf_op jit(solution)/shard_map/dot_general | solution.py:148
  179.3 21.1 %all_to_all.37 = bf16[16,4,64,128]{3,2,1,0:T(8,128)(2,1)S(1)} all-to-all(bf16[16,4,64,128]{3,2,1,0:T(8,128)(2,1)S(1)} %bitcast.74), channel_id=1, replica_groups=mesh['y'=4,'zh'=4,'zl'=4,'x'=4,'c'=2] {'y','x'}, dimensions={0} | all-to-all | bytes 2097152 | tf_op jit(solution)/shard_map/all_to_all | solution.py:31
  200.6 22.5 %all_to_all.38 = bf16[16,64,128]{2,1,0:T(8,128)(2,1)S(1)} all-to-all(bf16[16,64,128]{2,1,0:T(8,128)(2,1)S(1)} %bitcast.76), channel_id=1, replica_groups=mesh['y'=4,'zh'=4,'zl'=4,'x'=4,'c'=2] {'zh','zl'}, dimensions={0} | all-to-all | bytes 524288 | tf_op jit(solution)/shard_map/all_to_all | solution.py:31
  (64 shorter events, 25.2 us)
Async XLA Ops:
  0.6 43.2 %copy-start = (bf16[896,1280]{1,0:T(8,128)(2,1)S(1)}, bf16[896,1280]{1,0:T(8,128)(2,1)}, u32[]{:S(2)}) copy-start(bf16[896,1280]{1,0:T(8,128)(2,1)} %param.6) | copy-start | bytes 6881284
  0.6 0.9 copy-start.6
  2.3 33.1 %all-to-all-start = ((bf16[16,64,128]{2,1,0:T(8,128)(2,1)}), bf16[16,64,128]{2,1,0:T(8,128)(2,1)S(1)}, u32[]{:S(2)}, u32[]{:S(2)}) async-start(bf16[16,64,128]{2,1,0:T(8,128)(2,1)} %shard_map.68), calls=%async_computation | async-start | bytes 524288 | tf_op jit(solution)/shard_map/all_to_all | solution.py:31
  35.4 8.3 %copy-start.10 = (s32[1,192]{1,0:T(1,128)S(1)}, s32[1,192]{1,0:T(1,128)}, u32[]{:S(2)}) copy-start(s32[1,192]{1,0:T(1,128)} %param.7) | copy-start | bytes 2308
  36.7 23.5 %all-to-all-start.1 = ((bf16[16,4,64,128]{3,2,1,0:T(8,128)(2,1)}), bf16[16,4,64,128]{3,2,1,0:T(8,128)(2,1)S(1)}, u32[]{:S(2)}, u32[]{:S(2)}) async-start(bf16[16,4,64,128]{3,2,1,0:T(8,128)(2,1)} %bitcast.73), calls=%async_computation.1 | async-start | bytes 2097152 | tf_op jit(solution)/shard_map/all_to_all | solution.py:31
  60.2 4.5 %collective-permute-start = (bf16[4,16,64,128]{3,2,1,0:T(8,128)(2,1)S(1)}, bf16[4,16,64,128]{3,2,1,0:T(8,128)(2,1)S(1)}, u32[]{:S(2)}, u32[]{:S(2)}) collective-permute-start(bf16[4,16,64,128]{3,2,1,0:T(8,128)(2,1)S(1)} %bitcast.69), channel_id=1, source_target_pairs={{0,1},{1,0},{2,3},{3,2},{4,5},{5,4},{6,7},{7,6},{8,9},{9,8},{10,11... | collective-permute-start | bytes 3145736 | tf_op jit(solution)/shard_map/ppermute | solution.py:27
  69.3 1.6 copy-start.7
  73.0 12.0 %collective-permute-start.3 = (f32[96,896]{1,0:T(8,128)S(1)}, f32[96,896]{1,0:T(8,128)S(1)}, u32[]{:S(2)}, u32[]{:S(2)}) collective-permute-start(f32[96,896]{1,0:T(8,128)S(1)} %get-tuple-element.34), channel_id=1, source_target_pairs={{0,384},{128,0},{256,128},{384,256},{1,385},{129,1},{257,129},{385... | collective-permute-start | bytes 1032200 | tf_op jit(solution)/shard_map/ppermute | solution.py:23
  76.0 13.2 %collective-permute-start.1 = (f32[96,896]{1,0:T(8,128)S(1)}, f32[96,896]{1,0:T(8,128)S(1)}, u32[]{:S(2)}, u32[]{:S(2)}) collective-permute-start(f32[96,896]{1,0:T(8,128)S(1)} %get-tuple-element.35), channel_id=1, source_target_pairs={{0,128},{128,256},{256,384},{384,0},{1,129},{129,257},{257,385},{3... | collective-permute-start | bytes 1032200 | tf_op jit(solution)/shard_map/ppermute | solution.py:23
  85.5 18.5 %collective-permute-start.4 = (f32[192,896]{1,0:T(8,128)S(1)}, f32[192,896]{1,0:T(8,128)S(1)}, u32[]{:S(2)}, u32[]{:S(2)}) collective-permute-start(f32[192,896]{1,0:T(8,128)S(1)} %fusion.4), channel_id=1, source_target_pairs={{0,384},{128,0},{256,128},{384,256},{1,385},{129,1},{257,129},{385... | collective-permute-start | bytes 2064392 | tf_op jit(solution)/shard_map/ppermute | solution.py:23
  89.8 19.5 %collective-permute-start.2 = (f32[192,896]{1,0:T(8,128)S(1)}, f32[192,896]{1,0:T(8,128)S(1)}, u32[]{:S(2)}, u32[]{:S(2)}) collective-permute-start(f32[192,896]{1,0:T(8,128)S(1)} %fusion.5), channel_id=1, source_target_pairs={{0,128},{128,256},{256,384},{384,0},{1,129},{129,257},{257,385},{3... | collective-permute-start | bytes 2064392 | tf_op jit(solution)/shard_map/ppermute | solution.py:23
  104.0 0.9 copy-start.2
  109.3 0.9 copy-start.4
  110.2 1.1 copy-start.3
  111.3 1.1 copy-start.5
  112.9 1.1 copy-start.1
  144.9 21.9 %all-to-all-start.4 = ((bf16[4,192,896]{2,1,0:T(8,128)(2,1)}), bf16[4,192,896]{2,1,0:T(8,128)(2,1)}, u32[]{:S(2)}, u32[]{:S(2)}) async-start(bf16[4,192,896]{2,1,0:T(8,128)(2,1)} %copy-done.1), calls=%async_computation.4 | async-start | bytes 2752512 | tf_op jit(solution)/shard_map/all_to_all | solution.py:31
  166.9 8.6 %copy-start.9 = (bf16[768,1280]{1,0:T(8,128)(2,1)S(1)}, bf16[768,1280]{1,0:T(8,128)(2,1)}, u32[]{:S(2)}) copy-start(bf16[768,1280]{1,0:T(8,128)(2,1)} %pad_maximum_fusion) | copy-start | bytes 5898244
  173.6 5.3 %collective-permute-start.5 = (bf16[4,16,64,128]{3,2,1,0:T(8,128)(2,1)S(1)}, bf16[4,16,64,128]{3,2,1,0:T(8,128)(2,1)S(1)}, u32[]{:S(2)}, u32[]{:S(2)}) collective-permute-start(bf16[4,16,64,128]{3,2,1,0:T(8,128)(2,1)S(1)} %get-tuple-element.29), channel_id=1, source_target_pairs={{0,1},{1,0},{2,3},{3,2},{4,5},{5,4},{6,7},{7,6},{8,9},{9,8},{10,11... | collective-permute-start | bytes 3145736 | tf_op jit(solution)/shard_map/ppermute | solution.py:27
  175.5 3.4 %copy-start.8 = (f32[4,16,64,128]{3,2,1,0:T(8,128)S(1)}, f32[4,16,64,128]{3,2,1,0:T(8,128)}, u32[]{:S(2)}) copy-start(f32[4,16,64,128]{3,2,1,0:T(8,128)} %get-tuple-element.28) | copy-start | bytes 6291460

commit v4 on v3

--- a/solution.py
+++ b/solution.py
@@ -31,13 +31,14 @@
     return lax.all_to_all(a, axes, 0, 0, tiled=True)
 
 
-def call(kernel, out, ins, *args, flops=0, nbytes=0):
+def call(kernel, out, ins, *args, flops=0, nbytes=0, scratch=()):
     return pl.pallas_call(
         kernel,
         out_shape=out,
         in_specs=ins,
+        scratch_shapes=list(scratch),
         out_specs=[VMEM] * len(out) if isinstance(out, (list, tuple)) else VMEM,
-        compiler_params=pltpu.CompilerParams(vmem_limit_bytes=48 * 2**20),
+        compiler_params=pltpu.CompilerParams(vmem_limit_bytes=16 * 2**20),
         cost_estimate=pl.CostEstimate(flops=flops, bytes_accessed=nbytes, transcendentals=0),
     )(*args)
 
@@ -77,16 +78,14 @@
     return lax.broadcasted_iota(i32, (TOK, TOK), 0) == lax.broadcasted_iota(i32, (TOK, TOK), 1)
 
 
-def softmax_kernel(own_ref, up_ref, down_ref, place_ref, rows_ref, exps_ref, facts_ref):
-    logits = own_ref[...] + up_ref[...] + down_ref[...]
+def softmax_kernel(logits_ref, place_ref, rows_ref, exps_ref, facts_ref):
+    logits = logits_ref[...]
     top = jnp.max(logits, axis=1, keepdims=True)
     shifted = jnp.exp(logits - top)
     lse = top + jnp.log(jnp.sum(shifted, axis=1, keepdims=True))
     places = lax.broadcasted_iota(i32, logits.shape, 1)
     at_target = jnp.sum(jnp.where(place_ref[...] == places, logits, 0.0), axis=1, keepdims=True)
-    exps = shifted.astype(bf16)
-    for b in range(BINS):
-        exps_ref[b] = exps
+    exps_ref[...] = shifted.astype(bf16)
     same = eye()
     lanes = [jnp.sum(jnp.where(same, v, 0.0), axis=0, keepdims=True) for v in (lse, top, at_target)]
     facts = jnp.concatenate(lanes + [rows_ref[...], jnp.zeros((3, TOK), f32)], axis=0)
@@ -105,7 +104,7 @@
         o_ref[k] = rows
 
 
-def grad_kernel(where_ref, lse_ref, facts_ref, exps_ref, head_ref, grads_ref, kept_ref, sent_ref):
+def grad_kernel(where_ref, lse_ref, facts_ref, exps0, exps1, exps2, exps3, head_ref, grads_ref, kept_ref, sent_ref, norms_ref):
     lse = lse_ref[...]
     top = jnp.max(lse, axis=0)
     log_norm = top + jnp.log(jnp.sum(jnp.exp(lse - top[None]), axis=0))
@@ -114,14 +113,16 @@
     def column(row):
         return jnp.sum(jnp.where(same, row, 0.0), axis=1, keepdims=True)
 
-    places = lax.broadcasted_iota(i32, exps_ref.shape[1:], 1) + where_ref[1]
-    for b in range(BINS):
+    norms_ref[...] = log_norm
+    places = lax.broadcasted_iota(i32, exps0.shape, 1) + where_ref[1]
+    for r, exps_ref in enumerate([exps0, exps1, exps2, exps3]):
+        b = lax.rem(where_ref[2] + r, BINS)
         mine = facts_ref[8 * b + where_ref[0]]
-        norm = log_norm[b : b + 1]
+        norm = norms_ref[pl.ds(b, 1)]
         scale = column(mine[3:4] * jnp.exp(mine[1:2] - norm))
         hit = column(mine[3:4] * (jnp.exp(mine[2:3] - norm) - 1.0))
         target = column(mine[4:5]).astype(i32)
-        grads = jnp.where(target == places, hit, exps_ref[b].astype(f32) * scale).astype(bf16)
+        grads = jnp.where(target == places, hit, exps_ref[...].astype(f32) * scale).astype(bf16)
         grads_ref[b] = grads
         half = head_ref.shape[0] // 2
         for h, ref in ((1, sent_ref), (0, kept_ref)):
@@ -185,13 +186,6 @@
     up = shift(up + jnp.concatenate([from_left, nothing]), 1)
     down = shift(down + jnp.concatenate([nothing, from_right]), 3)
 
-    features = jnp.concatenate(
-        [
-            (dot(own_cols[b], order[:hw], 0, 0) + dot(other_cols[b], order[hw:], 0, 0)).astype(bf16)
-            for b in range(BINS)
-        ]
-    )
-
     mask_f = loss_mask[0].astype(f32)
     seg_ids = segments[0]
     same = (seg_ids[:, None] == seg_ids[None, :]).astype(f32)
@@ -201,22 +195,29 @@
     vocab_start = (shard + lax.axis_index("c")) * vocab_rows
     place = (targets[0] - vocab_start)[:, None]
     rows = jnp.stack([weight, targets[0].astype(f32)])
-    here = jnp.stack([lax.axis_index("x") * 2 + lax.axis_index("c"), vocab_start]).astype(i32)
-    up, down, own, features, place, rows = lax.optimization_barrier((up, down, own, features, place, rows))
+    here = jnp.stack([lax.axis_index("x") * 2 + lax.axis_index("c"), vocab_start, y]).astype(i32)
 
     exps, facts = call(
         softmax_kernel,
-        [shape(BINS, TOK, vocab_rows, dtype=bf16), shape(32, 8, TOK)],
-        [VMEM] * 5,
-        own,
-        up,
-        down,
+        [shape(TOK, vocab_rows, dtype=bf16), shape(32, 8, TOK)],
+        [VMEM] * 3,
+        own + up + down,
         place,
         rows,
     )
+    exps, facts, own_cols, other_cols = lax.optimization_barrier((exps, facts, own_cols, other_cols))
+
+    every_exp = [exps, shift(exps, 3), shift(exps, 2), shift(exps, 1)]
     facts = exchange(facts, ("y", "x", "c"))
     lse = exchange(call(combine_kernel, shape(16, BINS, TOK), [VMEM], facts), Z)
-    exps = exchange(exps, "y")
+    lse, facts, every_exp = lax.optimization_barrier((lse, facts, every_exp))
+
+    features = jnp.concatenate(
+        [
+            (dot(own_cols[b], order[:hw], 0, 0) + dot(other_cols[b], order[hw:], 0, 0)).astype(bf16)
+            for b in range(BINS)
+        ]
+    )
 
     grads, kept, sent = call(
         grad_kernel,
@@ -225,12 +226,13 @@
             shape(BINS, 16, 64, 128),
             shape(BINS, 16, 64, 128, dtype=bf16),
         ],
-        [SMEM] + [VMEM] * 4,
+        [SMEM] + [VMEM] * 7,
         here,
         lse,
         facts,
-        exps,
+        *every_exp,
         head_t,
+        scratch=[pltpu.VMEM((BINS, TOK), f32)],
     )
     terms = swap_core(sent)
     grad_head = dot(grads.reshape(BINS * TOK, vocab_rows), features, 0, 0).astype(bf16)

time: 225 us -> 213 us (0.947)
  blocking collectives: 74.5 us -> 42.5 us
  starting transfers between devices: 42.2 us -> 62.4 us
  matrix products: 18.9 us -> 26.6 us
  local copies, waits for them, and re-layouts: 8.17 us -> 5.19 us
    all_to_all x4 -> x2, blocking collectives: 74.5 us -> 42.5 us  [exchange(): return lax.all_to_all(a, axes, 0, 0, tiled=True)]
    ppermute x4 -> x7, starting transfers between devices: 11.9 us -> 24.4 us  [shift(): return lax.ppermute(a, 'y', [(i, (i + k) % BINS) for i in range(BINS)])]
    dot_general x18, matrix products: 18.9 us -> 26.6 us  [dot(): lax.dot_general(a, b, (((ca,), (cb,)), ((), ())), preferred_element_type=...]
    all_to_all x3 -> x4, starting transfers between devices: 26.6 us -> 34.2 us  [exchange(): return lax.all_to_all(a, axes, 0, 0, tiled=True)]
    unnamed x22 -> x26, local copies, waits for them, and re-layouts: 6.69 us -> 3.68 us
    all_to_all x3 -> x4, waiting for transfers between devices: 44.5 us -> 41.8 us  [exchange(): return lax.all_to_all(a, axes, 0, 0, tiled=True)]
    ppermute x4 -> x7, waiting for transfers between devices: 18.5 us -> 19.2 us  [shift(): return lax.ppermute(a, 'y', [(i, (i + k) % BINS) for i in range(BINS)])]
  transfers between devices with their start and end apart: 9 -> 13, of which waited for: 7 -> 8; matrix products, arithmetic and copies ran while one was open for 8% -> 13% of each run, Pallas kernels for 0% -> 0%
where the time goes in v4:
time: 213 us; the launch traced here: 211 us
  starting transfers between devices  62.4 us (29%)
  waiting for transfers between devices  61.8 us (29%)
  blocking collectives  42.5 us (20%)
  matrix products  26.6 us (12%)
  Pallas kernels  6.94 us (3%)
  local copies, waits for them, and re-layouts  5.19 us (2%)
  other arithmetic  5.07 us (2%)
    all_to_all x2, blocking collectives, exchange(): return lax.all_to_all(a, axes, 0, 0, tiled=True)  42.5 us
    all_to_all x4, waiting for transfers between devices, exchange(): return lax.all_to_all(a, axes, 0, 0, tiled=True)  41.8 us
    all_to_all x4, starting transfers between devices, exchange(): return lax.all_to_all(a, axes, 0, 0, tiled=True)  34.2 us
    dot_general x18, matrix products, dot(): lax.dot_general(a, b, (((ca,), (cb,)), ((), ())), preferred_element_type=...  26.6 us
    ppermute x7, starting transfers between devices, shift(): return lax.ppermute(a, 'y', [(i, (i + k) % BINS) for i in range(BINS)])  24.4 us
    ppermute x7, waiting for transfers between devices, shift(): return lax.ppermute(a, 'y', [(i, (i + k) % BINS) for i in range(BINS)])  19.2 us
    pallas_call x6, Pallas kernels, call(): pl.pallas_call(kernel, out_shape=out, in_specs=ins, scratch_shapes=list(s...  6.94 us
  transfers between devices with their start and end apart: 13, of which 8 were waited for; matrix products, arithmetic and copies ran while one was open for 13% of the time, Pallas kernels for 0%

profile of v4, /device:TPU:32, one launch (start us, length us, event | category | flops | bytes accessed | tf_op | source)
XLA Modules:
  0.0 211.5 jit_solution(8087509548309294751)
XLA Ops:
  2.3 15.2 %all-to-all-start = ((bf16[16,64,128]{2,1,0:T(8,128)(2,1)}), bf16[16,64,128]{2,1,0:T(8,128)(2,1)S(1)}, u32[]{:S(2)}, u32[]{:S(2)}) async-start(bf16[16,64,128]{2,1,0:T(8,128)(2,1)} %shard_map.68), calls=%async_computation | async-start | bytes 524288 | tf_op jit(solution)/shard_map/all_to_all | solution.py:31
  20.0 15.4 %all-to-all-done = bf16[16,64,128]{2,1,0:T(8,128)(2,1)S(1)} async-done(((bf16[16,64,128]{2,1,0:T(8,128)(2,1)}), bf16[16,64,128]{2,1,0:T(8,128)(2,1)S(1)}, u32[]{:S(2)}, u32[]{:S(2)}) %all-to-all-start) | async-done | bytes 262176 | tf_op jit(solution)/shard_map/all_to_all | solution.py:31
  36.7 7.0 %all-to-all-start.1 = ((bf16[16,4,64,128]{3,2,1,0:T(8,128)(2,1)}), bf16[16,4,64,128]{3,2,1,0:T(8,128)(2,1)S(1)}, u32[]{:S(2)}, u32[]{:S(2)}) async-start(bf16[16,4,64,128]{3,2,1,0:T(8,128)(2,1)} %bitcast.73), calls=%async_computation.1 | async-start | bytes 2097152 | tf_op jit(solution)/shard_map/all_to_all | solution.py:31
  43.8 5.0 %convolution_convert_fusion.1.head_ref = bf16[1280,896]{1,0:T(8,128)(2,1)} fusion(bf16[896,1280]{1,0:T(8,128)(2,1)S(1)} %copy-done, s32[1280]{0:T(1024)S(1)} %fusion.76), kind=kOutput, calls=%fused_computation.2 | convolution fusion | flops 2938798080 | bytes 4592640 | tf_op jit(solution)/shard_map/dot_general | solution.py:149
  48.8 11.5 %all-to-all-done.1 = bf16[16,4,64,128]{3,2,1,0:T(8,128)(2,1)S(1)} async-done(((bf16[16,4,64,128]{3,2,1,0:T(8,128)(2,1)}), bf16[16,4,64,128]{3,2,1,0:T(8,128)(2,1)S(1)}, u32[]{:S(2)}, u32[]{:S(2)}) %all-to-all-start.1) | async-done | bytes 1048608 | tf_op jit(solution)/shard_map/all_to_all | solution.py:31
  67.3 1.9 collective-permute-start.1
  69.7 5.1 %collective-permute-start.3 = (f32[96,896]{1,0:T(8,128)S(1)}, f32[96,896]{1,0:T(8,128)S(1)}, u32[]{:S(2)}, u32[]{:S(2)}) collective-permute-start(f32[96,896]{1,0:T(8,128)S(1)} %get-tuple-element.43), channel_id=1, source_target_pairs={{0,384},{128,0},{256,128},{384,256},{1,385},{129,1},{257,129},{385... | collective-permute-start | bytes 1032200 | tf_op jit(solution)/shard_map/ppermute | solution.py:23
  75.4 5.5 %collective-permute-done.1 = f32[96,896]{1,0:T(8,128)S(1)} collective-permute-done((f32[96,896]{1,0:T(8,128)S(1)}, f32[96,896]{1,0:T(8,128)S(1)}, u32[]{:S(2)}, u32[]{:S(2)}) %collective-permute-start.1) | collective-permute-done | bytes 344096 | tf_op jit(solution)/shard_map/ppermute | solution.py:23
  81.4 1.9 collective-permute-start.2
  83.9 5.1 %collective-permute-start.4 = (f32[192,896]{1,0:T(8,128)S(1)}, f32[192,896]{1,0:T(8,128)S(1)}, u32[]{:S(2)}, u32[]{:S(2)}) collective-permute-start(f32[192,896]{1,0:T(8,128)S(1)} %fusion.11), channel_id=1, source_target_pairs={{0,384},{128,0},{256,128},{384,256},{1,385},{129,1},{257,129},{385... | collective-permute-start | bytes 2064392 | tf_op jit(solution)/shard_map/ppermute | solution.py:23
  89.6 11.9 %collective-permute-done.2 = f32[192,896]{1,0:T(8,128)S(1)} collective-permute-done((f32[192,896]{1,0:T(8,128)S(1)}, f32[192,896]{1,0:T(8,128)S(1)}, u32[]{:S(2)}, u32[]{:S(2)}) %collective-permute-start.2) | collective-permute-done | bytes 688160 | tf_op jit(solution)/shard_map/ppermute | solution.py:23
  105.9 5.6 %collective-permute-start.5 = (bf16[192,896]{1,0:T(8,128)(2,1)S(1)}, bf16[192,896]{1,0:T(8,128)(2,1)S(1)}, u32[]{:S(2)}, u32[]{:S(2)}) collective-permute-start(bf16[192,896]{1,0:T(8,128)(2,1)S(1)} %get-tuple-element.31.exps0), channel_id=1, source_target_pairs={{0,384},{128,0},{256,128},{384,256},{1,385},{129,1},{257,129},{385... | collective-permute-start | bytes 1032200 | tf_op jit(solution)/shard_map/ppermute | solution.py:23
  111.5 1.9 collective-permute-start.6
  113.4 2.8 %collective-permute-start.7 = (bf16[192,896]{1,0:T(8,128)(2,1)S(1)}, bf16[192,896]{1,0:T(8,128)(2,1)}, u32[]{:S(2)}, u32[]{:S(2)}) collective-permute-start(bf16[192,896]{1,0:T(8,128)(2,1)S(1)} %get-tuple-element.31.exps0), channel_id=1, source_target_pairs={{0,128},{128,256},{256,384},{384,0},{1,129},{129,257},{257,385},{3... | collective-permute-start | bytes 1032200 | tf_op jit(solution)/shard_map/ppermute | solution.py:23
  119.5 4.6 %all-to-all-start.2 = ((f32[32,8,192]{2,1,0:T(8,128)}), f32[32,8,192]{2,1,0:T(8,128)S(1)}, u32[]{:S(2)}, u32[]{:S(2)}) async-start(f32[32,8,192]{2,1,0:T(8,128)} %copy-done.5), calls=%async_computation.2 | async-start | bytes 524288 | tf_op jit(solution)/shard_map/all_to_all | solution.py:31
  124.1 2.9 %fusion.21 = f32[192,1280]{1,0:T(8,128)} fusion(pred[1280,1280]{1,0:T(32,128)(4,1)} %copy-done.7, bf16[4,640,192]{2,1,0:T(8,128)(2,1)} %copy-done.4), kind=kOutput, calls=%fused_computation.34 | convolution fusion | flops 314572800 | bytes 2129920 | tf_op jit(solution)/shard_map/dot_general | solution.py:149
  127.0 6.4 %all-to-all-done.2.facts_ref = f32[32,8,192]{2,1,0:T(8,128)S(1)} async-done(((f32[32,8,192]{2,1,0:T(8,128)}), f32[32,8,192]{2,1,0:T(8,128)S(1)}, u32[]{:S(2)}, u32[]{:S(2)}) %all-to-all-start.2) | async-done | bytes 196640 | tf_op jit(solution)/shard_map/all_to_all | solution.py:31
  134.0 7.3 %all-to-all-start.3 = ((f32[16,4,192]{2,1,0:T(4,128)}), f32[16,4,192]{2,1,0:T(4,128)S(1)}, u32[]{:S(2)}, u32[]{:S(2)}) async-start(f32[16,4,192]{2,1,0:T(4,128)} %shard_map.72), calls=%async_computation.3 | async-start | bytes 131072 | tf_op jit(solution)/shard_map/all_to_all | solution.py:31
  141.3 3.0 %fusion.2 = bf16[192,1280]{1,0:T(8,128)(2,1)} fusion(f32[192,1280]{1,0:T(8,128)} %fusion.21, pred[1280,1280]{1,0:T(32,128)(4,1)} %copy-done.7, bf16[4,640,192]{2,1,0:T(8,128)(2,1)} %copy-done.3), kind=kOutput, calls=%fused_computation.9 | convolution fusion | flops 315064320 | bytes 2621440 | tf_op jit(solution)/shard_map/dot_general | solution.py:149
  144.4 8.6 %all-to-all-done.3.lse_ref = f32[16,4,192]{2,1,0:T(4,128)S(1)} async-done(((f32[16,4,192]{2,1,0:T(4,128)}), f32[16,4,192]{2,1,0:T(4,128)S(1)}, u32[]{:S(2)}, u32[]{:S(2)}) %all-to-all-start.3) | async-done | bytes 49184 | tf_op jit(solution)/shard_map/all_to_all | solution.py:31
  154.6 4.4 %shard_map.73 = (bf16[4,192,896]{2,1,0:T(8,128)(2,1)S(1)}, f32[4,16,64,128]{3,2,1,0:T(8,128)S(1)}, bf16[4,16,64,128]{3,2,1,0:T(8,128)(2,1)S(1)}) custom-call(s32[3]{0:T(128)S(1)} %pad_add_fusion.where_ref, f32[16,4,192]{2,1,0:T(4,128)S(1)} %all-to-all-done.3.lse_ref, f32[32,8,192]{2,1,0:T(8,128)S(1)} %all-to-all-done.2.facts_ref, ...), custom_call_target="tpu_custom_call" | custom-call | tf_op jit(solution)/shard_map/pallas_call | solution.py:35
  164.3 3.4 %convolution_convert_fusion = bf16[896,1280]{1,0:T(8,128)(2,1)} fusion(bf16[768,896]{1,0:T(8,128)(2,1)S(1)} %bitcast.72, bf16[192,1280]{1,0:T(8,128)(2,1)S(1)} %fusion.3, bf16[192,1280]{1,0:T(8,128)(2,1)S(1)} %copy-done.12, bf16[192,1280]{1,0:T(8,128)(2,1)S(1)} %copy-done.11, bf16[192,1280]{1,0:T(8,128)(2,1)S(1)} %copy-done.10), kind=kOutput, calls=%fused_computation.1 | convolution fusion | flops 1770618880 | bytes 5636096 | tf_op jit(solution)/shard_map/dot_general | solution.py:149
  168.1 21.2 %all_to_all.30 = bf16[16,4,64,128]{3,2,1,0:T(8,128)(2,1)S(1)} all-to-all(bf16[16,4,64,128]{3,2,1,0:T(8,128)(2,1)S(1)} %bitcast.74), channel_id=1, replica_groups=mesh['y'=4,'zh'=4,'zl'=4,'x'=4,'c'=2] {'y','x'}, dimensions={0} | all-to-all | bytes 2097152 | tf_op jit(solution)/shard_map/all_to_all | solution.py:31
  189.5 21.3 %all_to_all.31 = bf16[16,64,128]{2,1,0:T(8,128)(2,1)S(1)} all-to-all(bf16[16,64,128]{2,1,0:T(8,128)(2,1)S(1)} %bitcast.76), channel_id=1, replica_groups=mesh['y'=4,'zh'=4,'zl'=4,'x'=4,'c'=2] {'zh','zl'}, dimensions={0} | all-to-all | bytes 524288 | tf_op jit(solution)/shard_map/all_to_all | solution.py:31
  (73 shorter events, 31.5 us)
Async XLA Ops:
  0.6 43.1 %copy-start = (bf16[896,1280]{1,0:T(8,128)(2,1)S(1)}, bf16[896,1280]{1,0:T(8,128)(2,1)}, u32[]{:S(2)}) copy-start(bf16[896,1280]{1,0:T(8,128)(2,1)} %param.6) | copy-start | bytes 6881284
  2.3 33.1 %all-to-all-start = ((bf16[16,64,128]{2,1,0:T(8,128)(2,1)}), bf16[16,64,128]{2,1,0:T(8,128)(2,1)S(1)}, u32[]{:S(2)}, u32[]{:S(2)}) async-start(bf16[16,64,128]{2,1,0:T(8,128)(2,1)} %shard_map.68), calls=%async_computation | async-start | bytes 524288 | tf_op jit(solution)/shard_map/all_to_all | solution.py:31
  36.7 23.5 %all-to-all-start.1 = ((bf16[16,4,64,128]{3,2,1,0:T(8,128)(2,1)}), bf16[16,4,64,128]{3,2,1,0:T(8,128)(2,1)S(1)}, u32[]{:S(2)}, u32[]{:S(2)}) async-start(bf16[16,4,64,128]{3,2,1,0:T(8,128)(2,1)} %bitcast.73), calls=%async_computation.1 | async-start | bytes 2097152 | tf_op jit(solution)/shard_map/all_to_all | solution.py:31
  60.2 4.5 %collective-permute-start = (bf16[4,16,64,128]{3,2,1,0:T(8,128)(2,1)S(1)}, bf16[4,16,64,128]{3,2,1,0:T(8,128)(2,1)S(1)}, u32[]{:S(2)}, u32[]{:S(2)}) collective-permute-start(bf16[4,16,64,128]{3,2,1,0:T(8,128)(2,1)S(1)} %bitcast.69), channel_id=1, source_target_pairs={{0,1},{1,0},{2,3},{3,2},{4,5},{5,4},{6,7},{7,6},{8,9},{9,8},{10,11... | collective-permute-start | bytes 3145736 | tf_op jit(solution)/shard_map/ppermute | solution.py:27
  63.6 54.3 %copy-start.7 = (pred[1280,1280]{1,0:T(32,128)(4,1)}, pred[1280,1280]{1,0:T(32,128)(4,1)S(1)}, u32[]{:S(2)}) copy-start(pred[1280,1280]{1,0:T(32,128)(4,1)S(1)} %iota_compare_fusion) | copy-start | bytes 4915204
  63.9 41.1 %copy-start.4 = (bf16[4,640,192]{2,1,0:T(8,128)(2,1)}, bf16[4,640,192]{2,1,0:T(8,128)(2,1)S(1)}, u32[]{:S(2)}) copy-start(bf16[4,640,192]{2,1,0:T(8,128)(2,1)S(1)} %shard_map.69) | copy-start | bytes 2949124
  64.0 2.3 %copy-start.1 = (bf16[1280,896]{1,0:T(8,128)(2,1)S(1)}, bf16[1280,896]{1,0:T(8,128)(2,1)}, u32[]{:S(2)}) copy-start(bf16[1280,896]{1,0:T(8,128)(2,1)} %convolution_convert_fusion.1.head_ref) | copy-start | bytes 6881284
  66.3 51.6 %copy-start.3 = (bf16[4,640,192]{2,1,0:T(8,128)(2,1)}, bf16[4,640,192]{2,1,0:T(8,128)(2,1)S(1)}, u32[]{:S(2)}) copy-start(bf16[4,640,192]{2,1,0:T(8,128)(2,1)S(1)} %shard_map.70) | copy-start | bytes 2949124
  67.3 13.6 %collective-permute-start.1 = (f32[96,896]{1,0:T(8,128)S(1)}, f32[96,896]{1,0:T(8,128)S(1)}, u32[]{:S(2)}, u32[]{:S(2)}) collective-permute-start(f32[96,896]{1,0:T(8,128)S(1)} %get-tuple-element.42), channel_id=1, source_target_pairs={{0,128},{128,256},{256,384},{384,0},{1,129},{129,257},{257,385},{3... | collective-permute-start | bytes 1032200 | tf_op jit(solution)/shard_map/ppermute | solution.py:23
  69.7 13.6 %collective-permute-start.3 = (f32[96,896]{1,0:T(8,128)S(1)}, f32[96,896]{1,0:T(8,128)S(1)}, u32[]{:S(2)}, u32[]{:S(2)}) collective-permute-start(f32[96,896]{1,0:T(8,128)S(1)} %get-tuple-element.43), channel_id=1, source_target_pairs={{0,384},{128,0},{256,128},{384,256},{1,385},{129,1},{257,129},{385... | collective-permute-start | bytes 1032200 | tf_op jit(solution)/shard_map/ppermute | solution.py:23
  81.4 7.7 %copy-start.9 = (s32[1,192]{1,0:T(1,128)S(1)}, s32[1,192]{1,0:T(1,128)}, u32[]{:S(2)}) copy-start(s32[1,192]{1,0:T(1,128)} %param.9) | copy-start | bytes 2308
  81.4 20.2 %collective-permute-start.2 = (f32[192,896]{1,0:T(8,128)S(1)}, f32[192,896]{1,0:T(8,128)S(1)}, u32[]{:S(2)}, u32[]{:S(2)}) collective-permute-start(f32[192,896]{1,0:T(8,128)S(1)} %fusion.12), channel_id=1, source_target_pairs={{0,128},{128,256},{256,384},{384,0},{1,129},{129,257},{257,385},{3... | collective-permute-start | bytes 2064392 | tf_op jit(solution)/shard_map/ppermute | solution.py:23
  83.9 19.4 %collective-permute-start.4 = (f32[192,896]{1,0:T(8,128)S(1)}, f32[192,896]{1,0:T(8,128)S(1)}, u32[]{:S(2)}, u32[]{:S(2)}) collective-permute-start(f32[192,896]{1,0:T(8,128)S(1)} %fusion.11), channel_id=1, source_target_pairs={{0,384},{128,0},{256,128},{384,256},{1,385},{129,1},{257,129},{385... | collective-permute-start | bytes 2064392 | tf_op jit(solution)/shard_map/ppermute | solution.py:23
  104.2 7.3 %copy-start.5 = (f32[32,8,192]{2,1,0:T(8,128)}, f32[32,8,192]{2,1,0:T(8,128)S(1)}, u32[]{:S(2)}) copy-start(f32[32,8,192]{2,1,0:T(8,128)S(1)} %get-tuple-element.27) | copy-start | bytes 589828
  105.9 38.5 %collective-permute-start.5 = (bf16[192,896]{1,0:T(8,128)(2,1)S(1)}, bf16[192,896]{1,0:T(8,128)(2,1)S(1)}, u32[]{:S(2)}, u32[]{:S(2)}) collective-permute-start(bf16[192,896]{1,0:T(8,128)(2,1)S(1)} %get-tuple-element.31.exps0), channel_id=1, source_target_pairs={{0,384},{128,0},{256,128},{384,256},{1,385},{129,1},{257,129},{385... | collective-permute-start | bytes 1032200 | tf_op jit(solution)/shard_map/ppermute | solution.py:23
  111.5 32.9 %collective-permute-start.6 = (bf16[192,896]{1,0:T(8,128)(2,1)S(1)}, bf16[192,896]{1,0:T(8,128)(2,1)}, u32[]{:S(2)}, u32[]{:S(2)}) collective-permute-start(bf16[192,896]{1,0:T(8,128)(2,1)S(1)} %get-tuple-element.31.exps0), channel_id=1, source_target_pairs={{0,256},{128,384},{256,0},{384,128},{1,257},{129,385},{257,1},{385... | collective-permute-start | bytes 1032200 | tf_op jit(solution)/shard_map/ppermute | solution.py:23
  113.4 30.9 %collective-permute-start.7 = (bf16[192,896]{1,0:T(8,128)(2,1)S(1)}, bf16[192,896]{1,0:T(8,128)(2,1)}, u32[]{:S(2)}, u32[]{:S(2)}) collective-permute-start(bf16[192,896]{1,0:T(8,128)(2,1)S(1)} %get-tuple-element.31.exps0), channel_id=1, source_target_pairs={{0,128},{128,256},{256,384},{384,0},{1,129},{129,257},{257,385},{3... | collective-permute-start | bytes 1032200 | tf_op jit(solution)/shard_map/ppermute | solution.py:23
  119.5 13.8 %all-to-all-start.2 = ((f32[32,8,192]{2,1,0:T(8,128)}), f32[32,8,192]{2,1,0:T(8,128)S(1)}, u32[]{:S(2)}, u32[]{:S(2)}) async-start(f32[32,8,192]{2,1,0:T(8,128)} %copy-done.5), calls=%async_computation.2 | async-start | bytes 524288 | tf_op jit(solution)/shard_map/all_to_all | solution.py:31
  134.0 18.9 %all-to-all-start.3 = ((f32[16,4,192]{2,1,0:T(4,128)}), f32[16,4,192]{2,1,0:T(4,128)S(1)}, u32[]{:S(2)}, u32[]{:S(2)}) async-start(f32[16,4,192]{2,1,0:T(4,128)} %shard_map.72), calls=%async_computation.3 | async-start | bytes 131072 | tf_op jit(solution)/shard_map/all_to_all | solution.py:31
  154.6 6.3 %copy-start.8 = (pred[1280,1280]{1,0:T(32,128)(4,1)S(1)}, pred[1280,1280]{1,0:T(32,128)(4,1)}, u32[]{:S(2)}) copy-start(pred[1280,1280]{1,0:T(32,128)(4,1)} %copy-done.7) | copy-start | bytes 4915204
  159.0 8.8 %collective-permute-start.8 = (bf16[4,16,64,128]{3,2,1,0:T(8,128)(2,1)S(1)}, bf16[4,16,64,128]{3,2,1,0:T(8,128)(2,1)S(1)}, u32[]{:S(2)}, u32[]{:S(2)}) collective-permute-start(bf16[4,16,64,128]{3,2,1,0:T(8,128)(2,1)S(1)} %get-tuple-element.36), channel_id=1, source_target_pairs={{0,1},{1,0},{2,3},{3,2},{4,5},{5,4},{6,7},{7,6},{8,9},{9,8},{10,11... | collective-permute-start | bytes 3145736 | tf_op jit(solution)/shard_map/ppermute | solution.py:27
  162.5 1.8 copy-start.10
  162.6 1.8 copy-start.11
  162.6 1.8 copy-start.12
  (2 other events, 2.5 us)

commit v5 on v4

--- a/solution.py
+++ b/solution.py
@@ -16,6 +16,7 @@
 COLS, TOK, HIGH, EXTRA = 40, 192, 64, 24
 f32, bf16, i32 = jnp.float32, jnp.bfloat16, jnp.int32
 VMEM = pl.BlockSpec(memory_space=pltpu.VMEM)
+FREE = pl.BlockSpec()
 SMEM = pl.BlockSpec(memory_space=pltpu.SMEM)
 
 
@@ -82,13 +83,14 @@
     logits = logits_ref[...]
     top = jnp.max(logits, axis=1, keepdims=True)
     shifted = jnp.exp(logits - top)
-    lse = top + jnp.log(jnp.sum(shifted, axis=1, keepdims=True))
+    total = jnp.sum(shifted, axis=1, keepdims=True)
+    lse = top + jnp.log(total)
     places = lax.broadcasted_iota(i32, logits.shape, 1)
     at_target = jnp.sum(jnp.where(place_ref[...] == places, logits, 0.0), axis=1, keepdims=True)
-    exps_ref[...] = shifted.astype(bf16)
+    exps_ref[...] = (shifted * (1.0 / total)).astype(bf16)
     same = eye()
-    lanes = [jnp.sum(jnp.where(same, v, 0.0), axis=0, keepdims=True) for v in (lse, top, at_target)]
-    facts = jnp.concatenate(lanes + [rows_ref[...], jnp.zeros((3, TOK), f32)], axis=0)
+    lanes = [jnp.sum(jnp.where(same, v, 0.0), axis=0, keepdims=True) for v in (lse, at_target)]
+    facts = jnp.concatenate(lanes + [rows_ref[...]], axis=0)
     for k in range(32):
         facts_ref[k] = facts
 
@@ -119,9 +121,9 @@
         b = lax.rem(where_ref[2] + r, BINS)
         mine = facts_ref[8 * b + where_ref[0]]
         norm = norms_ref[pl.ds(b, 1)]
-        scale = column(mine[3:4] * jnp.exp(mine[1:2] - norm))
-        hit = column(mine[3:4] * (jnp.exp(mine[2:3] - norm) - 1.0))
-        target = column(mine[4:5]).astype(i32)
+        scale = column(mine[2:3] * jnp.exp(mine[0:1] - norm))
+        hit = column(mine[2:3] * (jnp.exp(mine[1:2] - norm) - 1.0))
+        target = column(mine[3:4]).astype(i32)
         grads = jnp.where(target == places, hit, exps_ref[...].astype(f32) * scale).astype(bf16)
         grads_ref[b] = grads
         half = head_ref.shape[0] // 2
@@ -136,6 +138,13 @@
                 ref[b, p] = packed(terms[COLS * p : COLS * (p + 1)]).astype(ref.dtype)
 
 
+def head_kernel(own_ref, other_ref, grads_ref, o_ref):
+    half = own_ref.shape[1]
+    for h, ref in enumerate([own_ref, other_ref]):
+        total = sum(jnp.dot(ref[b], grads_ref[b], preferred_element_type=f32) for b in range(BINS))
+        o_ref[h * half : (h + 1) * half, :] = total.astype(bf16)
+
+
 def column_order(width):
     half = width // 2
     p = lax.broadcasted_iota(i32, (width, 1), 0)
@@ -160,14 +169,15 @@
     own_packed = exchange(
         jnp.broadcast_to(along_z, (BINS, 4, 4, 64, 128)).reshape(16, 4, 64, 128), ("y", "x")
     ).reshape(BINS, 16, 64, 128)
-    other_packed = swap_core(own_packed)
     order = column_order(width)
     head_t = dot(order, head, 1, 1).astype(bf16)
+    own_packed, head_t = lax.optimization_barrier((own_packed, head_t))
+    other_packed = swap_core(own_packed)
     unpack = functools.partial(
         call, unpack_kernel, shape(BINS, hw, TOK, dtype=bf16), [VMEM], nbytes=4 * 2**20
     )
     own_cols = unpack(own_packed)
-    own_cols, head_t, other_packed = lax.optimization_barrier((own_cols, head_t, other_packed))
+    own_cols, other_packed = lax.optimization_barrier((own_cols, other_packed))
     other_cols = unpack(other_packed)
 
     def pick(a, b):
@@ -199,25 +209,18 @@
 
     exps, facts = call(
         softmax_kernel,
-        [shape(TOK, vocab_rows, dtype=bf16), shape(32, 8, TOK)],
+        [shape(TOK, vocab_rows, dtype=bf16), shape(32, 4, TOK)],
         [VMEM] * 3,
         own + up + down,
         place,
         rows,
     )
-    exps, facts, own_cols, other_cols = lax.optimization_barrier((exps, facts, own_cols, other_cols))
+    exps, facts = lax.optimization_barrier((exps, facts))
 
     every_exp = [exps, shift(exps, 3), shift(exps, 2), shift(exps, 1)]
     facts = exchange(facts, ("y", "x", "c"))
     lse = exchange(call(combine_kernel, shape(16, BINS, TOK), [VMEM], facts), Z)
     lse, facts, every_exp = lax.optimization_barrier((lse, facts, every_exp))
-
-    features = jnp.concatenate(
-        [
-            (dot(own_cols[b], order[:hw], 0, 0) + dot(other_cols[b], order[hw:], 0, 0)).astype(bf16)
-            for b in range(BINS)
-        ]
-    )
 
     grads, kept, sent = call(
         grad_kernel,
@@ -226,7 +229,7 @@
             shape(BINS, 16, 64, 128),
             shape(BINS, 16, 64, 128, dtype=bf16),
         ],
-        [SMEM] + [VMEM] * 7,
+        [SMEM] + [VMEM] * 6 + [FREE],
         here,
         lse,
         facts,
@@ -235,13 +238,16 @@
         scratch=[pltpu.VMEM((BINS, TOK), f32)],
     )
     terms = swap_core(sent)
-    grad_head = dot(grads.reshape(BINS * TOK, vocab_rows), features, 0, 0).astype(bf16)
-    terms, grad_head = lax.optimization_barrier((terms, grad_head))
+    head_terms = call(
+        head_kernel, shape(width, vocab_rows, dtype=bf16), [FREE, FREE, VMEM], own_cols, other_cols, grads, flops=2 * 10**9
+    )
+    terms, head_terms = lax.optimization_barrier((terms, head_terms))
     terms = (kept + terms.astype(f32)).astype(bf16).reshape(16, 4, 64, 128)
     terms = exchange(terms, ("y", "x")).reshape(BINS, 4, 4, 64, 128)
     terms = jnp.sum(terms.astype(f32), axis=1).astype(bf16).reshape(16, 64, 128)
     terms = exchange(terms, Z)
     grad_hidden = unpacked(jnp.sum(terms.astype(f32), axis=0)).astype(bf16).T
+    grad_head = dot(head_terms, order, 0, 0).astype(bf16)
     return (grad_hidden, grad_head)
 
 

time: 213 us -> 208 us (0.977)
  blocking collectives: 42.5 us -> 66.8 us
  starting transfers between devices: 62.4 us -> 47.9 us
  waiting for transfers between devices: 61.8 us -> 52.2 us
  matrix products: 26.6 us -> 19.9 us
  Pallas kernels: 6.94 us -> 9.68 us
    all_to_all x2 -> x3, blocking collectives: 42.5 us -> 66.8 us  [exchange(): return lax.all_to_all(a, axes, 0, 0, tiled=True)]
    all_to_all x4 -> x3, starting transfers between devices: 34.2 us -> 18.8 us  [exchange(): return lax.all_to_all(a, axes, 0, 0, tiled=True)]
    all_to_all x4 -> x3, waiting for transfers between devices: 41.8 us -> 34.7 us  [exchange(): return lax.all_to_all(a, axes, 0, 0, tiled=True)]
    dot_general x18 -> x10, matrix products: 26.6 us -> 19.9 us  [dot(): lax.dot_general(a, b, (((ca,), (cb,)), ((), ())), preferred_element_type=...]
    ppermute x7, waiting for transfers between devices: 19.2 us -> 15.4 us  [shift(): return lax.ppermute(a, 'y', [(i, (i + k) % BINS) for i in range(BINS)])]
    pallas_call x6 -> x7, Pallas kernels: 6.94 us -> 9.68 us  [call(): pl.pallas_call(kernel, out_shape=out, in_specs=ins, scratch_shapes=list(s...]
  transfers between devices with their start and end apart: 13 -> 12, of which waited for: 8 -> 7; matrix products, arithmetic and copies ran while one was open for 13% -> 9% of each run, Pallas kernels for 0% -> 2%
where the time goes in v5:
time: 208 us; the launch traced here: 207 us
  blocking collectives  66.8 us (32%)
  waiting for transfers between devices  52.2 us (25%)
  starting transfers between devices  47.9 us (23%)
  matrix products  19.9 us (10%)
  Pallas kernels  9.68 us (5%)
  local copies, waits for them, and re-layouts  5.72 us (3%)
  other arithmetic  3.4 us (2%)
    all_to_all x3, blocking collectives, exchange(): return lax.all_to_all(a, axes, 0, 0, tiled=True)  66.8 us
    all_to_all x3, waiting for transfers between devices, exchange(): return lax.all_to_all(a, axes, 0, 0, tiled=True)  34.7 us
    ppermute x7, starting transfers between devices, shift(): return lax.ppermute(a, 'y', [(i, (i + k) % BINS) for i in range(BINS)])  25.1 us
    dot_general x10, matrix products, dot(): lax.dot_general(a, b, (((ca,), (cb,)), ((), ())), preferred_element_type=...  19.9 us
    all_to_all x3, starting transfers between devices, exchange(): return lax.all_to_all(a, axes, 0, 0, tiled=True)  18.8 us
    ppermute x7, waiting for transfers between devices, shift(): return lax.ppermute(a, 'y', [(i, (i + k) % BINS) for i in range(BINS)])  15.4 us
    pallas_call x7, Pallas kernels, call(): pl.pallas_call(kernel, out_shape=out, in_specs=ins, scratch_shapes=list(s...  9.68 us
    unnamed x26, local copies, waits for them, and re-layouts  4.22 us
  transfers between devices with their start and end apart: 12, of which 7 were waited for; matrix products, arithmetic and copies ran while one was open for 9% of the time, Pallas kernels for 2%

profile of v5, /device:TPU:32, one launch (start us, length us, event | category | flops | bytes accessed | tf_op | source)
XLA Modules:
  0.0 206.7 jit_solution(7806027254055613602)
XLA Ops:
  1.6 32.9 %all_to_all.30 = bf16[16,64,128]{2,1,0:T(8,128)(2,1)S(1)} all-to-all(bf16[16,64,128]{2,1,0:T(8,128)(2,1)S(1)} %shard_map.68), channel_id=1, replica_groups=mesh['y'=4,'zh'=4,'zl'=4,'x'=4,'c'=2] {'zh','zl'}, dimensions={0} | all-to-all | bytes 524288 | tf_op jit(solution)/shard_map/all_to_all | solution.py:32
  35.8 7.0 %all-to-all-start.1 = ((bf16[16,4,64,128]{3,2,1,0:T(8,128)(2,1)}), bf16[16,4,64,128]{3,2,1,0:T(8,128)(2,1)S(1)}, u32[]{:S(2)}, u32[]{:S(2)}) async-start(bf16[16,4,64,128]{3,2,1,0:T(8,128)(2,1)} %bitcast.51), calls=%async_computation.1 | async-start | bytes 2097152 | tf_op jit(solution)/shard_map/all_to_all | solution.py:32
  42.9 5.0 %fusion.2.head_ref = bf16[1280,896]{1,0:T(8,128)(2,1)} fusion(bf16[896,1280]{1,0:T(8,128)(2,1)S(1)} %copy-done, s32[1280]{0:T(1024)S(1)} %fusion.47), kind=kOutput, calls=%fused_computation.3 | convolution fusion | flops 2938798080 | bytes 4592640 | tf_op jit(solution)/shard_map/dot_general | solution.py:158
  47.9 11.5 %all-to-all-done.1 = bf16[16,4,64,128]{3,2,1,0:T(8,128)(2,1)S(1)} async-done(((bf16[16,4,64,128]{3,2,1,0:T(8,128)(2,1)}), bf16[16,4,64,128]{3,2,1,0:T(8,128)(2,1)S(1)}, u32[]{:S(2)}, u32[]{:S(2)}) %all-to-all-start.1) | async-done | bytes 1048608 | tf_op jit(solution)/shard_map/all_to_all | solution.py:32
  61.9 2.1 %collective-permute-done.a_ref = bf16[4,16,64,128]{3,2,1,0:T(8,128)(2,1)} collective-permute-done((bf16[4,16,64,128]{3,2,1,0:T(8,128)(2,1)S(1)}, bf16[4,16,64,128]{3,2,1,0:T(8,128)(2,1)}, u32[]{:S(2)}, u32[]{:S(2)}) %collective-permute-start) | collective-permute-done | bytes 1048608 | tf_op jit(solution)/shard_map/ppermute | solution.py:28
  66.7 1.9 collective-permute-start.1
  69.1 5.1 %collective-permute-start.3 = (f32[96,896]{1,0:T(8,128)S(1)}, f32[96,896]{1,0:T(8,128)S(1)}, u32[]{:S(2)}, u32[]{:S(2)}) collective-permute-start(f32[96,896]{1,0:T(8,128)S(1)} %get-tuple-element.37), channel_id=1, source_target_pairs={{0,384},{128,0},{256,128},{384,256},{1,385},{129,1},{257,129},{385... | collective-permute-start | bytes 1032200 | tf_op jit(solution)/shard_map/ppermute | solution.py:24
  74.8 5.1 %collective-permute-done.1 = f32[96,896]{1,0:T(8,128)S(1)} collective-permute-done((f32[96,896]{1,0:T(8,128)S(1)}, f32[96,896]{1,0:T(8,128)S(1)}, u32[]{:S(2)}, u32[]{:S(2)}) %collective-permute-start.1) | collective-permute-done | bytes 344096 | tf_op jit(solution)/shard_map/ppermute | solution.py:24
  81.2 2.0 collective-permute-start.2
  84.6 5.1 %collective-permute-start.4 = (f32[192,896]{1,0:T(8,128)}, f32[192,896]{1,0:T(8,128)}, u32[]{:S(2)}, u32[]{:S(2)}) collective-permute-start(f32[192,896]{1,0:T(8,128)} %pad_add_fusion), channel_id=1, source_target_pairs={{0,384},{128,0},{256,128},{384,256},{1,385},{129,1},{257,129},{385... | collective-permute-start | bytes 2064392 | tf_op jit(solution)/shard_map/ppermute | solution.py:24
  93.7 7.6 %collective-permute-done.2 = f32[192,896]{1,0:T(8,128)S(1)} collective-permute-done((f32[192,896]{1,0:T(8,128)}, f32[192,896]{1,0:T(8,128)S(1)}, u32[]{:S(2)}, u32[]{:S(2)}) %collective-permute-start.2) | collective-permute-done | bytes 688160 | tf_op jit(solution)/shard_map/ppermute | solution.py:24
  101.3 2.6 %collective-permute-done.4 = f32[192,896]{1,0:T(8,128)} collective-permute-done((f32[192,896]{1,0:T(8,128)}, f32[192,896]{1,0:T(8,128)}, u32[]{:S(2)}, u32[]{:S(2)}) %collective-permute-start.4) | collective-permute-done | bytes 688160 | tf_op jit(solution)/shard_map/ppermute | solution.py:24
  107.5 7.1 %collective-permute-start.6 = (bf16[192,896]{1,0:T(8,128)(2,1)S(1)}, bf16[192,896]{1,0:T(8,128)(2,1)S(1)}, u32[]{:S(2)}, u32[]{:S(2)}) collective-permute-start(bf16[192,896]{1,0:T(8,128)(2,1)S(1)} %get-tuple-element.27.exps0), channel_id=1, source_target_pairs={{0,256},{128,384},{256,0},{384,128},{1,257},{129,385},{257,1},{385... | collective-permute-start | bytes 1032200 | tf_op jit(solution)/shard_map/ppermute | solution.py:24
  114.5 1.9 collective-permute-start.5
  116.4 12.2 %all_to_all.31.facts_ref = f32[32,4,192]{2,1,0:T(4,128)S(1)} all-to-all(f32[32,4,192]{2,1,0:T(4,128)S(1)} %get-tuple-element.23), channel_id=1, replica_groups=mesh['y'=4,'zh'=4,'zl'=4,'x'=4,'c'=2] {'y','x','c'}, dimensions={0} | all-to-all | bytes 196608 | tf_op jit(solution)/shard_map/all_to_all | solution.py:32
  129.3 7.3 %all-to-all-start.3 = ((f32[16,4,192]{2,1,0:T(4,128)}), f32[16,4,192]{2,1,0:T(4,128)S(1)}, u32[]{:S(2)}, u32[]{:S(2)}) async-start(f32[16,4,192]{2,1,0:T(4,128)} %copy-done.7), calls=%async_computation.3 | async-start | bytes 131072 | tf_op jit(solution)/shard_map/all_to_all | solution.py:32
  136.7 12.0 %all-to-all-done.3.lse_ref = f32[16,4,192]{2,1,0:T(4,128)S(1)} async-done(((f32[16,4,192]{2,1,0:T(4,128)}), f32[16,4,192]{2,1,0:T(4,128)S(1)}, u32[]{:S(2)}, u32[]{:S(2)}) %all-to-all-start.3) | async-done | bytes 49184 | tf_op jit(solution)/shard_map/all_to_all | solution.py:32
  150.4 4.3 %shard_map.73 = (bf16[4,192,896]{2,1,0:T(8,128)(2,1)S(1)}, f32[4,16,64,128]{3,2,1,0:T(8,128)S(1)}, bf16[4,16,64,128]{3,2,1,0:T(8,128)(2,1)S(1)}) custom-call(s32[3]{0:T(128)S(1)} %pad_add_fusion.2.where_ref, f32[16,4,192]{2,1,0:T(4,128)S(1)} %all-to-all-done.3.lse_ref, f32[32,4,192]{2,1,0:T(4,128)S(1)} %all_to_all.31.facts_ref, ...), custom_call_target="tpu_custom_call" | custom-call | tf_op jit(solution)/shard_map/pallas_call | solution.py:36
  154.8 2.1 %collective-permute-start.8 = (bf16[4,16,64,128]{3,2,1,0:T(8,128)(2,1)S(1)}, bf16[4,16,64,128]{3,2,1,0:T(8,128)(2,1)S(1)}, u32[]{:S(2)}, u32[]{:S(2)}) collective-permute-start(bf16[4,16,64,128]{3,2,1,0:T(8,128)(2,1)S(1)} %get-tuple-element.32), channel_id=1, source_target_pairs={{0,1},{1,0},{2,3},{3,2},{4,5},{5,4},{6,7},{7,6},{8,9},{9,8},{10,11... | collective-permute-start | bytes 3145736 | tf_op jit(solution)/shard_map/ppermute | solution.py:28
  156.9 2.9 %shard_map.74 = bf16[1280,896]{1,0:T(8,128)(2,1)S(1)} custom-call(bf16[4,640,192]{2,1,0:T(8,128)(2,1)S(1)} %copy-done.4, bf16[4,640,192]{2,1,0:T(8,128)(2,1)S(1)} %copy-done.6, bf16[4,192,896]{2,1,0:T(8,128)(2,1)S(1)} %get-tuple-element.33.grads_ref), custom_call_target="tpu_custom_call" | custom-call | flops 2000000000 | tf_op jit(solution)/shard_map/pallas_call | solution.py:36
  161.2 21.7 %all_to_all.32 = bf16[16,4,64,128]{3,2,1,0:T(8,128)(2,1)S(1)} all-to-all(bf16[16,4,64,128]{3,2,1,0:T(8,128)(2,1)S(1)} %bitcast.52), channel_id=1, replica_groups=mesh['y'=4,'zh'=4,'zl'=4,'x'=4,'c'=2] {'y','x'}, dimensions={0} | all-to-all | bytes 2097152 | tf_op jit(solution)/shard_map/all_to_all | solution.py:32
  183.8 4.4 %all-to-all-start.5 = ((bf16[16,64,128]{2,1,0:T(8,128)(2,1)}), bf16[16,64,128]{2,1,0:T(8,128)(2,1)S(1)}, u32[]{:S(2)}, u32[]{:S(2)}) async-start(bf16[16,64,128]{2,1,0:T(8,128)(2,1)} %bitcast.21), calls=%async_computation.5 | async-start | bytes 524288 | tf_op jit(solution)/shard_map/all_to_all | solution.py:32
  188.2 6.5 %fusion.3 = bf16[896,1280]{1,0:T(8,128)(2,1)} fusion(bf16[1280,896]{1,0:T(8,128)(2,1)} %copy-done.9, s32[1280]{0:T(1024)S(1)} %fusion.47), kind=kOutput, calls=%fused_computation.4 | convolution fusion | flops 2938798080 | bytes 4592640 | tf_op jit(solution)/shard_map/dot_general | solution.py:158
  194.7 11.2 %all-to-all-done.5 = bf16[16,64,128]{2,1,0:T(8,128)(2,1)S(1)} async-done(((bf16[16,64,128]{2,1,0:T(8,128)(2,1)}), bf16[16,64,128]{2,1,0:T(8,128)(2,1)S(1)}, u32[]{:S(2)}, u32[]{:S(2)}) %all-to-all-start.5) | async-done | bytes 262176 | tf_op jit(solution)/shard_map/all_to_all | solution.py:32
  (65 shorter events, 23.8 us)
Async XLA Ops:
  0.6 42.2 %copy-start = (bf16[896,1280]{1,0:T(8,128)(2,1)S(1)}, bf16[896,1280]{1,0:T(8,128)(2,1)}, u32[]{:S(2)}) copy-start(bf16[896,1280]{1,0:T(8,128)(2,1)} %param.6) | copy-start | bytes 6881284
  0.6 0.9 copy-start.8
  35.8 23.5 %all-to-all-start.1 = ((bf16[16,4,64,128]{3,2,1,0:T(8,128)(2,1)}), bf16[16,4,64,128]{3,2,1,0:T(8,128)(2,1)S(1)}, u32[]{:S(2)}, u32[]{:S(2)}) async-start(bf16[16,4,64,128]{3,2,1,0:T(8,128)(2,1)} %bitcast.51), calls=%async_computation.1 | async-start | bytes 2097152 | tf_op jit(solution)/shard_map/all_to_all | solution.py:32
  42.9 18.4 %copy-start.10 = (s32[1,192]{1,0:T(1,128)S(1)}, s32[1,192]{1,0:T(1,128)}, u32[]{:S(2)}) copy-start(s32[1,192]{1,0:T(1,128)} %param.9) | copy-start | bytes 2308
  42.9 18.4 %copy-start.11 = (s32[1,192]{1,0:T(1,128)S(1)}, s32[1,192]{1,0:T(1,128)}, u32[]{:S(2)}) copy-start(s32[1,192]{1,0:T(1,128)} %param.8) | copy-start | bytes 2308
  59.3 4.7 %collective-permute-start = (bf16[4,16,64,128]{3,2,1,0:T(8,128)(2,1)S(1)}, bf16[4,16,64,128]{3,2,1,0:T(8,128)(2,1)}, u32[]{:S(2)}, u32[]{:S(2)}) collective-permute-start(bf16[4,16,64,128]{3,2,1,0:T(8,128)(2,1)S(1)} %bitcast.48), channel_id=1, source_target_pairs={{0,1},{1,0},{2,3},{3,2},{4,5},{5,4},{6,7},{7,6},{8,9},{9,8},{10,11... | collective-permute-start | bytes 3145736 | tf_op jit(solution)/shard_map/ppermute | solution.py:28
  61.9 12.3 %copy-start.3 = (bf16[4,640,192]{2,1,0:T(8,128)(2,1)}, bf16[4,640,192]{2,1,0:T(8,128)(2,1)S(1)}, u32[]{:S(2)}) copy-start(bf16[4,640,192]{2,1,0:T(8,128)(2,1)S(1)} %shard_map.69.own_ref) | copy-start | bytes 2949124
  61.9 3.7 %copy-start.1 = (bf16[1280,896]{1,0:T(8,128)(2,1)S(1)}, bf16[1280,896]{1,0:T(8,128)(2,1)}, u32[]{:S(2)}) copy-start(bf16[1280,896]{1,0:T(8,128)(2,1)} %fusion.2.head_ref) | copy-start | bytes 6881284
  65.6 17.7 %copy-start.5 = (bf16[4,640,192]{2,1,0:T(8,128)(2,1)}, bf16[4,640,192]{2,1,0:T(8,128)(2,1)S(1)}, u32[]{:S(2)}) copy-start(bf16[4,640,192]{2,1,0:T(8,128)(2,1)S(1)} %shard_map.70.other_ref) | copy-start | bytes 2949124
  66.7 13.2 %collective-permute-start.1 = (f32[96,896]{1,0:T(8,128)S(1)}, f32[96,896]{1,0:T(8,128)S(1)}, u32[]{:S(2)}, u32[]{:S(2)}) collective-permute-start(f32[96,896]{1,0:T(8,128)S(1)} %get-tuple-element.36), channel_id=1, source_target_pairs={{0,128},{128,256},{256,384},{384,0},{1,129},{129,257},{257,385},{3... | collective-permute-start | bytes 1032200 | tf_op jit(solution)/shard_map/ppermute | solution.py:24
  69.1 14.2 %collective-permute-start.3 = (f32[96,896]{1,0:T(8,128)S(1)}, f32[96,896]{1,0:T(8,128)S(1)}, u32[]{:S(2)}, u32[]{:S(2)}) collective-permute-start(f32[96,896]{1,0:T(8,128)S(1)} %get-tuple-element.37), channel_id=1, source_target_pairs={{0,384},{128,0},{256,128},{384,256},{1,385},{129,1},{257,129},{385... | collective-permute-start | bytes 1032200 | tf_op jit(solution)/shard_map/ppermute | solution.py:24
  81.2 8.6 %copy-start.12 = (s32[1,192]{1,0:T(1,128)S(1)}, s32[1,192]{1,0:T(1,128)}, u32[]{:S(2)}) copy-start(s32[1,192]{1,0:T(1,128)} %param.7) | copy-start | bytes 2308
  81.2 20.1 %collective-permute-start.2 = (f32[192,896]{1,0:T(8,128)}, f32[192,896]{1,0:T(8,128)S(1)}, u32[]{:S(2)}, u32[]{:S(2)}) collective-permute-start(f32[192,896]{1,0:T(8,128)} %pad_add_fusion.1), channel_id=1, source_target_pairs={{0,128},{128,256},{256,384},{384,0},{1,129},{129,257},{257,385},{3... | collective-permute-start | bytes 2064392 | tf_op jit(solution)/shard_map/ppermute | solution.py:24
  84.6 19.3 %collective-permute-start.4 = (f32[192,896]{1,0:T(8,128)}, f32[192,896]{1,0:T(8,128)}, u32[]{:S(2)}, u32[]{:S(2)}) collective-permute-start(f32[192,896]{1,0:T(8,128)} %pad_add_fusion), channel_id=1, source_target_pairs={{0,384},{128,0},{256,128},{384,256},{1,385},{129,1},{257,129},{385... | collective-permute-start | bytes 2064392 | tf_op jit(solution)/shard_map/ppermute | solution.py:24
  105.5 43.2 %collective-permute-start.7 = (bf16[192,896]{1,0:T(8,128)(2,1)S(1)}, bf16[192,896]{1,0:T(8,128)(2,1)S(1)}, u32[]{:S(2)}, u32[]{:S(2)}) collective-permute-start(bf16[192,896]{1,0:T(8,128)(2,1)S(1)} %get-tuple-element.27.exps0), channel_id=1, source_target_pairs={{0,128},{128,256},{256,384},{384,0},{1,129},{129,257},{257,385},{3... | collective-permute-start | bytes 1032200 | tf_op jit(solution)/shard_map/ppermute | solution.py:24
  107.5 41.3 %collective-permute-start.6 = (bf16[192,896]{1,0:T(8,128)(2,1)S(1)}, bf16[192,896]{1,0:T(8,128)(2,1)S(1)}, u32[]{:S(2)}, u32[]{:S(2)}) collective-permute-start(bf16[192,896]{1,0:T(8,128)(2,1)S(1)} %get-tuple-element.27.exps0), channel_id=1, source_target_pairs={{0,256},{128,384},{256,0},{384,128},{1,257},{129,385},{257,1},{385... | collective-permute-start | bytes 1032200 | tf_op jit(solution)/shard_map/ppermute | solution.py:24
  114.5 34.3 %collective-permute-start.5 = (bf16[192,896]{1,0:T(8,128)(2,1)S(1)}, bf16[192,896]{1,0:T(8,128)(2,1)}, u32[]{:S(2)}, u32[]{:S(2)}) collective-permute-start(bf16[192,896]{1,0:T(8,128)(2,1)S(1)} %get-tuple-element.27.exps0), channel_id=1, source_target_pairs={{0,384},{128,0},{256,128},{384,256},{1,385},{129,1},{257,129},{385... | collective-permute-start | bytes 1032200 | tf_op jit(solution)/shard_map/ppermute | solution.py:24
  129.3 19.4 %all-to-all-start.3 = ((f32[16,4,192]{2,1,0:T(4,128)}), f32[16,4,192]{2,1,0:T(4,128)S(1)}, u32[]{:S(2)}, u32[]{:S(2)}) async-start(f32[16,4,192]{2,1,0:T(4,128)} %copy-done.7), calls=%async_computation.3 | async-start | bytes 131072 | tf_op jit(solution)/shard_map/all_to_all | solution.py:32
  148.8 1.6 copy-start.2
  150.4 6.5 %copy-start.4 = (bf16[4,640,192]{2,1,0:T(8,128)(2,1)S(1)}, bf16[4,640,192]{2,1,0:T(8,128)(2,1)}, u32[]{:S(2)}) copy-start(bf16[4,640,192]{2,1,0:T(8,128)(2,1)} %copy-done.3) | copy-start | bytes 2949124
  150.4 6.5 %copy-start.6 = (bf16[4,640,192]{2,1,0:T(8,128)(2,1)S(1)}, bf16[4,640,192]{2,1,0:T(8,128)(2,1)}, u32[]{:S(2)}) copy-start(bf16[4,640,192]{2,1,0:T(8,128)(2,1)} %copy-done.5) | copy-start | bytes 2949124
  154.8 5.0 %collective-permute-start.8 = (bf16[4,16,64,128]{3,2,1,0:T(8,128)(2,1)S(1)}, bf16[4,16,64,128]{3,2,1,0:T(8,128)(2,1)S(1)}, u32[]{:S(2)}, u32[]{:S(2)}) collective-permute-start(bf16[4,16,64,128]{3,2,1,0:T(8,128)(2,1)S(1)} %get-tuple-element.32), channel_id=1, source_target_pairs={{0,1},{1,0},{2,3},{3,2},{4,5},{5,4},{6,7},{7,6},{8,9},{9,8},{10,11... | collective-permute-start | bytes 3145736 | tf_op jit(solution)/shard_map/ppermute | solution.py:28
  159.8 1.4 copy-start.9
  183.8 22.2 %all-to-all-start.5 = ((bf16[16,64,128]{2,1,0:T(8,128)(2,1)}), bf16[16,64,128]{2,1,0:T(8,128)(2,1)S(1)}, u32[]{:S(2)}, u32[]{:S(2)}) async-start(bf16[16,64,128]{2,1,0:T(8,128)(2,1)} %bitcast.21), calls=%async_computation.5 | async-start | bytes 524288 | tf_op jit(solution)/shard_map/all_to_all | solution.py:32
  (1 other events, 0.6 us)

commit v6 on v5

--- a/solution.py
+++ b/solution.py
@@ -79,7 +79,7 @@
     return lax.broadcasted_iota(i32, (TOK, TOK), 0) == lax.broadcasted_iota(i32, (TOK, TOK), 1)
 
 
-def softmax_kernel(logits_ref, place_ref, rows_ref, exps_ref, facts_ref):
+def softmax_kernel(logits_ref, place_ref, row_ref, exps_ref, lse_ref, facts_ref):
     logits = logits_ref[...]
     top = jnp.max(logits, axis=1, keepdims=True)
     shifted = jnp.exp(logits - top)
@@ -90,52 +90,55 @@
     exps_ref[...] = (shifted * (1.0 / total)).astype(bf16)
     same = eye()
     lanes = [jnp.sum(jnp.where(same, v, 0.0), axis=0, keepdims=True) for v in (lse, at_target)]
-    facts = jnp.concatenate(lanes + [rows_ref[...]], axis=0)
+    facts_ref[...] = jnp.concatenate(lanes + [row_ref[...]], axis=0)
+    for k in range(16):
+        lse_ref[k] = lanes[0]
+
+
+def log_sum_exp(part):
+    top = jnp.max(part, axis=0, keepdims=True)
+    return top + jnp.log(jnp.sum(jnp.exp(part - top), axis=0, keepdims=True))
+
+
+def combine_kernel(lse_ref, facts_ref, o_ref):
+    total = log_sum_exp(jnp.concatenate([lse_ref[k] for k in range(16)], axis=0))
+    rows = jnp.concatenate([total, facts_ref[...]], axis=0)
     for k in range(32):
-        facts_ref[k] = facts
-
-
-def combine_kernel(facts_ref, o_ref):
-    rows = []
-    for b in range(BINS):
-        part = jnp.concatenate([facts_ref[8 * b + k][0:1] for k in range(8)], axis=0)
-        top = jnp.max(part, axis=0, keepdims=True)
-        rows.append(top + jnp.log(jnp.sum(jnp.exp(part - top), axis=0, keepdims=True)))
-    rows = jnp.concatenate(rows, axis=0)
-    for k in range(16):
         o_ref[k] = rows
 
 
-def grad_kernel(where_ref, lse_ref, facts_ref, exps0, exps1, exps2, exps3, head_ref, grads_ref, kept_ref, sent_ref, norms_ref):
-    lse = lse_ref[...]
-    top = jnp.max(lse, axis=0)
-    log_norm = top + jnp.log(jnp.sum(jnp.exp(lse - top[None]), axis=0))
+def put_terms(columns, grads, ref, b):
+    terms = lax.dot_general(columns, grads, (((1,), (1,)), ((), ())), preferred_element_type=f32)
+    for p in range(16):
+        ref[b, p] = packed(terms[COLS * p : COLS * (p + 1)]).astype(ref.dtype)
+
+
+def grad_kernel(where_ref, facts_ref, exps0, exps1, exps2, exps3, head_ref, grads_ref, sent_ref):
     same = eye()
 
     def column(row):
         return jnp.sum(jnp.where(same, row, 0.0), axis=1, keepdims=True)
 
-    norms_ref[...] = log_norm
+    half = head_ref.shape[0] // 2
     places = lax.broadcasted_iota(i32, exps0.shape, 1) + where_ref[1]
     for r, exps_ref in enumerate([exps0, exps1, exps2, exps3]):
         b = lax.rem(where_ref[2] + r, BINS)
+        norm = log_sum_exp(jnp.concatenate([facts_ref[8 * b + k][0:1] for k in range(8)], axis=0))
         mine = facts_ref[8 * b + where_ref[0]]
-        norm = norms_ref[pl.ds(b, 1)]
-        scale = column(mine[2:3] * jnp.exp(mine[0:1] - norm))
-        hit = column(mine[2:3] * (jnp.exp(mine[1:2] - norm) - 1.0))
-        target = column(mine[3:4]).astype(i32)
+        code = mine[3:4].astype(i32)
+        counts = (code & 63).astype(f32)
+        weight = jnp.where(counts > 0, loss_scale / jnp.maximum(counts, 1.0), 0.0)
+        scale = column(weight * jnp.exp(mine[1:2] - norm))
+        hit = column(weight * (jnp.exp(mine[2:3] - norm) - 1.0))
+        target = column((code >> 6).astype(f32)).astype(i32)
         grads = jnp.where(target == places, hit, exps_ref[...].astype(f32) * scale).astype(bf16)
         grads_ref[b] = grads
-        half = head_ref.shape[0] // 2
-        for h, ref in ((1, sent_ref), (0, kept_ref)):
-            terms = lax.dot_general(
-                head_ref[h * half : (h + 1) * half],
-                grads,
-                (((1,), (1,)), ((), ())),
-                preferred_element_type=f32,
-            )
-            for p in range(16):
-                ref[b, p] = packed(terms[COLS * p : COLS * (p + 1)]).astype(ref.dtype)
+        put_terms(head_ref[half:], grads, sent_ref, b)
+
+
+def kept_kernel(head_ref, grads_ref, kept_ref):
+    for b in range(BINS):
+        put_terms(head_ref[: head_ref.shape[0] // 2], grads_ref[b], kept_ref, b)
 
 
 def head_kernel(own_ref, other_ref, grads_ref, o_ref):
@@ -192,6 +195,7 @@
     up = partial_logits(1)
     down = partial_logits(3)
     own = partial_logits(0)
+    up, down = lax.optimization_barrier((up, down))
     nothing = jnp.zeros((half, vocab_rows), f32)
     up = shift(up + jnp.concatenate([from_left, nothing]), 1)
     down = shift(down + jnp.concatenate([nothing, from_right]), 3)
@@ -200,48 +204,42 @@
     seg_ids = segments[0]
     same = (seg_ids[:, None] == seg_ids[None, :]).astype(f32)
     counts = jnp.sum(same * mask_f[None, :], axis=1)
-    weight = loss_scale * mask_f / jnp.maximum(counts, 1.0)
     shard = ((lax.axis_index("zh") * 4 + lax.axis_index("zl")) * 4 + lax.axis_index("x")) * 2
     vocab_start = (shard + lax.axis_index("c")) * vocab_rows
     place = (targets[0] - vocab_start)[:, None]
-    rows = jnp.stack([weight, targets[0].astype(f32)])
+    row = (64 * targets + loss_mask * counts.astype(i32)[None]).astype(f32)
     here = jnp.stack([lax.axis_index("x") * 2 + lax.axis_index("c"), vocab_start, y]).astype(i32)
 
-    exps, facts = call(
+    exps, lse, facts = call(
         softmax_kernel,
-        [shape(TOK, vocab_rows, dtype=bf16), shape(32, 4, TOK)],
+        [shape(TOK, vocab_rows, dtype=bf16), shape(16, 1, TOK), shape(3, TOK)],
         [VMEM] * 3,
         own + up + down,
         place,
-        rows,
-    )
-    exps, facts = lax.optimization_barrier((exps, facts))
+        row,
+    )
+    exps, lse = lax.optimization_barrier((exps, lse))
 
     every_exp = [exps, shift(exps, 3), shift(exps, 2), shift(exps, 1)]
+    facts = call(combine_kernel, shape(32, 4, TOK), [VMEM] * 2, exchange(lse, Z), facts)
     facts = exchange(facts, ("y", "x", "c"))
-    lse = exchange(call(combine_kernel, shape(16, BINS, TOK), [VMEM], facts), Z)
-    lse, facts, every_exp = lax.optimization_barrier((lse, facts, every_exp))
-
-    grads, kept, sent = call(
+    facts, every_exp = lax.optimization_barrier((facts, every_exp))
+
+    grads, sent = call(
         grad_kernel,
-        [
-            shape(BINS, TOK, vocab_rows, dtype=bf16),
-            shape(BINS, 16, 64, 128),
-            shape(BINS, 16, 64, 128, dtype=bf16),
-        ],
-        [SMEM] + [VMEM] * 6 + [FREE],
+        [shape(BINS, TOK, vocab_rows, dtype=bf16), shape(BINS, 16, 64, 128, dtype=bf16)],
+        [SMEM] + [VMEM] * 5 + [FREE],
         here,
-        lse,
         facts,
         *every_exp,
         head_t,
-        scratch=[pltpu.VMEM((BINS, TOK), f32)],
     )
     terms = swap_core(sent)
+    kept = call(kept_kernel, shape(BINS, 16, 64, 128), [FREE, VMEM], head_t, grads, flops=10**9)
     head_terms = call(
         head_kernel, shape(width, vocab_rows, dtype=bf16), [FREE, FREE, VMEM], own_cols, other_cols, grads, flops=2 * 10**9
     )
-    terms, head_terms = lax.optimization_barrier((terms, head_terms))
+    terms, kept = lax.optimization_barrier((terms, kept))
     terms = (kept + terms.astype(f32)).astype(bf16).reshape(16, 4, 64, 128)
     terms = exchange(terms, ("y", "x")).reshape(BINS, 4, 4, 64, 128)
     terms = jnp.sum(terms.astype(f32), axis=1).astype(bf16).reshape(16, 64, 128)

time: 208 us -> 204 us (0.981)
  blocking collectives: 66.8 us -> 53.6 us
  waiting for transfers between devices: 52.2 us -> 58.7 us
  matrix products: 19.9 us -> 16.6 us
  local copies, waits for them, and re-layouts: 5.72 us -> 8.03 us
    all_to_all x3 -> x2, blocking collectives: 66.8 us -> 53.6 us  [exchange(): return lax.all_to_all(a, axes, 0, 0, tiled=True)]
    all_to_all x3 -> x4, starting transfers between devices: 18.8 us -> 25.4 us  [exchange(): return lax.all_to_all(a, axes, 0, 0, tiled=True)]
    ppermute x7, starting transfers between devices: 25.1 us -> 19.4 us  [shift(): return lax.ppermute(a, 'y', [(i, (i + k) % BINS) for i in range(BINS)])]
    ppermute x7, waiting for transfers between devices: 15.4 us -> 18.9 us  [shift(): return lax.ppermute(a, 'y', [(i, (i + k) % BINS) for i in range(BINS)])]
    dot_general x10, matrix products: 19.9 us -> 16.6 us  [dot(): lax.dot_general(a, b, (((ca,), (cb,)), ((), ())), preferred_element_type=...]
    unnamed x26, local copies, waits for them, and re-layouts: 4.22 us -> 6.53 us
    all_to_all x3 -> x4, waiting for transfers between devices: 34.7 us -> 36.7 us  [exchange(): return lax.all_to_all(a, axes, 0, 0, tiled=True)]
    pallas_call x7 -> x8, Pallas kernels: 9.68 us -> 11 us  [call(): pl.pallas_call(kernel, out_shape=out, in_specs=ins, scratch_shapes=list(s...]
  transfers between devices with their start and end apart: 12 -> 13, of which waited for: 7 -> 9; matrix products, arithmetic and copies ran while one was open for 9% -> 8% of each run, Pallas kernels for 2% -> 3%
where the time goes in v6:
time: 204 us; the launch traced here: 203 us
  waiting for transfers between devices  58.7 us (29%)
  blocking collectives  53.6 us (26%)
  starting transfers between devices  48.7 us (24%)
  matrix products  16.6 us (8%)
  Pallas kernels  11 us (5%)
  local copies, waits for them, and re-layouts  8.03 us (4%)
  other arithmetic  5.22 us (3%)
    all_to_all x2, blocking collectives, exchange(): return lax.all_to_all(a, axes, 0, 0, tiled=True)  53.6 us
    all_to_all x4, waiting for transfers between devices, exchange(): return lax.all_to_all(a, axes, 0, 0, tiled=True)  36.7 us
    all_to_all x4, starting transfers between devices, exchange(): return lax.all_to_all(a, axes, 0, 0, tiled=True)  25.4 us
    ppermute x7, starting transfers between devices, shift(): return lax.ppermute(a, 'y', [(i, (i + k) % BINS) for i in range(BINS)])  19.4 us
    ppermute x7, waiting for transfers between devices, shift(): return lax.ppermute(a, 'y', [(i, (i + k) % BINS) for i in range(BINS)])  18.9 us
    dot_general x10, matrix products, dot(): lax.dot_general(a, b, (((ca,), (cb,)), ((), ())), preferred_element_type=...  16.6 us
    pallas_call x8, Pallas kernels, call(): pl.pallas_call(kernel, out_shape=out, in_specs=ins, scratch_shapes=list(s...  11 us
    unnamed x26, local copies, waits for them, and re-layouts  6.53 us
  transfers between devices with their start and end apart: 13, of which 9 were waited for; matrix products, arithmetic and copies ran while one was open for 8% of the time, Pallas kernels for 3%

profile of v6, /device:TPU:32, one launch (start us, length us, event | category | flops | bytes accessed | tf_op | source)
XLA Modules:
  0.0 202.9 jit_solution(11741480250502519309)
XLA Ops:
  1.6 32.9 %all_to_all.30 = bf16[16,64,128]{2,1,0:T(8,128)(2,1)S(1)} all-to-all(bf16[16,64,128]{2,1,0:T(8,128)(2,1)S(1)} %shard_map.68), channel_id=1, replica_groups=mesh['y'=4,'zh'=4,'zl'=4,'x'=4,'c'=2] {'zh','zl'}, dimensions={0} | all-to-all | bytes 524288 | tf_op jit(solution)/shard_map/all_to_all | solution.py:32
  35.8 7.0 %all-to-all-start.1 = ((bf16[16,4,64,128]{3,2,1,0:T(8,128)(2,1)}), bf16[16,4,64,128]{3,2,1,0:T(8,128)(2,1)S(1)}, u32[]{:S(2)}, u32[]{:S(2)}) async-start(bf16[16,4,64,128]{3,2,1,0:T(8,128)(2,1)} %bitcast.47), calls=%async_computation.1 | async-start | bytes 2097152 | tf_op jit(solution)/shard_map/all_to_all | solution.py:32
  42.9 5.0 %fusion.2.head_ref = bf16[1280,896]{1,0:T(8,128)(2,1)} fusion(bf16[896,1280]{1,0:T(8,128)(2,1)S(1)} %copy-done, s32[1280]{0:T(1024)S(1)} %fusion.39), kind=kOutput, calls=%fused_computation.3 | convolution fusion | flops 2938798080 | bytes 4592640 | tf_op jit(solution)/shard_map/dot_general | solution.py:161
  47.9 11.5 %all-to-all-done.1 = bf16[16,4,64,128]{3,2,1,0:T(8,128)(2,1)S(1)} async-done(((bf16[16,4,64,128]{3,2,1,0:T(8,128)(2,1)}), bf16[16,4,64,128]{3,2,1,0:T(8,128)(2,1)S(1)}, u32[]{:S(2)}, u32[]{:S(2)}) %all-to-all-start.1) | async-done | bytes 1048608 | tf_op jit(solution)/shard_map/all_to_all | solution.py:32
  61.9 2.1 %collective-permute-done.a_ref = bf16[4,16,64,128]{3,2,1,0:T(8,128)(2,1)} collective-permute-done((bf16[4,16,64,128]{3,2,1,0:T(8,128)(2,1)S(1)}, bf16[4,16,64,128]{3,2,1,0:T(8,128)(2,1)}, u32[]{:S(2)}, u32[]{:S(2)}) %collective-permute-start) | collective-permute-done | bytes 1048608 | tf_op jit(solution)/shard_map/ppermute | solution.py:28
  67.7 2.6 %collective-permute-start.3 = (f32[96,896]{1,0:T(8,128)S(1)}, f32[96,896]{1,0:T(8,128)S(1)}, u32[]{:S(2)}, u32[]{:S(2)}) collective-permute-start(f32[96,896]{1,0:T(8,128)S(1)} %get-tuple-element.43), channel_id=1, source_target_pairs={{0,384},{128,0},{256,128},{384,256},{1,385},{129,1},{257,129},{385... | collective-permute-start | bytes 1032200 | tf_op jit(solution)/shard_map/ppermute | solution.py:24
  70.8 3.3 %collective-permute-start.1 = (f32[96,896]{1,0:T(8,128)S(1)}, f32[96,896]{1,0:T(8,128)S(1)}, u32[]{:S(2)}, u32[]{:S(2)}) collective-permute-start(f32[96,896]{1,0:T(8,128)S(1)} %get-tuple-element.42), channel_id=1, source_target_pairs={{0,128},{128,256},{256,384},{384,0},{1,129},{129,257},{257,385},{3... | collective-permute-start | bytes 1032200 | tf_op jit(solution)/shard_map/ppermute | solution.py:24
  74.6 5.1 %collective-permute-done.3 = f32[96,896]{1,0:T(8,128)S(1)} collective-permute-done((f32[96,896]{1,0:T(8,128)S(1)}, f32[96,896]{1,0:T(8,128)S(1)}, u32[]{:S(2)}, u32[]{:S(2)}) %collective-permute-start.3) | collective-permute-done | bytes 344096 | tf_op jit(solution)/shard_map/ppermute | solution.py:24
  80.6 3.8 %collective-permute-start.4 = (f32[192,896]{1,0:T(8,128)}, f32[192,896]{1,0:T(8,128)S(1)}, u32[]{:S(2)}, u32[]{:S(2)}) collective-permute-start(f32[192,896]{1,0:T(8,128)} %pad_add_fusion), channel_id=1, source_target_pairs={{0,384},{128,0},{256,128},{384,256},{1,385},{129,1},{257,129},{385... | collective-permute-start | bytes 2064392 | tf_op jit(solution)/shard_map/ppermute | solution.py:24
  85.3 2.0 %collective-permute-start.2 = (f32[192,896]{1,0:T(8,128)}, f32[192,896]{1,0:T(8,128)}, u32[]{:S(2)}, u32[]{:S(2)}) collective-permute-start(f32[192,896]{1,0:T(8,128)} %pad_add_fusion.1), channel_id=1, source_target_pairs={{0,128},{128,256},{256,384},{384,0},{1,129},{129,257},{257,385},{3... | collective-permute-start | bytes 2064392 | tf_op jit(solution)/shard_map/ppermute | solution.py:24
  91.2 8.1 %collective-permute-done.4 = f32[192,896]{1,0:T(8,128)S(1)} collective-permute-done((f32[192,896]{1,0:T(8,128)}, f32[192,896]{1,0:T(8,128)S(1)}, u32[]{:S(2)}, u32[]{:S(2)}) %collective-permute-start.4) | collective-permute-done | bytes 688160 | tf_op jit(solution)/shard_map/ppermute | solution.py:24
  99.3 5.7 %collective-permute-done.2 = f32[192,896]{1,0:T(8,128)} collective-permute-done((f32[192,896]{1,0:T(8,128)}, f32[192,896]{1,0:T(8,128)}, u32[]{:S(2)}, u32[]{:S(2)}) %collective-permute-start.2) | collective-permute-done | bytes 688160 | tf_op jit(solution)/shard_map/ppermute | solution.py:24
  109.1 3.0 %collective-permute-start.6 = (bf16[192,896]{1,0:T(8,128)(2,1)S(1)}, bf16[192,896]{1,0:T(8,128)(2,1)S(1)}, u32[]{:S(2)}, u32[]{:S(2)}) collective-permute-start(bf16[192,896]{1,0:T(8,128)(2,1)S(1)} %get-tuple-element.34.exps0), channel_id=1, source_target_pairs={{0,256},{128,384},{256,0},{384,128},{1,257},{129,385},{257,1},{385... | collective-permute-start | bytes 1032200 | tf_op jit(solution)/shard_map/ppermute | solution.py:24
  112.2 2.8 %collective-permute-start.7 = (bf16[192,896]{1,0:T(8,128)(2,1)S(1)}, bf16[192,896]{1,0:T(8,128)(2,1)}, u32[]{:S(2)}, u32[]{:S(2)}) collective-permute-start(bf16[192,896]{1,0:T(8,128)(2,1)S(1)} %get-tuple-element.34.exps0), channel_id=1, source_target_pairs={{0,128},{128,256},{256,384},{384,0},{1,129},{129,257},{257,385},{3... | collective-permute-start | bytes 1032200 | tf_op jit(solution)/shard_map/ppermute | solution.py:24
  115.0 7.0 %all-to-all-start.2 = ((f32[16,1,192]{2,1,0:T(1,128)}), f32[16,1,192]{2,1,0:T(1,128)S(1)}, u32[]{:S(2)}, u32[]{:S(2)}) async-start(f32[16,1,192]{2,1,0:T(1,128)} %get-tuple-element.30), calls=%async_computation.2 | async-start | bytes 32768 | tf_op jit(solution)/shard_map/all_to_all | solution.py:32
  122.0 11.3 %all-to-all-done.2.lse_ref = f32[16,1,192]{2,1,0:T(1,128)S(1)} async-done(((f32[16,1,192]{2,1,0:T(1,128)}), f32[16,1,192]{2,1,0:T(1,128)S(1)}, u32[]{:S(2)}, u32[]{:S(2)}) %all-to-all-start.2) | async-done | bytes 12320 | tf_op jit(solution)/shard_map/all_to_all | solution.py:32
  134.0 6.6 %all-to-all-start.3 = ((f32[32,4,192]{2,1,0:T(4,128)}), f32[32,4,192]{2,1,0:T(4,128)S(1)}, u32[]{:S(2)}, u32[]{:S(2)}) async-start(f32[32,4,192]{2,1,0:T(4,128)} %shard_map.72), calls=%async_computation.3 | async-start | bytes 262144 | tf_op jit(solution)/shard_map/all_to_all | solution.py:32
  140.7 7.7 %all-to-all-done.3.facts_ref = f32[32,4,192]{2,1,0:T(4,128)S(1)} async-done(((f32[32,4,192]{2,1,0:T(4,128)}), f32[32,4,192]{2,1,0:T(4,128)S(1)}, u32[]{:S(2)}, u32[]{:S(2)}) %all-to-all-start.3) | async-done | bytes 98336 | tf_op jit(solution)/shard_map/all_to_all | solution.py:32
  150.1 2.9 %shard_map.73 = (bf16[4,192,896]{2,1,0:T(8,128)(2,1)S(1)}, bf16[4,16,64,128]{3,2,1,0:T(8,128)(2,1)S(1)}) custom-call(s32[3]{0:T(128)S(1)} %pad_add_fusion.2.where_ref, f32[32,4,192]{2,1,0:T(4,128)S(1)} %all-to-all-done.3.facts_ref, bf16[192,896]{1,0:T(8,128)(2,1)S(1)} %get-tuple-element.34.exps0, bf16[192,896]{1,0:T(8,128)(2,1)S(1)} %collective-permute-done.5.exps1, ...), custom_call_target="tpu_custom_call" | custom-call | tf_op jit(solution)/shard_map/pallas_call | solution.py:36
  157.9 20.6 %all_to_all.31 = bf16[16,4,64,128]{3,2,1,0:T(8,128)(2,1)S(1)} all-to-all(bf16[16,4,64,128]{3,2,1,0:T(8,128)(2,1)S(1)} %bitcast.48), channel_id=1, replica_groups=mesh['y'=4,'zh'=4,'zl'=4,'x'=4,'c'=2] {'y','x'}, dimensions={0} | all-to-all | bytes 2097152 | tf_op jit(solution)/shard_map/all_to_all | solution.py:32
  179.4 4.7 %all-to-all-start.5 = ((bf16[16,64,128]{2,1,0:T(8,128)(2,1)}), bf16[16,64,128]{2,1,0:T(8,128)(2,1)S(1)}, u32[]{:S(2)}, u32[]{:S(2)}) async-start(bf16[16,64,128]{2,1,0:T(8,128)(2,1)} %bitcast.21), calls=%async_computation.5 | async-start | bytes 524288 | tf_op jit(solution)/shard_map/all_to_all | solution.py:32
  188.1 2.9 %shard_map.75 = bf16[1280,896]{1,0:T(8,128)(2,1)S(1)} custom-call(bf16[4,640,192]{2,1,0:T(8,128)(2,1)S(1)} %copy-done.4, bf16[4,640,192]{2,1,0:T(8,128)(2,1)S(1)} %copy-done.6, bf16[4,192,896]{2,1,0:T(8,128)(2,1)S(1)} %copy-done.8), custom_call_target="tpu_custom_call" | custom-call | flops 2000000000 | tf_op jit(solution)/shard_map/pallas_call | solution.py:36
  191.0 4.9 %fusion.3 = bf16[896,1280]{1,0:T(8,128)(2,1)} fusion(bf16[1280,896]{1,0:T(8,128)(2,1)S(1)} %shard_map.75, s32[1280]{0:T(1024)S(1)} %fusion.39), kind=kOutput, calls=%fused_computation.4 | convolution fusion | flops 2938798080 | bytes 4592640 | tf_op jit(solution)/shard_map/dot_general | solution.py:161
  195.8 6.3 %all-to-all-done.5 = bf16[16,64,128]{2,1,0:T(8,128)(2,1)S(1)} async-done(((bf16[16,64,128]{2,1,0:T(8,128)(2,1)}), bf16[16,64,128]{2,1,0:T(8,128)(2,1)S(1)}, u32[]{:S(2)}, u32[]{:S(2)}) %all-to-all-start.5) | async-done | bytes 262176 | tf_op jit(solution)/shard_map/all_to_all | solution.py:32
  (67 shorter events, 32.0 us)
Async XLA Ops:
  0.6 42.2 %copy-start = (bf16[896,1280]{1,0:T(8,128)(2,1)S(1)}, bf16[896,1280]{1,0:T(8,128)(2,1)}, u32[]{:S(2)}) copy-start(bf16[896,1280]{1,0:T(8,128)(2,1)} %param.6) | copy-start | bytes 6881284
  35.8 23.5 %all-to-all-start.1 = ((bf16[16,4,64,128]{3,2,1,0:T(8,128)(2,1)}), bf16[16,4,64,128]{3,2,1,0:T(8,128)(2,1)S(1)}, u32[]{:S(2)}, u32[]{:S(2)}) async-start(bf16[16,4,64,128]{3,2,1,0:T(8,128)(2,1)} %bitcast.47), calls=%async_computation.1 | async-start | bytes 2097152 | tf_op jit(solution)/shard_map/all_to_all | solution.py:32
  42.9 18.4 %copy-start.11 = (s32[1,192]{1,0:T(1,128)S(1)}, s32[1,192]{1,0:T(1,128)}, u32[]{:S(2)}) copy-start(s32[1,192]{1,0:T(1,128)} %param.9) | copy-start | bytes 2308
  42.9 18.4 %copy-start.10 = (s32[1,192]{1,0:T(1,128)S(1)}, s32[1,192]{1,0:T(1,128)}, u32[]{:S(2)}) copy-start(s32[1,192]{1,0:T(1,128)} %param.8) | copy-start | bytes 2308
  59.3 4.7 %collective-permute-start = (bf16[4,16,64,128]{3,2,1,0:T(8,128)(2,1)S(1)}, bf16[4,16,64,128]{3,2,1,0:T(8,128)(2,1)}, u32[]{:S(2)}, u32[]{:S(2)}) collective-permute-start(bf16[4,16,64,128]{3,2,1,0:T(8,128)(2,1)S(1)} %bitcast.44), channel_id=1, source_target_pairs={{0,1},{1,0},{2,3},{3,2},{4,5},{5,4},{6,7},{7,6},{8,9},{9,8},{10,11... | collective-permute-start | bytes 3145736 | tf_op jit(solution)/shard_map/ppermute | solution.py:28
  61.9 8.4 %copy-start.3 = (bf16[4,640,192]{2,1,0:T(8,128)(2,1)}, bf16[4,640,192]{2,1,0:T(8,128)(2,1)S(1)}, u32[]{:S(2)}) copy-start(bf16[4,640,192]{2,1,0:T(8,128)(2,1)S(1)} %shard_map.69.own_ref) | copy-start | bytes 2949124
  61.9 3.7 %copy-start.1 = (bf16[1280,896]{1,0:T(8,128)(2,1)S(1)}, bf16[1280,896]{1,0:T(8,128)(2,1)}, u32[]{:S(2)}) copy-start(bf16[1280,896]{1,0:T(8,128)(2,1)} %fusion.2.head_ref) | copy-start | bytes 6881284
  65.6 8.4 %copy-start.5 = (bf16[4,640,192]{2,1,0:T(8,128)(2,1)}, bf16[4,640,192]{2,1,0:T(8,128)(2,1)S(1)}, u32[]{:S(2)}) copy-start(bf16[4,640,192]{2,1,0:T(8,128)(2,1)S(1)} %shard_map.70.other_ref) | copy-start | bytes 2949124
  67.7 12.0 %collective-permute-start.3 = (f32[96,896]{1,0:T(8,128)S(1)}, f32[96,896]{1,0:T(8,128)S(1)}, u32[]{:S(2)}, u32[]{:S(2)}) collective-permute-start(f32[96,896]{1,0:T(8,128)S(1)} %get-tuple-element.43), channel_id=1, source_target_pairs={{0,384},{128,0},{256,128},{384,256},{1,385},{129,1},{257,129},{385... | collective-permute-start | bytes 1032200 | tf_op jit(solution)/shard_map/ppermute | solution.py:24
  70.8 13.6 %collective-permute-start.1 = (f32[96,896]{1,0:T(8,128)S(1)}, f32[96,896]{1,0:T(8,128)S(1)}, u32[]{:S(2)}, u32[]{:S(2)}) collective-permute-start(f32[96,896]{1,0:T(8,128)S(1)} %get-tuple-element.42), channel_id=1, source_target_pairs={{0,128},{128,256},{256,384},{384,0},{1,129},{129,257},{257,385},{3... | collective-permute-start | bytes 1032200 | tf_op jit(solution)/shard_map/ppermute | solution.py:24
  74.6 12.8 %copy-start.12 = (s32[1,192]{1,0:T(1,128)S(1)}, s32[1,192]{1,0:T(1,128)}, u32[]{:S(2)}) copy-start(s32[1,192]{1,0:T(1,128)} %param.7) | copy-start | bytes 2308
  80.6 18.7 %collective-permute-start.4 = (f32[192,896]{1,0:T(8,128)}, f32[192,896]{1,0:T(8,128)S(1)}, u32[]{:S(2)}, u32[]{:S(2)}) collective-permute-start(f32[192,896]{1,0:T(8,128)} %pad_add_fusion), channel_id=1, source_target_pairs={{0,384},{128,0},{256,128},{384,256},{1,385},{129,1},{257,129},{385... | collective-permute-start | bytes 2064392 | tf_op jit(solution)/shard_map/ppermute | solution.py:24
  85.3 19.8 %collective-permute-start.2 = (f32[192,896]{1,0:T(8,128)}, f32[192,896]{1,0:T(8,128)}, u32[]{:S(2)}, u32[]{:S(2)}) collective-permute-start(f32[192,896]{1,0:T(8,128)} %pad_add_fusion.1), channel_id=1, source_target_pairs={{0,128},{128,256},{256,384},{384,0},{1,129},{129,257},{257,385},{3... | collective-permute-start | bytes 2064392 | tf_op jit(solution)/shard_map/ppermute | solution.py:24
  107.2 41.2 %collective-permute-start.5 = (bf16[192,896]{1,0:T(8,128)(2,1)S(1)}, bf16[192,896]{1,0:T(8,128)(2,1)S(1)}, u32[]{:S(2)}, u32[]{:S(2)}) collective-permute-start(bf16[192,896]{1,0:T(8,128)(2,1)S(1)} %get-tuple-element.34.exps0), channel_id=1, source_target_pairs={{0,384},{128,0},{256,128},{384,256},{1,385},{129,1},{257,129},{385... | collective-permute-start | bytes 1032200 | tf_op jit(solution)/shard_map/ppermute | solution.py:24
  109.1 39.3 %collective-permute-start.6 = (bf16[192,896]{1,0:T(8,128)(2,1)S(1)}, bf16[192,896]{1,0:T(8,128)(2,1)S(1)}, u32[]{:S(2)}, u32[]{:S(2)}) collective-permute-start(bf16[192,896]{1,0:T(8,128)(2,1)S(1)} %get-tuple-element.34.exps0), channel_id=1, source_target_pairs={{0,256},{128,384},{256,0},{384,128},{1,257},{129,385},{257,1},{385... | collective-permute-start | bytes 1032200 | tf_op jit(solution)/shard_map/ppermute | solution.py:24
  112.2 36.3 %collective-permute-start.7 = (bf16[192,896]{1,0:T(8,128)(2,1)S(1)}, bf16[192,896]{1,0:T(8,128)(2,1)}, u32[]{:S(2)}, u32[]{:S(2)}) collective-permute-start(bf16[192,896]{1,0:T(8,128)(2,1)S(1)} %get-tuple-element.34.exps0), channel_id=1, source_target_pairs={{0,128},{128,256},{256,384},{384,0},{1,129},{129,257},{257,385},{3... | collective-permute-start | bytes 1032200 | tf_op jit(solution)/shard_map/ppermute | solution.py:24
  115.0 18.3 %all-to-all-start.2 = ((f32[16,1,192]{2,1,0:T(1,128)}), f32[16,1,192]{2,1,0:T(1,128)S(1)}, u32[]{:S(2)}, u32[]{:S(2)}) async-start(f32[16,1,192]{2,1,0:T(1,128)} %get-tuple-element.30), calls=%async_computation.2 | async-start | bytes 32768 | tf_op jit(solution)/shard_map/all_to_all | solution.py:32
  134.0 14.4 %all-to-all-start.3 = ((f32[32,4,192]{2,1,0:T(4,128)}), f32[32,4,192]{2,1,0:T(4,128)S(1)}, u32[]{:S(2)}, u32[]{:S(2)}) async-start(f32[32,4,192]{2,1,0:T(4,128)} %shard_map.72), calls=%async_computation.3 | async-start | bytes 262144 | tf_op jit(solution)/shard_map/all_to_all | solution.py:32
  148.4 1.6 copy-start.2
  153.0 3.6 %copy-start.7 = (bf16[4,192,896]{2,1,0:T(8,128)(2,1)}, bf16[4,192,896]{2,1,0:T(8,128)(2,1)S(1)}, u32[]{:S(2)}) copy-start(bf16[4,192,896]{2,1,0:T(8,128)(2,1)S(1)} %get-tuple-element.39.grads_ref) | copy-start | bytes 4128772
  153.0 4.6 %collective-permute-start.8 = (bf16[4,16,64,128]{3,2,1,0:T(8,128)(2,1)S(1)}, bf16[4,16,64,128]{3,2,1,0:T(8,128)(2,1)S(1)}, u32[]{:S(2)}, u32[]{:S(2)}) collective-permute-start(bf16[4,16,64,128]{3,2,1,0:T(8,128)(2,1)S(1)} %get-tuple-element.38), channel_id=1, source_target_pairs={{0,1},{1,0},{2,3},{3,2},{4,5},{5,4},{6,7},{7,6},{8,9},{9,8},{10,11... | collective-permute-start | bytes 3145736 | tf_op jit(solution)/shard_map/ppermute | solution.py:28
  179.4 22.7 %all-to-all-start.5 = ((bf16[16,64,128]{2,1,0:T(8,128)(2,1)}), bf16[16,64,128]{2,1,0:T(8,128)(2,1)S(1)}, u32[]{:S(2)}, u32[]{:S(2)}) async-start(bf16[16,64,128]{2,1,0:T(8,128)(2,1)} %bitcast.21), calls=%async_computation.5 | async-start | bytes 524288 | tf_op jit(solution)/shard_map/all_to_all | solution.py:32
  184.1 1.3 copy-start.4
  186.7 1.3 copy-start.8
  (2 other events, 2.2 us)

commit v7 on v6

--- a/solution.py
+++ b/solution.py
@@ -190,6 +190,7 @@
         return dot(pick(own_cols, at[r]), head_t[:hw], 0, 0) + dot(pick(other_cols, at[r]), head_t[hw:], 0, 0)
 
     far = partial_logits(2)
+    far, own_cols, other_cols = lax.optimization_barrier((far, own_cols, other_cols))
     from_left = shift(far[:half], 1)
     from_right = shift(far[half:], 3)
     up = partial_logits(1)
@@ -221,7 +222,7 @@
     exps, lse = lax.optimization_barrier((exps, lse))
 
     every_exp = [exps, shift(exps, 3), shift(exps, 2), shift(exps, 1)]
-    facts = call(combine_kernel, shape(32, 4, TOK), [VMEM] * 2, exchange(lse, Z), facts)
+    facts = call(combine_kernel, shape(32, 4, TOK), [VMEM] * 2, exchange(lse, Z), facts, flops=3 * 10**10)
     facts = exchange(facts, ("y", "x", "c"))
     facts, every_exp = lax.optimization_barrier((facts, every_exp))
 

time: 204 us -> 199 us (0.975)
  waiting for transfers between devices: 58.7 us -> 49.4 us
  starting transfers between devices: 48.7 us -> 52.5 us
    all_to_all x4, waiting for transfers between devices: 36.7 us -> 28.5 us  [exchange(): return lax.all_to_all(a, axes, 0, 0, tiled=True)]
    all_to_all x4, starting transfers between devices: 25.4 us -> 29.2 us  [exchange(): return lax.all_to_all(a, axes, 0, 0, tiled=True)]
    unnamed x26 -> x28, local copies, waits for them, and re-layouts: 6.53 us -> 7.18 us
  transfers between devices with their start and end apart: 13 -> 13, of which waited for: 9 -> 9; matrix products, arithmetic and copies ran while one was open for 8% -> 9% of each run, Pallas kernels for 3% -> 2%
where the time goes in v7:
time: 199 us; the launch traced here: 197 us
  blocking collectives  53.6 us (27%)
  starting transfers between devices  52.5 us (26%)
  waiting for transfers between devices  49.4 us (25%)
  matrix products  16.5 us (8%)
  Pallas kernels  10.4 us (5%)
  local copies, waits for them, and re-layouts  8.69 us (4%)
  other arithmetic  5.21 us (3%)
    all_to_all x2, blocking collectives, exchange(): return lax.all_to_all(a, axes, 0, 0, tiled=True)  53.6 us
    all_to_all x4, starting transfers between devices, exchange(): return lax.all_to_all(a, axes, 0, 0, tiled=True)  29.2 us
    all_to_all x4, waiting for transfers between devices, exchange(): return lax.all_to_all(a, axes, 0, 0, tiled=True)  28.5 us
    ppermute x7, starting transfers between devices, shift(): return lax.ppermute(a, 'y', [(i, (i + k) % BINS) for i in range(BINS)])  19.4 us
    ppermute x7, waiting for transfers between devices, shift(): return lax.ppermute(a, 'y', [(i, (i + k) % BINS) for i in range(BINS)])  17.9 us
    dot_general x10, matrix products, dot(): lax.dot_general(a, b, (((ca,), (cb,)), ((), ())), preferred_element_type=...  16.5 us
    pallas_call x8, Pallas kernels, call(): pl.pallas_call(kernel, out_shape=out, in_specs=ins, scratch_shapes=list(s...  10.4 us
    unnamed x28, local copies, waits for them, and re-layouts  7.18 us
  transfers between devices with their start and end apart: 13, of which 9 were waited for; matrix products, arithmetic and copies ran while one was open for 9% of the time, Pallas kernels for 2%

profile of v7, /device:TPU:32, one launch (start us, length us, event | category | flops | bytes accessed | tf_op | source)
XLA Modules:
  0.0 197.5 jit_solution(16816685254729666323)
XLA Ops:
  1.6 32.9 %all_to_all.30 = bf16[16,64,128]{2,1,0:T(8,128)(2,1)S(1)} all-to-all(bf16[16,64,128]{2,1,0:T(8,128)(2,1)S(1)} %shard_map.68), channel_id=1, replica_groups=mesh['y'=4,'zh'=4,'zl'=4,'x'=4,'c'=2] {'zh','zl'}, dimensions={0} | all-to-all | bytes 524288 | tf_op jit(solution)/shard_map/all_to_all | solution.py:32
  35.8 7.0 %all-to-all-start.1 = ((bf16[16,4,64,128]{3,2,1,0:T(8,128)(2,1)}), bf16[16,4,64,128]{3,2,1,0:T(8,128)(2,1)S(1)}, u32[]{:S(2)}, u32[]{:S(2)}) async-start(bf16[16,4,64,128]{3,2,1,0:T(8,128)(2,1)} %bitcast.47), calls=%async_computation.1 | async-start | bytes 2097152 | tf_op jit(solution)/shard_map/all_to_all | solution.py:32
  42.9 5.0 %fusion.2.head_ref = bf16[1280,896]{1,0:T(8,128)(2,1)} fusion(bf16[896,1280]{1,0:T(8,128)(2,1)S(1)} %copy-done, s32[1280]{0:T(1024)S(1)} %fusion.39), kind=kOutput, calls=%fused_computation.3 | convolution fusion | flops 2938798080 | bytes 4592640 | tf_op jit(solution)/shard_map/dot_general | solution.py:161
  47.9 11.5 %all-to-all-done.1 = bf16[16,4,64,128]{3,2,1,0:T(8,128)(2,1)S(1)} async-done(((bf16[16,4,64,128]{3,2,1,0:T(8,128)(2,1)}), bf16[16,4,64,128]{3,2,1,0:T(8,128)(2,1)S(1)}, u32[]{:S(2)}, u32[]{:S(2)}) %all-to-all-start.1) | async-done | bytes 1048608 | tf_op jit(solution)/shard_map/all_to_all | solution.py:32
  61.9 2.1 %collective-permute-done.a_ref = bf16[4,16,64,128]{3,2,1,0:T(8,128)(2,1)} collective-permute-done((bf16[4,16,64,128]{3,2,1,0:T(8,128)(2,1)S(1)}, bf16[4,16,64,128]{3,2,1,0:T(8,128)(2,1)}, u32[]{:S(2)}, u32[]{:S(2)}) %collective-permute-start) | collective-permute-done | bytes 1048608 | tf_op jit(solution)/shard_map/ppermute | solution.py:28
  66.7 2.6 %collective-permute-start.3 = (f32[96,896]{1,0:T(8,128)S(1)}, f32[96,896]{1,0:T(8,128)S(1)}, u32[]{:S(2)}, u32[]{:S(2)}) collective-permute-start(f32[96,896]{1,0:T(8,128)S(1)} %get-tuple-element.49), channel_id=1, source_target_pairs={{0,384},{128,0},{256,128},{384,256},{1,385},{129,1},{257,129},{385... | collective-permute-start | bytes 1032200 | tf_op jit(solution)/shard_map/ppermute | solution.py:24
  69.3 3.3 %collective-permute-start.1 = (f32[96,896]{1,0:T(8,128)S(1)}, f32[96,896]{1,0:T(8,128)S(1)}, u32[]{:S(2)}, u32[]{:S(2)}) collective-permute-start(f32[96,896]{1,0:T(8,128)S(1)} %get-tuple-element.48), channel_id=1, source_target_pairs={{0,128},{128,256},{256,384},{384,0},{1,129},{129,257},{257,385},{3... | collective-permute-start | bytes 1032200 | tf_op jit(solution)/shard_map/ppermute | solution.py:24
  74.6 4.1 %collective-permute-done.3 = f32[96,896]{1,0:T(8,128)S(1)} collective-permute-done((f32[96,896]{1,0:T(8,128)S(1)}, f32[96,896]{1,0:T(8,128)S(1)}, u32[]{:S(2)}, u32[]{:S(2)}) %collective-permute-start.3) | collective-permute-done | bytes 344096 | tf_op jit(solution)/shard_map/ppermute | solution.py:24
  79.6 3.8 %collective-permute-start.4 = (f32[192,896]{1,0:T(8,128)}, f32[192,896]{1,0:T(8,128)S(1)}, u32[]{:S(2)}, u32[]{:S(2)}) collective-permute-start(f32[192,896]{1,0:T(8,128)} %pad_add_fusion), channel_id=1, source_target_pairs={{0,384},{128,0},{256,128},{384,256},{1,385},{129,1},{257,129},{385... | collective-permute-start | bytes 2064392 | tf_op jit(solution)/shard_map/ppermute | solution.py:24
  84.3 2.0 %collective-permute-start.2 = (f32[192,896]{1,0:T(8,128)}, f32[192,896]{1,0:T(8,128)}, u32[]{:S(2)}, u32[]{:S(2)}) collective-permute-start(f32[192,896]{1,0:T(8,128)} %pad_add_fusion.1), channel_id=1, source_target_pairs={{0,128},{128,256},{256,384},{384,0},{1,129},{129,257},{257,385},{3... | collective-permute-start | bytes 2064392 | tf_op jit(solution)/shard_map/ppermute | solution.py:24
  90.2 8.1 %collective-permute-done.4 = f32[192,896]{1,0:T(8,128)S(1)} collective-permute-done((f32[192,896]{1,0:T(8,128)}, f32[192,896]{1,0:T(8,128)S(1)}, u32[]{:S(2)}, u32[]{:S(2)}) %collective-permute-start.4) | collective-permute-done | bytes 688160 | tf_op jit(solution)/shard_map/ppermute | solution.py:24
  98.3 5.7 %collective-permute-done.2 = f32[192,896]{1,0:T(8,128)} collective-permute-done((f32[192,896]{1,0:T(8,128)}, f32[192,896]{1,0:T(8,128)}, u32[]{:S(2)}, u32[]{:S(2)}) %collective-permute-start.2) | collective-permute-done | bytes 688160 | tf_op jit(solution)/shard_map/ppermute | solution.py:24
  106.2 7.0 %all-to-all-start.2 = ((f32[16,1,192]{2,1,0:T(1,128)}), f32[16,1,192]{2,1,0:T(1,128)S(1)}, u32[]{:S(2)}, u32[]{:S(2)}) async-start(f32[16,1,192]{2,1,0:T(1,128)} %get-tuple-element.36), calls=%async_computation.2 | async-start | bytes 32768 | tf_op jit(solution)/shard_map/all_to_all | solution.py:32
  115.2 3.2 %collective-permute-start.6 = (bf16[192,896]{1,0:T(8,128)(2,1)S(1)}, bf16[192,896]{1,0:T(8,128)(2,1)S(1)}, u32[]{:S(2)}, u32[]{:S(2)}) collective-permute-start(bf16[192,896]{1,0:T(8,128)(2,1)S(1)} %get-tuple-element.40.exps0), channel_id=1, source_target_pairs={{0,256},{128,384},{256,0},{384,128},{1,257},{129,385},{257,1},{385... | collective-permute-start | bytes 1032200 | tf_op jit(solution)/shard_map/ppermute | solution.py:24
  118.4 2.6 %collective-permute-start.7 = (bf16[192,896]{1,0:T(8,128)(2,1)S(1)}, bf16[192,896]{1,0:T(8,128)(2,1)}, u32[]{:S(2)}, u32[]{:S(2)}) collective-permute-start(bf16[192,896]{1,0:T(8,128)(2,1)S(1)} %get-tuple-element.40.exps0), channel_id=1, source_target_pairs={{0,128},{128,256},{256,384},{384,0},{1,129},{129,257},{257,385},{3... | collective-permute-start | bytes 1032200 | tf_op jit(solution)/shard_map/ppermute | solution.py:24
  121.0 3.5 %all-to-all-done.2.lse_ref = f32[16,1,192]{2,1,0:T(1,128)S(1)} async-done(((f32[16,1,192]{2,1,0:T(1,128)}), f32[16,1,192]{2,1,0:T(1,128)S(1)}, u32[]{:S(2)}, u32[]{:S(2)}) %all-to-all-start.2) | async-done | bytes 12320 | tf_op jit(solution)/shard_map/all_to_all | solution.py:32
  125.2 3.9 %all-to-all-start.3 = ((f32[32,4,192]{2,1,0:T(4,128)}), f32[32,4,192]{2,1,0:T(4,128)S(1)}, u32[]{:S(2)}, u32[]{:S(2)}) async-start(f32[32,4,192]{2,1,0:T(4,128)} %copy-done.9), calls=%async_computation.3 | async-start | bytes 262144 | tf_op jit(solution)/shard_map/all_to_all | solution.py:32
  129.2 7.7 %all-to-all-done.3.facts_ref = f32[32,4,192]{2,1,0:T(4,128)S(1)} async-done(((f32[32,4,192]{2,1,0:T(4,128)}), f32[32,4,192]{2,1,0:T(4,128)S(1)}, u32[]{:S(2)}, u32[]{:S(2)}) %all-to-all-start.3) | async-done | bytes 98336 | tf_op jit(solution)/shard_map/all_to_all | solution.py:32
  138.5 2.9 %shard_map.73 = (bf16[4,192,896]{2,1,0:T(8,128)(2,1)S(1)}, bf16[4,16,64,128]{3,2,1,0:T(8,128)(2,1)S(1)}) custom-call(s32[3]{0:T(128)S(1)} %pad_add_fusion.2.where_ref, f32[32,4,192]{2,1,0:T(4,128)S(1)} %all-to-all-done.3.facts_ref, bf16[192,896]{1,0:T(8,128)(2,1)S(1)} %get-tuple-element.40.exps0, bf16[192,896]{1,0:T(8,128)(2,1)S(1)} %collective-permute-done.5.exps1, ...), custom_call_target="tpu_custom_call" | custom-call | tf_op jit(solution)/shard_map/pallas_call | solution.py:36
  146.3 20.6 %all_to_all.31 = bf16[16,4,64,128]{3,2,1,0:T(8,128)(2,1)S(1)} all-to-all(bf16[16,4,64,128]{3,2,1,0:T(8,128)(2,1)S(1)} %bitcast.48), channel_id=1, replica_groups=mesh['y'=4,'zh'=4,'zl'=4,'x'=4,'c'=2] {'y','x'}, dimensions={0} | all-to-all | bytes 2097152 | tf_op jit(solution)/shard_map/all_to_all | solution.py:32
  167.9 11.3 %all-to-all-start.5 = ((bf16[16,64,128]{2,1,0:T(8,128)(2,1)}), bf16[16,64,128]{2,1,0:T(8,128)(2,1)S(1)}, u32[]{:S(2)}, u32[]{:S(2)}) async-start(bf16[16,64,128]{2,1,0:T(8,128)(2,1)} %bitcast.21), calls=%async_computation.5 | async-start | bytes 524288 | tf_op jit(solution)/shard_map/all_to_all | solution.py:32
  183.1 2.9 %shard_map.75 = bf16[1280,896]{1,0:T(8,128)(2,1)S(1)} custom-call(bf16[4,640,192]{2,1,0:T(8,128)(2,1)S(1)} %copy-done.4, bf16[4,640,192]{2,1,0:T(8,128)(2,1)S(1)} %copy-done.6, bf16[4,192,896]{2,1,0:T(8,128)(2,1)S(1)} %copy-done.8), custom_call_target="tpu_custom_call" | custom-call | flops 2000000000 | tf_op jit(solution)/shard_map/pallas_call | solution.py:36
  186.0 4.9 %fusion.3 = bf16[896,1280]{1,0:T(8,128)(2,1)} fusion(bf16[1280,896]{1,0:T(8,128)(2,1)S(1)} %shard_map.75, s32[1280]{0:T(1024)S(1)} %fusion.39), kind=kOutput, calls=%fused_computation.4 | convolution fusion | flops 2938798080 | bytes 4592640 | tf_op jit(solution)/shard_map/dot_general | solution.py:161
  190.9 5.8 %all-to-all-done.5 = bf16[16,64,128]{2,1,0:T(8,128)(2,1)S(1)} async-done(((bf16[16,64,128]{2,1,0:T(8,128)(2,1)}), bf16[16,64,128]{2,1,0:T(8,128)(2,1)S(1)}, u32[]{:S(2)}, u32[]{:S(2)}) %all-to-all-start.5) | async-done | bytes 262176 | tf_op jit(solution)/shard_map/all_to_all | solution.py:32
  (69 shorter events, 32.0 us)
Async XLA Ops:
  0.6 42.2 %copy-start = (bf16[896,1280]{1,0:T(8,128)(2,1)S(1)}, bf16[896,1280]{1,0:T(8,128)(2,1)}, u32[]{:S(2)}) copy-start(bf16[896,1280]{1,0:T(8,128)(2,1)} %param.6) | copy-start | bytes 6881284
  35.8 23.5 %all-to-all-start.1 = ((bf16[16,4,64,128]{3,2,1,0:T(8,128)(2,1)}), bf16[16,4,64,128]{3,2,1,0:T(8,128)(2,1)S(1)}, u32[]{:S(2)}, u32[]{:S(2)}) async-start(bf16[16,4,64,128]{3,2,1,0:T(8,128)(2,1)} %bitcast.47), calls=%async_computation.1 | async-start | bytes 2097152 | tf_op jit(solution)/shard_map/all_to_all | solution.py:32
  42.9 18.4 %copy-start.12 = (s32[1,192]{1,0:T(1,128)S(1)}, s32[1,192]{1,0:T(1,128)}, u32[]{:S(2)}) copy-start(s32[1,192]{1,0:T(1,128)} %param.9) | copy-start | bytes 2308
  42.9 18.4 %copy-start.11 = (s32[1,192]{1,0:T(1,128)S(1)}, s32[1,192]{1,0:T(1,128)}, u32[]{:S(2)}) copy-start(s32[1,192]{1,0:T(1,128)} %param.8) | copy-start | bytes 2308
  59.3 4.7 %collective-permute-start = (bf16[4,16,64,128]{3,2,1,0:T(8,128)(2,1)S(1)}, bf16[4,16,64,128]{3,2,1,0:T(8,128)(2,1)}, u32[]{:S(2)}, u32[]{:S(2)}) collective-permute-start(bf16[4,16,64,128]{3,2,1,0:T(8,128)(2,1)S(1)} %bitcast.44), channel_id=1, source_target_pairs={{0,1},{1,0},{2,3},{3,2},{4,5},{5,4},{6,7},{7,6},{8,9},{9,8},{10,11... | collective-permute-start | bytes 3145736 | tf_op jit(solution)/shard_map/ppermute | solution.py:28
  61.9 11.6 %copy-start.3 = (bf16[4,640,192]{2,1,0:T(8,128)(2,1)}, bf16[4,640,192]{2,1,0:T(8,128)(2,1)S(1)}, u32[]{:S(2)}) copy-start(bf16[4,640,192]{2,1,0:T(8,128)(2,1)S(1)} %shard_map.69.own_ref) | copy-start | bytes 2949124
  61.9 3.7 %copy-start.1 = (bf16[1280,896]{1,0:T(8,128)(2,1)S(1)}, bf16[1280,896]{1,0:T(8,128)(2,1)}, u32[]{:S(2)}) copy-start(bf16[1280,896]{1,0:T(8,128)(2,1)} %fusion.2.head_ref) | copy-start | bytes 6881284
  65.6 8.4 %copy-start.5 = (bf16[4,640,192]{2,1,0:T(8,128)(2,1)}, bf16[4,640,192]{2,1,0:T(8,128)(2,1)S(1)}, u32[]{:S(2)}) copy-start(bf16[4,640,192]{2,1,0:T(8,128)(2,1)S(1)} %shard_map.70.other_ref) | copy-start | bytes 2949124
  66.7 12.0 %collective-permute-start.3 = (f32[96,896]{1,0:T(8,128)S(1)}, f32[96,896]{1,0:T(8,128)S(1)}, u32[]{:S(2)}, u32[]{:S(2)}) collective-permute-start(f32[96,896]{1,0:T(8,128)S(1)} %get-tuple-element.49), channel_id=1, source_target_pairs={{0,384},{128,0},{256,128},{384,256},{1,385},{129,1},{257,129},{385... | collective-permute-start | bytes 1032200 | tf_op jit(solution)/shard_map/ppermute | solution.py:24
  69.3 14.1 %collective-permute-start.1 = (f32[96,896]{1,0:T(8,128)S(1)}, f32[96,896]{1,0:T(8,128)S(1)}, u32[]{:S(2)}, u32[]{:S(2)}) collective-permute-start(f32[96,896]{1,0:T(8,128)S(1)} %get-tuple-element.48), channel_id=1, source_target_pairs={{0,128},{128,256},{256,384},{384,0},{1,129},{129,257},{257,385},{3... | collective-permute-start | bytes 1032200 | tf_op jit(solution)/shard_map/ppermute | solution.py:24
  74.6 11.8 %copy-start.13 = (s32[1,192]{1,0:T(1,128)S(1)}, s32[1,192]{1,0:T(1,128)}, u32[]{:S(2)}) copy-start(s32[1,192]{1,0:T(1,128)} %param.7) | copy-start | bytes 2308
  79.6 18.7 %collective-permute-start.4 = (f32[192,896]{1,0:T(8,128)}, f32[192,896]{1,0:T(8,128)S(1)}, u32[]{:S(2)}, u32[]{:S(2)}) collective-permute-start(f32[192,896]{1,0:T(8,128)} %pad_add_fusion), channel_id=1, source_target_pairs={{0,384},{128,0},{256,128},{384,256},{1,385},{129,1},{257,129},{385... | collective-permute-start | bytes 2064392 | tf_op jit(solution)/shard_map/ppermute | solution.py:24
  84.3 19.8 %collective-permute-start.2 = (f32[192,896]{1,0:T(8,128)}, f32[192,896]{1,0:T(8,128)}, u32[]{:S(2)}, u32[]{:S(2)}) collective-permute-start(f32[192,896]{1,0:T(8,128)} %pad_add_fusion.1), channel_id=1, source_target_pairs={{0,128},{128,256},{256,384},{384,0},{1,129},{129,257},{257,385},{3... | collective-permute-start | bytes 2064392 | tf_op jit(solution)/shard_map/ppermute | solution.py:24
  106.2 18.3 %all-to-all-start.2 = ((f32[16,1,192]{2,1,0:T(1,128)}), f32[16,1,192]{2,1,0:T(1,128)S(1)}, u32[]{:S(2)}, u32[]{:S(2)}) async-start(f32[16,1,192]{2,1,0:T(1,128)} %get-tuple-element.36), calls=%async_computation.2 | async-start | bytes 32768 | tf_op jit(solution)/shard_map/all_to_all | solution.py:32
  113.2 23.6 %collective-permute-start.5 = (bf16[192,896]{1,0:T(8,128)(2,1)S(1)}, bf16[192,896]{1,0:T(8,128)(2,1)S(1)}, u32[]{:S(2)}, u32[]{:S(2)}) collective-permute-start(bf16[192,896]{1,0:T(8,128)(2,1)S(1)} %get-tuple-element.40.exps0), channel_id=1, source_target_pairs={{0,384},{128,0},{256,128},{384,256},{1,385},{129,1},{257,129},{385... | collective-permute-start | bytes 1032200 | tf_op jit(solution)/shard_map/ppermute | solution.py:24
  115.2 21.7 %collective-permute-start.6 = (bf16[192,896]{1,0:T(8,128)(2,1)S(1)}, bf16[192,896]{1,0:T(8,128)(2,1)S(1)}, u32[]{:S(2)}, u32[]{:S(2)}) collective-permute-start(bf16[192,896]{1,0:T(8,128)(2,1)S(1)} %get-tuple-element.40.exps0), channel_id=1, source_target_pairs={{0,256},{128,384},{256,0},{384,128},{1,257},{129,385},{257,1},{385... | collective-permute-start | bytes 1032200 | tf_op jit(solution)/shard_map/ppermute | solution.py:24
  118.4 18.5 %collective-permute-start.7 = (bf16[192,896]{1,0:T(8,128)(2,1)S(1)}, bf16[192,896]{1,0:T(8,128)(2,1)}, u32[]{:S(2)}, u32[]{:S(2)}) collective-permute-start(bf16[192,896]{1,0:T(8,128)(2,1)S(1)} %get-tuple-element.40.exps0), channel_id=1, source_target_pairs={{0,128},{128,256},{256,384},{384,0},{1,129},{129,257},{257,385},{3... | collective-permute-start | bytes 1032200 | tf_op jit(solution)/shard_map/ppermute | solution.py:24
  125.2 11.7 %all-to-all-start.3 = ((f32[32,4,192]{2,1,0:T(4,128)}), f32[32,4,192]{2,1,0:T(4,128)S(1)}, u32[]{:S(2)}, u32[]{:S(2)}) async-start(f32[32,4,192]{2,1,0:T(4,128)} %copy-done.9), calls=%async_computation.3 | async-start | bytes 262144 | tf_op jit(solution)/shard_map/all_to_all | solution.py:32
  136.9 1.6 copy-start.2
  141.4 3.6 %copy-start.7 = (bf16[4,192,896]{2,1,0:T(8,128)(2,1)}, bf16[4,192,896]{2,1,0:T(8,128)(2,1)S(1)}, u32[]{:S(2)}) copy-start(bf16[4,192,896]{2,1,0:T(8,128)(2,1)S(1)} %get-tuple-element.45.grads_ref) | copy-start | bytes 4128772
  141.4 4.6 %collective-permute-start.8 = (bf16[4,16,64,128]{3,2,1,0:T(8,128)(2,1)S(1)}, bf16[4,16,64,128]{3,2,1,0:T(8,128)(2,1)S(1)}, u32[]{:S(2)}, u32[]{:S(2)}) collective-permute-start(bf16[4,16,64,128]{3,2,1,0:T(8,128)(2,1)S(1)} %get-tuple-element.44), channel_id=1, source_target_pairs={{0,1},{1,0},{2,3},{3,2},{4,5},{5,4},{6,7},{7,6},{8,9},{9,8},{10,11... | collective-permute-start | bytes 3145736 | tf_op jit(solution)/shard_map/ppermute | solution.py:28
  167.9 28.9 %all-to-all-start.5 = ((bf16[16,64,128]{2,1,0:T(8,128)(2,1)}), bf16[16,64,128]{2,1,0:T(8,128)(2,1)S(1)}, u32[]{:S(2)}, u32[]{:S(2)}) async-start(bf16[16,64,128]{2,1,0:T(8,128)(2,1)} %bitcast.21), calls=%async_computation.5 | async-start | bytes 524288 | tf_op jit(solution)/shard_map/all_to_all | solution.py:32
  179.2 1.3 copy-start.4
  181.8 1.3 copy-start.8
  (3 other events, 2.9 us)

commit v8 on v7

--- a/solution.py
+++ b/solution.py
@@ -238,7 +238,7 @@
     terms = swap_core(sent)
     kept = call(kept_kernel, shape(BINS, 16, 64, 128), [FREE, VMEM], head_t, grads, flops=10**9)
     head_terms = call(
-        head_kernel, shape(width, vocab_rows, dtype=bf16), [FREE, FREE, VMEM], own_cols, other_cols, grads, flops=2 * 10**9
+        head_kernel, shape(width, vocab_rows, dtype=bf16), [FREE, FREE, FREE], own_cols, other_cols, grads, flops=2 * 10**9
     )
     terms, kept = lax.optimization_barrier((terms, kept))
     terms = (kept + terms.astype(f32)).astype(bf16).reshape(16, 4, 64, 128)

time: 199 us -> 199 us (level)
  no operation moved by 1% of the time
where the time goes in v8:
time: 199 us; the launch traced here: 197 us
  blocking collectives  53.6 us (27%)
  starting transfers between devices  52.5 us (26%)
  waiting for transfers between devices  49.4 us (25%)
  matrix products  16.5 us (8%)
  Pallas kernels  10.4 us (5%)
  local copies, waits for them, and re-layouts  8.69 us (4%)
  other arithmetic  5.21 us (3%)
    all_to_all x2, blocking collectives, exchange(): return lax.all_to_all(a, axes, 0, 0, tiled=True)  53.6 us
    all_to_all x4, starting transfers between devices, exchange(): return lax.all_to_all(a, axes, 0, 0, tiled=True)  29.2 us
    all_to_all x4, waiting for transfers between devices, exchange(): return lax.all_to_all(a, axes, 0, 0, tiled=True)  28.5 us
    ppermute x7, starting transfers between devices, shift(): return lax.ppermute(a, 'y', [(i, (i + k) % BINS) for i in range(BINS)])  19.4 us
    ppermute x7, waiting for transfers between devices, shift(): return lax.ppermute(a, 'y', [(i, (i + k) % BINS) for i in range(BINS)])  17.9 us
    dot_general x10, matrix products, dot(): lax.dot_general(a, b, (((ca,), (cb,)), ((), ())), preferred_element_type=...  16.5 us
    pallas_call x8, Pallas kernels, call(): pl.pallas_call(kernel, out_shape=out, in_specs=ins, scratch_shapes=list(s...  10.4 us
    unnamed x28, local copies, waits for them, and re-layouts  7.18 us
  transfers between devices with their start and end apart: 13, of which 9 were waited for; matrix products, arithmetic and copies ran while one was open for 9% of the time, Pallas kernels for 2%

profile of v8, /device:TPU:32, one launch (start us, length us, event | category | flops | bytes accessed | tf_op | source)
XLA Modules:
  0.0 197.5 jit_solution(16816685254729666323)
XLA Ops:
  1.6 32.9 %all_to_all.30 = bf16[16,64,128]{2,1,0:T(8,128)(2,1)S(1)} all-to-all(bf16[16,64,128]{2,1,0:T(8,128)(2,1)S(1)} %shard_map.68), channel_id=1, replica_groups=mesh['y'=4,'zh'=4,'zl'=4,'x'=4,'c'=2] {'zh','zl'}, dimensions={0} | all-to-all | bytes 524288 | tf_op jit(solution)/shard_map/all_to_all | solution.py:32
  35.8 7.0 %all-to-all-start.1 = ((bf16[16,4,64,128]{3,2,1,0:T(8,128)(2,1)}), bf16[16,4,64,128]{3,2,1,0:T(8,128)(2,1)S(1)}, u32[]{:S(2)}, u32[]{:S(2)}) async-start(bf16[16,4,64,128]{3,2,1,0:T(8,128)(2,1)} %bitcast.47), calls=%async_computation.1 | async-start | bytes 2097152 | tf_op jit(solution)/shard_map/all_to_all | solution.py:32
  42.9 5.0 %fusion.2.head_ref = bf16[1280,896]{1,0:T(8,128)(2,1)} fusion(bf16[896,1280]{1,0:T(8,128)(2,1)S(1)} %copy-done, s32[1280]{0:T(1024)S(1)} %fusion.39), kind=kOutput, calls=%fused_computation.3 | convolution fusion | flops 2938798080 | bytes 4592640 | tf_op jit(solution)/shard_map/dot_general | solution.py:161
  47.9 11.5 %all-to-all-done.1 = bf16[16,4,64,128]{3,2,1,0:T(8,128)(2,1)S(1)} async-done(((bf16[16,4,64,128]{3,2,1,0:T(8,128)(2,1)}), bf16[16,4,64,128]{3,2,1,0:T(8,128)(2,1)S(1)}, u32[]{:S(2)}, u32[]{:S(2)}) %all-to-all-start.1) | async-done | bytes 1048608 | tf_op jit(solution)/shard_map/all_to_all | solution.py:32
  61.9 2.1 %collective-permute-done.a_ref = bf16[4,16,64,128]{3,2,1,0:T(8,128)(2,1)} collective-permute-done((bf16[4,16,64,128]{3,2,1,0:T(8,128)(2,1)S(1)}, bf16[4,16,64,128]{3,2,1,0:T(8,128)(2,1)}, u32[]{:S(2)}, u32[]{:S(2)}) %collective-permute-start) | collective-permute-done | bytes 1048608 | tf_op jit(solution)/shard_map/ppermute | solution.py:28
  66.7 2.6 %collective-permute-start.3 = (f32[96,896]{1,0:T(8,128)S(1)}, f32[96,896]{1,0:T(8,128)S(1)}, u32[]{:S(2)}, u32[]{:S(2)}) collective-permute-start(f32[96,896]{1,0:T(8,128)S(1)} %get-tuple-element.49), channel_id=1, source_target_pairs={{0,384},{128,0},{256,128},{384,256},{1,385},{129,1},{257,129},{385... | collective-permute-start | bytes 1032200 | tf_op jit(solution)/shard_map/ppermute | solution.py:24
  69.3 3.3 %collective-permute-start.1 = (f32[96,896]{1,0:T(8,128)S(1)}, f32[96,896]{1,0:T(8,128)S(1)}, u32[]{:S(2)}, u32[]{:S(2)}) collective-permute-start(f32[96,896]{1,0:T(8,128)S(1)} %get-tuple-element.48), channel_id=1, source_target_pairs={{0,128},{128,256},{256,384},{384,0},{1,129},{129,257},{257,385},{3... | collective-permute-start | bytes 1032200 | tf_op jit(solution)/shard_map/ppermute | solution.py:24
  74.6 4.1 %collective-permute-done.3 = f32[96,896]{1,0:T(8,128)S(1)} collective-permute-done((f32[96,896]{1,0:T(8,128)S(1)}, f32[96,896]{1,0:T(8,128)S(1)}, u32[]{:S(2)}, u32[]{:S(2)}) %collective-permute-start.3) | collective-permute-done | bytes 344096 | tf_op jit(solution)/shard_map/ppermute | solution.py:24
  79.6 3.8 %collective-permute-start.4 = (f32[192,896]{1,0:T(8,128)}, f32[192,896]{1,0:T(8,128)S(1)}, u32[]{:S(2)}, u32[]{:S(2)}) collective-permute-start(f32[192,896]{1,0:T(8,128)} %pad_add_fusion), channel_id=1, source_target_pairs={{0,384},{128,0},{256,128},{384,256},{1,385},{129,1},{257,129},{385... | collective-permute-start | bytes 2064392 | tf_op jit(solution)/shard_map/ppermute | solution.py:24
  84.3 2.0 %collective-permute-start.2 = (f32[192,896]{1,0:T(8,128)}, f32[192,896]{1,0:T(8,128)}, u32[]{:S(2)}, u32[]{:S(2)}) collective-permute-start(f32[192,896]{1,0:T(8,128)} %pad_add_fusion.1), channel_id=1, source_target_pairs={{0,128},{128,256},{256,384},{384,0},{1,129},{129,257},{257,385},{3... | collective-permute-start | bytes 2064392 | tf_op jit(solution)/shard_map/ppermute | solution.py:24
  90.2 8.1 %collective-permute-done.4 = f32[192,896]{1,0:T(8,128)S(1)} collective-permute-done((f32[192,896]{1,0:T(8,128)}, f32[192,896]{1,0:T(8,128)S(1)}, u32[]{:S(2)}, u32[]{:S(2)}) %collective-permute-start.4) | collective-permute-done | bytes 688160 | tf_op jit(solution)/shard_map/ppermute | solution.py:24
  98.3 5.7 %collective-permute-done.2 = f32[192,896]{1,0:T(8,128)} collective-permute-done((f32[192,896]{1,0:T(8,128)}, f32[192,896]{1,0:T(8,128)}, u32[]{:S(2)}, u32[]{:S(2)}) %collective-permute-start.2) | collective-permute-done | bytes 688160 | tf_op jit(solution)/shard_map/ppermute | solution.py:24
  106.2 7.0 %all-to-all-start.2 = ((f32[16,1,192]{2,1,0:T(1,128)}), f32[16,1,192]{2,1,0:T(1,128)S(1)}, u32[]{:S(2)}, u32[]{:S(2)}) async-start(f32[16,1,192]{2,1,0:T(1,128)} %get-tuple-element.36), calls=%async_computation.2 | async-start | bytes 32768 | tf_op jit(solution)/shard_map/all_to_all | solution.py:32
  115.2 3.2 %collective-permute-start.6 = (bf16[192,896]{1,0:T(8,128)(2,1)S(1)}, bf16[192,896]{1,0:T(8,128)(2,1)S(1)}, u32[]{:S(2)}, u32[]{:S(2)}) collective-permute-start(bf16[192,896]{1,0:T(8,128)(2,1)S(1)} %get-tuple-element.40.exps0), channel_id=1, source_target_pairs={{0,256},{128,384},{256,0},{384,128},{1,257},{129,385},{257,1},{385... | collective-permute-start | bytes 1032200 | tf_op jit(solution)/shard_map/ppermute | solution.py:24
  118.4 2.6 %collective-permute-start.7 = (bf16[192,896]{1,0:T(8,128)(2,1)S(1)}, bf16[192,896]{1,0:T(8,128)(2,1)}, u32[]{:S(2)}, u32[]{:S(2)}) collective-permute-start(bf16[192,896]{1,0:T(8,128)(2,1)S(1)} %get-tuple-element.40.exps0), channel_id=1, source_target_pairs={{0,128},{128,256},{256,384},{384,0},{1,129},{129,257},{257,385},{3... | collective-permute-start | bytes 1032200 | tf_op jit(solution)/shard_map/ppermute | solution.py:24
  121.0 3.5 %all-to-all-done.2.lse_ref = f32[16,1,192]{2,1,0:T(1,128)S(1)} async-done(((f32[16,1,192]{2,1,0:T(1,128)}), f32[16,1,192]{2,1,0:T(1,128)S(1)}, u32[]{:S(2)}, u32[]{:S(2)}) %all-to-all-start.2) | async-done | bytes 12320 | tf_op jit(solution)/shard_map/all_to_all | solution.py:32
  125.2 3.9 %all-to-all-start.3 = ((f32[32,4,192]{2,1,0:T(4,128)}), f32[32,4,192]{2,1,0:T(4,128)S(1)}, u32[]{:S(2)}, u32[]{:S(2)}) async-start(f32[32,4,192]{2,1,0:T(4,128)} %copy-done.9), calls=%async_computation.3 | async-start | bytes 262144 | tf_op jit(solution)/shard_map/all_to_all | solution.py:32
  129.2 7.7 %all-to-all-done.3.facts_ref = f32[32,4,192]{2,1,0:T(4,128)S(1)} async-done(((f32[32,4,192]{2,1,0:T(4,128)}), f32[32,4,192]{2,1,0:T(4,128)S(1)}, u32[]{:S(2)}, u32[]{:S(2)}) %all-to-all-start.3) | async-done | bytes 98336 | tf_op jit(solution)/shard_map/all_to_all | solution.py:32
  138.5 2.9 %shard_map.73 = (bf16[4,192,896]{2,1,0:T(8,128)(2,1)S(1)}, bf16[4,16,64,128]{3,2,1,0:T(8,128)(2,1)S(1)}) custom-call(s32[3]{0:T(128)S(1)} %pad_add_fusion.2.where_ref, f32[32,4,192]{2,1,0:T(4,128)S(1)} %all-to-all-done.3.facts_ref, bf16[192,896]{1,0:T(8,128)(2,1)S(1)} %get-tuple-element.40.exps0, bf16[192,896]{1,0:T(8,128)(2,1)S(1)} %collective-permute-done.5.exps1, ...), custom_call_target="tpu_custom_call" | custom-call | tf_op jit(solution)/shard_map/pallas_call | solution.py:36
  146.3 20.6 %all_to_all.31 = bf16[16,4,64,128]{3,2,1,0:T(8,128)(2,1)S(1)} all-to-all(bf16[16,4,64,128]{3,2,1,0:T(8,128)(2,1)S(1)} %bitcast.48), channel_id=1, replica_groups=mesh['y'=4,'zh'=4,'zl'=4,'x'=4,'c'=2] {'y','x'}, dimensions={0} | all-to-all | bytes 2097152 | tf_op jit(solution)/shard_map/all_to_all | solution.py:32
  167.9 11.3 %all-to-all-start.5 = ((bf16[16,64,128]{2,1,0:T(8,128)(2,1)}), bf16[16,64,128]{2,1,0:T(8,128)(2,1)S(1)}, u32[]{:S(2)}, u32[]{:S(2)}) async-start(bf16[16,64,128]{2,1,0:T(8,128)(2,1)} %bitcast.21), calls=%async_computation.5 | async-start | bytes 524288 | tf_op jit(solution)/shard_map/all_to_all | solution.py:32
  183.1 2.9 %shard_map.75 = bf16[1280,896]{1,0:T(8,128)(2,1)S(1)} custom-call(bf16[4,640,192]{2,1,0:T(8,128)(2,1)S(1)} %copy-done.4, bf16[4,640,192]{2,1,0:T(8,128)(2,1)S(1)} %copy-done.6, bf16[4,192,896]{2,1,0:T(8,128)(2,1)S(1)} %copy-done.8), custom_call_target="tpu_custom_call" | custom-call | flops 2000000000 | tf_op jit(solution)/shard_map/pallas_call | solution.py:36
  186.0 4.9 %fusion.3 = bf16[896,1280]{1,0:T(8,128)(2,1)} fusion(bf16[1280,896]{1,0:T(8,128)(2,1)S(1)} %shard_map.75, s32[1280]{0:T(1024)S(1)} %fusion.39), kind=kOutput, calls=%fused_computation.4 | convolution fusion | flops 2938798080 | bytes 4592640 | tf_op jit(solution)/shard_map/dot_general | solution.py:161
  190.9 5.8 %all-to-all-done.5 = bf16[16,64,128]{2,1,0:T(8,128)(2,1)S(1)} async-done(((bf16[16,64,128]{2,1,0:T(8,128)(2,1)}), bf16[16,64,128]{2,1,0:T(8,128)(2,1)S(1)}, u32[]{:S(2)}, u32[]{:S(2)}) %all-to-all-start.5) | async-done | bytes 262176 | tf_op jit(solution)/shard_map/all_to_all | solution.py:32
  (69 shorter events, 32.0 us)
Async XLA Ops:
  0.6 42.2 %copy-start = (bf16[896,1280]{1,0:T(8,128)(2,1)S(1)}, bf16[896,1280]{1,0:T(8,128)(2,1)}, u32[]{:S(2)}) copy-start(bf16[896,1280]{1,0:T(8,128)(2,1)} %param.6) | copy-start | bytes 6881284
  35.8 23.5 %all-to-all-start.1 = ((bf16[16,4,64,128]{3,2,1,0:T(8,128)(2,1)}), bf16[16,4,64,128]{3,2,1,0:T(8,128)(2,1)S(1)}, u32[]{:S(2)}, u32[]{:S(2)}) async-start(bf16[16,4,64,128]{3,2,1,0:T(8,128)(2,1)} %bitcast.47), calls=%async_computation.1 | async-start | bytes 2097152 | tf_op jit(solution)/shard_map/all_to_all | solution.py:32
  42.9 18.4 %copy-start.12 = (s32[1,192]{1,0:T(1,128)S(1)}, s32[1,192]{1,0:T(1,128)}, u32[]{:S(2)}) copy-start(s32[1,192]{1,0:T(1,128)} %param.9) | copy-start | bytes 2308
  42.9 18.4 %copy-start.11 = (s32[1,192]{1,0:T(1,128)S(1)}, s32[1,192]{1,0:T(1,128)}, u32[]{:S(2)}) copy-start(s32[1,192]{1,0:T(1,128)} %param.8) | copy-start | bytes 2308
  59.3 4.7 %collective-permute-start = (bf16[4,16,64,128]{3,2,1,0:T(8,128)(2,1)S(1)}, bf16[4,16,64,128]{3,2,1,0:T(8,128)(2,1)}, u32[]{:S(2)}, u32[]{:S(2)}) collective-permute-start(bf16[4,16,64,128]{3,2,1,0:T(8,128)(2,1)S(1)} %bitcast.44), channel_id=1, source_target_pairs={{0,1},{1,0},{2,3},{3,2},{4,5},{5,4},{6,7},{7,6},{8,9},{9,8},{10,11... | collective-permute-start | bytes 3145736 | tf_op jit(solution)/shard_map/ppermute | solution.py:28
  61.9 11.6 %copy-start.3 = (bf16[4,640,192]{2,1,0:T(8,128)(2,1)}, bf16[4,640,192]{2,1,0:T(8,128)(2,1)S(1)}, u32[]{:S(2)}) copy-start(bf16[4,640,192]{2,1,0:T(8,128)(2,1)S(1)} %shard_map.69.own_ref) | copy-start | bytes 2949124
  61.9 3.7 %copy-start.1 = (bf16[1280,896]{1,0:T(8,128)(2,1)S(1)}, bf16[1280,896]{1,0:T(8,128)(2,1)}, u32[]{:S(2)}) copy-start(bf16[1280,896]{1,0:T(8,128)(2,1)} %fusion.2.head_ref) | copy-start | bytes 6881284
  65.6 8.4 %copy-start.5 = (bf16[4,640,192]{2,1,0:T(8,128)(2,1)}, bf16[4,640,192]{2,1,0:T(8,128)(2,1)S(1)}, u32[]{:S(2)}) copy-start(bf16[4,640,192]{2,1,0:T(8,128)(2,1)S(1)} %shard_map.70.other_ref) | copy-start | bytes 2949124
  66.7 12.0 %collective-permute-start.3 = (f32[96,896]{1,0:T(8,128)S(1)}, f32[96,896]{1,0:T(8,128)S(1)}, u32[]{:S(2)}, u32[]{:S(2)}) collective-permute-start(f32[96,896]{1,0:T(8,128)S(1)} %get-tuple-element.49), channel_id=1, source_target_pairs={{0,384},{128,0},{256,128},{384,256},{1,385},{129,1},{257,129},{385... | collective-permute-start | bytes 1032200 | tf_op jit(solution)/shard_map/ppermute | solution.py:24
  69.3 14.1 %collective-permute-start.1 = (f32[96,896]{1,0:T(8,128)S(1)}, f32[96,896]{1,0:T(8,128)S(1)}, u32[]{:S(2)}, u32[]{:S(2)}) collective-permute-start(f32[96,896]{1,0:T(8,128)S(1)} %get-tuple-element.48), channel_id=1, source_target_pairs={{0,128},{128,256},{256,384},{384,0},{1,129},{129,257},{257,385},{3... | collective-permute-start | bytes 1032200 | tf_op jit(solution)/shard_map/ppermute | solution.py:24
  74.6 11.8 %copy-start.13 = (s32[1,192]{1,0:T(1,128)S(1)}, s32[1,192]{1,0:T(1,128)}, u32[]{:S(2)}) copy-start(s32[1,192]{1,0:T(1,128)} %param.7) | copy-start | bytes 2308
  79.6 18.7 %collective-permute-start.4 = (f32[192,896]{1,0:T(8,128)}, f32[192,896]{1,0:T(8,128)S(1)}, u32[]{:S(2)}, u32[]{:S(2)}) collective-permute-start(f32[192,896]{1,0:T(8,128)} %pad_add_fusion), channel_id=1, source_target_pairs={{0,384},{128,0},{256,128},{384,256},{1,385},{129,1},{257,129},{385... | collective-permute-start | bytes 2064392 | tf_op jit(solution)/shard_map/ppermute | solution.py:24
  84.3 19.8 %collective-permute-start.2 = (f32[192,896]{1,0:T(8,128)}, f32[192,896]{1,0:T(8,128)}, u32[]{:S(2)}, u32[]{:S(2)}) collective-permute-start(f32[192,896]{1,0:T(8,128)} %pad_add_fusion.1), channel_id=1, source_target_pairs={{0,128},{128,256},{256,384},{384,0},{1,129},{129,257},{257,385},{3... | collective-permute-start | bytes 2064392 | tf_op jit(solution)/shard_map/ppermute | solution.py:24
  106.2 18.3 %all-to-all-start.2 = ((f32[16,1,192]{2,1,0:T(1,128)}), f32[16,1,192]{2,1,0:T(1,128)S(1)}, u32[]{:S(2)}, u32[]{:S(2)}) async-start(f32[16,1,192]{2,1,0:T(1,128)} %get-tuple-element.36), calls=%async_computation.2 | async-start | bytes 32768 | tf_op jit(solution)/shard_map/all_to_all | solution.py:32
  113.2 23.6 %collective-permute-start.5 = (bf16[192,896]{1,0:T(8,128)(2,1)S(1)}, bf16[192,896]{1,0:T(8,128)(2,1)S(1)}, u32[]{:S(2)}, u32[]{:S(2)}) collective-permute-start(bf16[192,896]{1,0:T(8,128)(2,1)S(1)} %get-tuple-element.40.exps0), channel_id=1, source_target_pairs={{0,384},{128,0},{256,128},{384,256},{1,385},{129,1},{257,129},{385... | collective-permute-start | bytes 1032200 | tf_op jit(solution)/shard_map/ppermute | solution.py:24
  115.2 21.7 %collective-permute-start.6 = (bf16[192,896]{1,0:T(8,128)(2,1)S(1)}, bf16[192,896]{1,0:T(8,128)(2,1)S(1)}, u32[]{:S(2)}, u32[]{:S(2)}) collective-permute-start(bf16[192,896]{1,0:T(8,128)(2,1)S(1)} %get-tuple-element.40.exps0), channel_id=1, source_target_pairs={{0,256},{128,384},{256,0},{384,128},{1,257},{129,385},{257,1},{385... | collective-permute-start | bytes 1032200 | tf_op jit(solution)/shard_map/ppermute | solution.py:24
  118.4 18.5 %collective-permute-start.7 = (bf16[192,896]{1,0:T(8,128)(2,1)S(1)}, bf16[192,896]{1,0:T(8,128)(2,1)}, u32[]{:S(2)}, u32[]{:S(2)}) collective-permute-start(bf16[192,896]{1,0:T(8,128)(2,1)S(1)} %get-tuple-element.40.exps0), channel_id=1, source_target_pairs={{0,128},{128,256},{256,384},{384,0},{1,129},{129,257},{257,385},{3... | collective-permute-start | bytes 1032200 | tf_op jit(solution)/shard_map/ppermute | solution.py:24
  125.2 11.7 %all-to-all-start.3 = ((f32[32,4,192]{2,1,0:T(4,128)}), f32[32,4,192]{2,1,0:T(4,128)S(1)}, u32[]{:S(2)}, u32[]{:S(2)}) async-start(f32[32,4,192]{2,1,0:T(4,128)} %copy-done.9), calls=%async_computation.3 | async-start | bytes 262144 | tf_op jit(solution)/shard_map/all_to_all | solution.py:32
  136.9 1.6 copy-start.2
  141.4 3.6 %copy-start.7 = (bf16[4,192,896]{2,1,0:T(8,128)(2,1)}, bf16[4,192,896]{2,1,0:T(8,128)(2,1)S(1)}, u32[]{:S(2)}) copy-start(bf16[4,192,896]{2,1,0:T(8,128)(2,1)S(1)} %get-tuple-element.45.grads_ref) | copy-start | bytes 4128772
  141.4 4.6 %collective-permute-start.8 = (bf16[4,16,64,128]{3,2,1,0:T(8,128)(2,1)S(1)}, bf16[4,16,64,128]{3,2,1,0:T(8,128)(2,1)S(1)}, u32[]{:S(2)}, u32[]{:S(2)}) collective-permute-start(bf16[4,16,64,128]{3,2,1,0:T(8,128)(2,1)S(1)} %get-tuple-element.44), channel_id=1, source_target_pairs={{0,1},{1,0},{2,3},{3,2},{4,5},{5,4},{6,7},{7,6},{8,9},{9,8},{10,11... | collective-permute-start | bytes 3145736 | tf_op jit(solution)/shard_map/ppermute | solution.py:28
  167.9 28.9 %all-to-all-start.5 = ((bf16[16,64,128]{2,1,0:T(8,128)(2,1)}), bf16[16,64,128]{2,1,0:T(8,128)(2,1)S(1)}, u32[]{:S(2)}, u32[]{:S(2)}) async-start(bf16[16,64,128]{2,1,0:T(8,128)(2,1)} %bitcast.21), calls=%async_computation.5 | async-start | bytes 524288 | tf_op jit(solution)/shard_map/all_to_all | solution.py:32
  179.2 1.3 copy-start.4
  181.8 1.3 copy-start.8
  (3 other events, 2.9 us)
